TPU v7x, 256 devices: a whole 4x4x8 slice. The times are simulated.
256 devices in a mesh: sub: 32 (over y, z_hi, x), grp: 8 (over z_lo, core).
Axes of the slice: x: 4, y: 4, z: 8 (z_hi: 2, z_lo: 4; z = z_hi * 4 + z_lo), core: 2. Of those that a mesh axis runs over, the one named last changes fastest.
Arguments:
- residual: bfloat16 [32, 8, 1536, 1024], P('sub', 'grp'), may hold values from -6 to 6
- weights: float32 [32, 8, 1536], P('sub', 'grp'), may hold values from 0.3 to 1
- face_map: int32 [32, 8, 4, 384], P('sub', 'grp'), may hold values from 0 to 383, each once within a row
- local_inverse: bfloat16 [32, 8, 1536, 1536], P('sub', 'grp'), may hold values from -1 to 3
- basis: bfloat16 [32, 8, 37, 1536], P('sub', 'grp'), may hold values from -0.15625 to 0.15625
- primal_index: int32 [32, 8, 37], P('sub', 'grp'), may hold values from 0 to 511, as said below
- group_inverse: float32 [8, 512, 512], P('grp'), may hold values from -1 to 3
- group_basis: float32 [8, 37, 512], P('grp'), may hold values from -0.25 to 0.25
- group_index: int32 [8, 37], P('grp'), may hold values from 0 to 147, as said below
- coarse_inverse: float32 [148, 148], replicated, may hold values from -1 to 3
Outputs:
- preconditioned: bfloat16 [32, 8, 1536, 1024], P('sub', 'grp')
Inputs may be any that keep to these rules, and one draw needn't show every extreme that they name: `primal_index`: within one subdomain the 37 entries are distinct. `group_index`: within one group the 37 entries are distinct. `face_map`: each row of 384 entries is a permutation.
All inputs are finite; a program needn't handle non-finite values.
Results may differ from a plain program's by a relative error of at most 0.0043.
The roundings to bfloat16 on the way count: a program that leaves them out, or rounds other values in their place, can miss the bound.
Values may be sent and summed in bfloat16 or wider, within the bound.
No kernel may reach another device: no remote copies, remote signals or barrier semaphores. Data moves between devices by JAX's collectives and lax.ppermute only.
A program may use at most 128 MiB of HBM per device.

v0:
```python
import jax
import jax.numpy as jnp
from jax import lax
from jax.sharding import PartitionSpec as P


def extended(shard, sides, width):
    for axis, dim in sides:
        size, length = (lax.axis_size(axis), shard.shape[dim])
        up = [(i, (i + 1) % size) for i in range(size - 1)]
        down = [(j, i) for i, j in up]
        last = lax.slice_in_dim(shard, length - width, length, axis=dim)
        initial = lax.slice_in_dim(shard, 0, width, axis=dim)
        before = lax.ppermute(last, axis, up)
        after = lax.ppermute(initial, axis, down)
        shard = jnp.concatenate([before, shard, after], axis=dim)
    return shard


def neighbour_faces(values_in, orders):
    face_count, face_size = orders.shape
    columns = values_in.shape[1]
    face_blocks = values_in.reshape(face_count, face_size, columns)
    along_sub = extended(face_blocks[0:2], (("sub", 0),), 1)
    along_grp = extended(face_blocks[2:4], (("grp", 0),), 1)
    arrived = jnp.stack([along_sub[0], along_sub[3], along_grp[0], along_grp[3]])
    picked = jax.vmap(lambda face_block, order_row: face_block[order_row])(arrived, orders)
    return picked.reshape(face_count * face_size, columns)


def contract_lead(left_side, right_side):
    return lax.dot_general(
        left_side,
        right_side,
        (((0,), (0,)), ((), ())),
        precision=lax.Precision.HIGHEST,
        preferred_element_type=jnp.float32,
    )


def local(
    residual,
    weights,
    face_map,
    local_inverse,
    basis,
    primal_index,
    group_inverse,
    group_basis,
    group_index,
    coarse_inverse,
):
    exact = lax.Precision.HIGHEST
    values_in = residual[0, 0]
    orders = face_map[0, 0]
    weighting = weights[0, 0][:, None]
    arrived = neighbour_faces(values_in, orders)
    own_part = (weighting * values_in.astype(jnp.float32)).astype(jnp.bfloat16)
    other_part = (weighting * arrived.astype(jnp.float32)).astype(jnp.bfloat16)
    inverse = local_inverse[0, 0]
    coarse_rows = basis[0, 0]
    local_part = jnp.dot(inverse, own_part, preferred_element_type=jnp.float32) + jnp.dot(
        inverse, other_part, preferred_element_type=jnp.float32
    )
    restricted = jnp.dot(coarse_rows, own_part, preferred_element_type=jnp.float32) + jnp.dot(
        coarse_rows, other_part, preferred_element_type=jnp.float32
    )
    slot_ids = primal_index[0, 0]
    level_two_size = group_inverse.shape[1]
    picker = (jnp.arange(level_two_size, dtype=jnp.int32)[:, None] == slot_ids[None, :]).astype(
        jnp.float32
    )
    g_inverse = group_inverse[0]
    g_basis = group_basis[0]
    g_slots = group_index[0]
    coarse_size = coarse_inverse.shape[0]
    picker_two = (jnp.arange(coarse_size, dtype=jnp.int32)[:, None] == g_slots[None, :]).astype(
        jnp.float32
    )
    partial_two = jnp.dot(picker, restricted, precision=exact)
    group_rhs = lax.psum(partial_two, "sub")
    coarse_part = jnp.dot(picker_two, jnp.dot(g_basis, group_rhs, precision=exact), precision=exact)
    coarse_rhs = lax.psum(coarse_part, "grp")
    coarse_sol = jnp.dot(coarse_inverse, coarse_rhs, precision=exact)
    coarse_at_group = contract_lead(picker_two, coarse_sol)
    group_sol = jnp.dot(g_inverse, group_rhs, precision=exact) + contract_lead(
        g_basis, coarse_at_group
    )
    primal_values = contract_lead(picker, group_sol).astype(jnp.bfloat16)
    lifted = lax.dot_general(
        coarse_rows, primal_values, (((0,), (0,)), ((), ())), preferred_element_type=jnp.float32
    )
    corrected = (local_part + lifted).astype(jnp.bfloat16)
    arrived_back = neighbour_faces(corrected, orders)
    result = (
        weighting * (corrected.astype(jnp.float32) + arrived_back.astype(jnp.float32))
    ).astype(jnp.bfloat16)
    return result[None, None]


def solution(mesh):
    placed = (
        P("sub", "grp", None, None),
        P("sub", "grp", None),
        P("sub", "grp", None, None),
        P("sub", "grp", None, None),
        P("sub", "grp", None, None),
        P("sub", "grp", None),
        P("grp", None, None),
        P("grp", None, None),
        P("grp", None),
        P(),
    )
    return jax.shard_map(
        local, mesh=mesh, in_specs=placed, out_specs=P("sub", "grp", None, None), check_vma=False
    )
```

profile of v0, /device:TPU:15, one launch (start us, length us, event | category | flops | bytes accessed | tf_op | source)
XLA Modules:
  0.0 747.6 jit_solution(1930824687781805139)
XLA Ops:
  6.5 0.0 copy-start
  6.5 0.0 all-reduce.3.cloned.1.call-start
  6.5 3.4 slice_bitcast_fusion.7
  10.0 8.7 %collective-permute-start = (bf16[1,384,1024]{2,1,0:T(8,128)(2,1)}, bf16[1,384,1024]{2,1,0:T(8,128)(2,1)S(1)}, u32[]{:S(2)}, u32[]{:S(2)}) collective-permute-start(bf16[1,384,1024]{2,1,0:T(8,128)(2,1)} %get-tuple-element.9), channel_id=1, source_target_pairs={{0,8},{8,16},{16,24},{24,32},{32,40},{40,48},{48,56},{56,64},{64,7... | collective-permute-start | bytes 2359304 | tf_op jit(solution)/shard_map/ppermute | solution.py:14
  18.7 1.9 collective-permute-start.1
  20.6 2.9 collective-permute-start.3
  23.5 2.7 collective-permute-start.2
  26.2 0.0 copy-done.9
  26.2 0.0 copy-done.10
  26.3 13.6 %collective-permute-done = bf16[1,384,1024]{2,1,0:T(8,128)(2,1)S(1)} collective-permute-done((bf16[1,384,1024]{2,1,0:T(8,128)(2,1)}, bf16[1,384,1024]{2,1,0:T(8,128)(2,1)S(1)}, u32[]{:S(2)}, u32[]{:S(2)}) %collective-permute-start) | collective-permute-done | bytes 786464 | tf_op jit(solution)/shard_map/ppermute | solution.py:14
  39.9 8.7 %collective-permute-done.1 = bf16[1,384,1024]{2,1,0:T(8,128)(2,1)S(1)} collective-permute-done((bf16[1,384,1024]{2,1,0:T(8,128)(2,1)}, bf16[1,384,1024]{2,1,0:T(8,128)(2,1)S(1)}, u32[]{:S(2)}, u32[]{:S(2)}) %collective-permute-start.1) | collective-permute-done | bytes 786464 | tf_op jit(solution)/shard_map/ppermute | solution.py:15
  48.6 14.4 %collective-permute-done.3 = bf16[1,384,1024]{2,1,0:T(8,128)(2,1)} collective-permute-done((bf16[1,384,1024]{2,1,0:T(8,128)(2,1)}, bf16[1,384,1024]{2,1,0:T(8,128)(2,1)}, u32[]{:S(2)}, u32[]{:S(2)}) %collective-permute-start.3) | collective-permute-done | bytes 786464 | tf_op jit(solution)/shard_map/ppermute | solution.py:15
  63.0 0.0 collective-permute-done.2
  63.0 3.0 pad_maximum_fusion
  66.0 31.7 %gather_fusion = bf16[1536,1024]{1,0:T(8,128)(2,1)} fusion(bf16[4,384,1024]{2,1,0:T(8,128)(2,1)} %pad_maximum_fusion, s32[1536]{0:T(1024)S(1)} %reshape.119), kind=kCustom, calls=%fused_computation | custom fusion | bytes 6303744 | tf_op jit(solution)/shard_map/vmap()/gather | solution.py:27
  97.6 2.5 fusion
  100.1 0.0 copy-start.2
  100.1 0.0 copy-start.5
  100.2 0.0 copy-done.6
  100.2 1.0 fusion.29
  101.2 2.0 copy-done.5
  103.2 1.5 fusion.15
  104.7 0.0 copy-done.2
  104.7 0.0 copy-done.12
  104.7 2.4 fusion.24
  107.1 0.0 all-reduce.3.cloned.1.call-update
  107.1 0.0 copy-start.7
  107.1 0.0 copy-start.11
  107.1 0.2 all-reduce.5.cloned.1.call-start
  107.3 10.4 %fusion.5 = f32[1024,1536]{1,0:T(8,128)} fusion(bf16[1,1,1536,1536]{3,2,1,0:T(8,128)(2,1)} %param.13, bf16[1,1,1536,1024]{3,2,1,0:T(8,128)(2,1)} %param.10, f32[1536]{0:T(1024)S(1)} %reduce), kind=kOutput, calls=%fused_computation.11 | convolution fusion | flops 4836556800 | bytes 14161920 | tf_op jit(solution)/shard_map/dot_general | solution.py:62
  117.8 379.3 %all-reduce.3.cloned.1.call-done = f32[512,1024]{1,0:T(8,128)} async-done(((f32[512,1024]{1,0:T(8,128)}), f32[512,1024]{1,0:T(8,128)}) %all-reduce.3.cloned.1.call-update) | async-done | bytes 2097168 | tf_op jit(solution)/shard_map/psum | solution.py:81
  497.0 0.0 copy-done.7
  497.0 5.0 fusion.34
  502.1 0.0 copy-done.11
  502.1 1.3 fusion.39
  503.4 0.0 all-reduce.5.cloned.1.call-update
  503.4 0.0 copy-start.3
  503.4 10.0 %fusion.3 = f32[1024,1536]{1,0:T(8,128)} fusion(bf16[1536,1024]{1,0:T(8,128)(2,1)} %bitcast.67, bf16[1,1,1536,1536]{3,2,1,0:T(8,128)(2,1)} %param.13), kind=kOutput, calls=%fused_computation.9 | convolution fusion | flops 4831838208 | bytes 14155776 | tf_op jit(solution)/shard_map/dot_general | solution.py:62
  513.4 0.0 copy-done
  513.4 0.0 copy-done.3
  513.4 6.7 fusion.21
  520.1 98.9 %all-reduce.5.cloned.1.call-done = f32[148,1024]{1,0:T(8,128)} async-done(((f32[148,1024]{1,0:T(8,128)}), f32[148,1024]{1,0:T(8,128)}) %all-reduce.5.cloned.1.call-update) | async-done | bytes 606224 | tf_op jit(solution)/shard_map/psum | solution.py:83
  619.0 0.0 copy-done.8
  619.0 2.9 fusion.47
  621.9 0.7 fusion.40
  622.6 1.8 fusion.32
  624.5 1.3 fusion.18
  625.8 4.1 fusion.7
  629.9 0.3 slice_bitcast_fusion.3
  630.2 1.3 copy-done.1
  631.5 7.0 collective-permute-start.4
  638.5 3.9 collective-permute-start.7
  642.5 1.9 collective-permute-start.6
  644.4 1.9 collective-permute-start.5
  646.3 25.2 %collective-permute-done.4 = bf16[1,384,1024]{1,2,0:T(8,128)(2,1)S(1)} collective-permute-done((bf16[1,384,1024]{1,2,0:T(8,128)(2,1)S(1)}, bf16[1,384,1024]{1,2,0:T(8,128)(2,1)S(1)}, u32[]{:S(2)}, u32[]{:S(2)}) %collective-permute-start.4) | collective-permute-done | bytes 786464 | tf_op jit(solution)/shard_map/ppermute | solution.py:14
  671.6 9.0 %collective-permute-done.7 = bf16[1,384,1024]{1,2,0:T(8,128)(2,1)S(1)} collective-permute-done((bf16[1,384,1024]{1,2,0:T(8,128)(2,1)S(1)}, bf16[1,384,1024]{1,2,0:T(8,128)(2,1)S(1)}, u32[]{:S(2)}, u32[]{:S(2)}) %collective-permute-start.7) | collective-permute-done | bytes 786464 | tf_op jit(solution)/shard_map/ppermute | solution.py:15
  680.6 0.6 collective-permute-done.6
  681.2 7.6 %collective-permute-done.5 = bf16[1,384,1024]{1,2,0:T(8,128)(2,1)S(1)} collective-permute-done((bf16[1,384,1024]{1,2,0:T(8,128)(2,1)S(1)}, bf16[1,384,1024]{1,2,0:T(8,128)(2,1)S(1)}, u32[]{:S(2)}, u32[]{:S(2)}) %collective-permute-start.5) | collective-permute-done | bytes 786464 | tf_op jit(solution)/shard_map/ppermute | solution.py:15
  688.8 1.9 pad_maximum_fusion.1
  690.7 4.7 copy.11
  695.4 30.6 %gather_fusion.1 = bf16[1536,1024]{1,0:T(8,128)(2,1)} fusion(bf16[4,384,1024]{2,1,0:T(8,128)(2,1)} %copy.11, s32[1536]{0:T(1024)S(1)} %reshape.119), kind=kCustom, calls=%fused_computation.1 | custom fusion | bytes 6303744 | tf_op jit(solution)/shard_map/vmap()/gather | solution.py:27
  726.0 4.7 copy.12
  730.7 5.5 fusion.9
  736.2 4.6 copy.13
  (12 shorter events, 0.1 us)
Async XLA Ops:
  6.5 506.8 %copy-start = (f32[1,512,512]{2,1,0:T(8,128)S(1)}, f32[1,512,512]{2,1,0:T(8,128)}, u32[]{:S(2)}) copy-start(f32[1,512,512]{2,1,0:T(8,128)} %param.16) | copy-start | bytes 3145732
  6.5 19.7 %copy-start.9 = (s32[1,1,4,384]{3,2,1,0:T(4,128)S(1)}, s32[1,1,4,384]{3,2,1,0:T(4,128)}, u32[]{:S(2)}) copy-start(s32[1,1,4,384]{3,2,1,0:T(4,128)} %param.12) | copy-start | bytes 18436
  6.5 19.7 %copy-start.10 = (f32[1,1,1536]{2,1,0:T(1,128)S(1)}, f32[1,1,1536]{2,1,0:T(1,128)}, u32[]{:S(2)}) copy-start(f32[1,1,1536]{2,1,0:T(1,128)} %param.11) | copy-start | bytes 18436
  6.5 490.5 %all-reduce.3.cloned.1.call-start = ((), (), s32[]{:S(2)}) async-start(), calls=%async_computation | async-start | bytes 4194304 | tf_op jit(solution)/shard_map/psum | solution.py:81
  10.0 30.0 %collective-permute-start = (bf16[1,384,1024]{2,1,0:T(8,128)(2,1)}, bf16[1,384,1024]{2,1,0:T(8,128)(2,1)S(1)}, u32[]{:S(2)}, u32[]{:S(2)}) collective-permute-start(bf16[1,384,1024]{2,1,0:T(8,128)(2,1)} %get-tuple-element.9), channel_id=1, source_target_pairs={{0,8},{8,16},{16,24},{24,32},{32,40},{40,48},{48,56},{56,64},{64,7... | collective-permute-start | bytes 2359304 | tf_op jit(solution)/shard_map/ppermute | solution.py:14
  18.7 29.9 %collective-permute-start.1 = (bf16[1,384,1024]{2,1,0:T(8,128)(2,1)}, bf16[1,384,1024]{2,1,0:T(8,128)(2,1)S(1)}, u32[]{:S(2)}, u32[]{:S(2)}) collective-permute-start(bf16[1,384,1024]{2,1,0:T(8,128)(2,1)} %get-tuple-element.10), channel_id=1, source_target_pairs={{8,0},{16,8},{24,16},{32,24},{40,32},{48,40},{56,48},{64,56},{72,6... | collective-permute-start | bytes 2359304 | tf_op jit(solution)/shard_map/ppermute | solution.py:15
  20.6 42.4 %collective-permute-start.3 = (bf16[1,384,1024]{2,1,0:T(8,128)(2,1)}, bf16[1,384,1024]{2,1,0:T(8,128)(2,1)}, u32[]{:S(2)}, u32[]{:S(2)}) collective-permute-start(bf16[1,384,1024]{2,1,0:T(8,128)(2,1)} %get-tuple-element.11), channel_id=1, source_target_pairs={{1,0},{2,1},{3,2},{4,3},{5,4},{6,5},{7,6},{9,8},{10,9},{11,10},{12... | collective-permute-start | bytes 2359304 | tf_op jit(solution)/shard_map/ppermute | solution.py:15
  23.5 39.5 %collective-permute-start.2 = (bf16[1,384,1024]{2,1,0:T(8,128)(2,1)S(1)}, bf16[1,384,1024]{2,1,0:T(8,128)(2,1)}, u32[]{:S(2)}, u32[]{:S(2)}) collective-permute-start(bf16[1,384,1024]{2,1,0:T(8,128)(2,1)S(1)} %get-tuple-element.12), channel_id=1, source_target_pairs={{0,1},{1,2},{2,3},{3,4},{4,5},{5,6},{6,7},{8,9},{9,10},{10,11},{11... | collective-permute-start | bytes 2359304 | tf_op jit(solution)/shard_map/ppermute | solution.py:14
  97.6 2.5 copy-start.6
  100.1 4.5 copy-start.2
  100.1 3.0 copy-start.5
  103.2 1.5 copy-start.12
  107.1 390.0 %copy-start.7 = (f32[1,37,512]{2,0,1:T(1,128)S(1)}, f32[1,37,512]{2,0,1:T(1,128)}, u32[]{:S(2)}) copy-start(f32[1,37,512]{2,0,1:T(1,128)} %param.17) | copy-start | bytes 227332
  107.1 395.0 %copy-start.11 = (s32[1,37]{1,0:T(1,128)S(1)}, s32[1,37]{1,0:T(1,128)}, u32[]{:S(2)}) copy-start(s32[1,37]{1,0:T(1,128)} %param.18) | copy-start | bytes 448
  107.1 511.9 %all-reduce.5.cloned.1.call-start = ((), (), s32[]{:S(2)}) async-start(), calls=%async_computation.1 | async-start | bytes 1245184 | tf_op jit(solution)/shard_map/psum | solution.py:83
  503.4 10.0 %copy-start.3 = (f32[512,1024]{1,0:T(8,128)S(1)}, f32[512,1024]{1,0:T(8,128)}, u32[]{:S(2)}) copy-start(f32[512,1024]{1,0:T(8,128)} %all-reduce.3.cloned.1.call-done) | copy-start | bytes 6291460
  513.4 105.6 %copy-start.8 = (f32[148,148]{1,0:T(8,128)S(1)}, f32[148,148]{1,0:T(8,128)}, u32[]{:S(2)}) copy-start(f32[148,148]{1,0:T(8,128)} %param.19) | copy-start | bytes 262852
  622.6 3.2 copy-start.4
  629.9 1.7 copy-start.1
  631.5 40.0 %collective-permute-start.4 = (bf16[1,384,1024]{1,2,0:T(8,128)(2,1)S(1)}, bf16[1,384,1024]{1,2,0:T(8,128)(2,1)S(1)}, u32[]{:S(2)}, u32[]{:S(2)}) collective-permute-start(bf16[1,384,1024]{1,2,0:T(8,128)(2,1)S(1)} %get-tuple-element.5), channel_id=1, source_target_pairs={{0,8},{8,16},{16,24},{24,32},{32,40},{40,48},{48,56},{56,64},{64,7... | collective-permute-start | bytes 2359304 | tf_op jit(solution)/shard_map/ppermute | solution.py:14
  638.5 42.0 %collective-permute-start.7 = (bf16[1,384,1024]{1,2,0:T(8,128)(2,1)S(1)}, bf16[1,384,1024]{1,2,0:T(8,128)(2,1)S(1)}, u32[]{:S(2)}, u32[]{:S(2)}) collective-permute-start(bf16[1,384,1024]{1,2,0:T(8,128)(2,1)S(1)} %get-tuple-element.6), channel_id=1, source_target_pairs={{1,0},{2,1},{3,2},{4,3},{5,4},{6,5},{7,6},{9,8},{10,9},{11,10},{12... | collective-permute-start | bytes 2359304 | tf_op jit(solution)/shard_map/ppermute | solution.py:15
  642.5 38.7 %collective-permute-start.6 = (bf16[1,384,1024]{1,2,0:T(8,128)(2,1)S(1)}, bf16[1,384,1024]{1,2,0:T(8,128)(2,1)S(1)}, u32[]{:S(2)}, u32[]{:S(2)}) collective-permute-start(bf16[1,384,1024]{1,2,0:T(8,128)(2,1)S(1)} %get-tuple-element.7), channel_id=1, source_target_pairs={{0,1},{1,2},{2,3},{3,4},{4,5},{5,6},{6,7},{8,9},{9,10},{10,11},{11... | collective-permute-start | bytes 2359304 | tf_op jit(solution)/shard_map/ppermute | solution.py:14
  644.4 44.4 %collective-permute-start.5 = (bf16[1,384,1024]{1,2,0:T(8,128)(2,1)S(1)}, bf16[1,384,1024]{1,2,0:T(8,128)(2,1)S(1)}, u32[]{:S(2)}, u32[]{:S(2)}) collective-permute-start(bf16[1,384,1024]{1,2,0:T(8,128)(2,1)S(1)} %get-tuple-element.8), channel_id=1, source_target_pairs={{8,0},{16,8},{24,16},{32,24},{40,32},{48,40},{56,48},{64,56},{72,6... | collective-permute-start | bytes 2359304 | tf_op jit(solution)/shard_map/ppermute | solution.py:15
Sparse Core Ops, SparseCore 0:
  107.2 389.7 all-reduce.2
  503.5 115.4 all-reduce.4
where the time goes:
time: 749 us; the launch traced here: 748 us
  waiting for transfers between devices  557 us (74%)
  local copies, waits for them, and re-layouts  83.3 us (11%)
  matrix products  49 us (7%)
  starting transfers between devices  31.2 us (4%)
  between operations  13.7 us (2%)
  other arithmetic  12.9 us (2%)
    psum x1, waiting for transfers between devices, local(): group_rhs = lax.psum(partial_two, 'sub')  379 us
    psum x1, waiting for transfers between devices, local(): coarse_rhs = lax.psum(coarse_part, 'grp')  98.9 us
    gather x4, local copies, waits for them, and re-layouts, neighbour_faces(): face_block[order_row]  66.9 us
    ppermute x4, waiting for transfers between devices, extended(): after = lax.ppermute(initial, axis, down)  39.7 us
    ppermute x4, waiting for transfers between devices, extended(): before = lax.ppermute(last, axis, up)  39.5 us
    ppermute x4, starting transfers between devices, extended(): before = lax.ppermute(last, axis, up)  20.3 us
  transfers between devices with their start and end apart: 10, of which 9 were waited for; matrix products, arithmetic and copies ran while one was open for 4% of the time, Pallas kernels for 0%

commit v1 on v0

v1 whole, which is shorter than its diff:
```python
import functools
import jax
import jax.numpy as jnp
from jax import lax
from jax.experimental import pallas as pl
from jax.experimental.pallas import tpu as pltpu
from jax.sharding import PartitionSpec as P

F32, BF16, I16, I32 = jnp.float32, jnp.bfloat16, jnp.int16, jnp.int32
LANES = 128
SLOT = 40
ROWS = 48
EXTRA = 16
BASE = 16
VMEM = 64 * 1024 * 1024
FREE = pl.CostEstimate(flops=0, bytes_accessed=0, transcendentals=0)
LONG = pl.CostEstimate(flops=10**12, bytes_accessed=0, transcendentals=0)


def dot(a, b, dims=((1,), (0,)), precision=None):
    return lax.dot_general(a, b, (dims, ((), ())), precision=precision, preferred_element_type=F32)


def whole(shape):
    return pl.BlockSpec(shape, lambda i: (0,) * len(shape))


def params():
    return pltpu.CompilerParams(vmem_limit_bytes=VMEM)


def spec(shape, place):
    return pl.BlockSpec(shape, lambda i: place(i))


def lanes_between(shape, low, high):
    lane = lax.broadcasted_iota(I32, shape, len(shape) - 1)
    return (lane >= low) & (lane < high)


def one_hot_lanes(size, index_row):
    ids = lax.broadcasted_iota(I32, (size, index_row.shape[1]), 0)
    return jnp.where(ids == index_row, 1.0, 0.0)


def first_kernel(fs, weights, orders, basis, x_one, x_two, low_out, high_out, one, two):
    one[...] = x_one[...]
    two[...] = x_two[...]

    @pl.when(pl.program_id(0) == 0)
    def _():
        nc = basis.shape[0]
        for face, out in enumerate((low_out, high_out)):
            at = slice(face * fs, (face + 1) * fs)
            part = basis[:, at]
            scaled = (part.astype(F32) * weights[:, at]).astype(BF16)
            turned = dot(scaled, one_hot_lanes(fs, orders[face : face + 1, :]).astype(BF16), ((1,), (1,)))
            out[...] = jnp.zeros_like(out)
            out[0:nc, :] = turned.astype(BF16)
            out[ROWS : ROWS + nc, :] = part


def first_stage(x, weights, orders, basis):
    nb, m = x.shape
    fs, width = nb // 4, m // 2
    col = lambda k: spec((fs, width), lambda i: (k, i))
    face = jax.ShapeDtypeStruct((fs, m), BF16)
    terms = jax.ShapeDtypeStruct((2 * ROWS, fs), BF16)
    return pl.pallas_call(
        functools.partial(first_kernel, fs),
        grid=(2,),
        in_specs=[whole(weights.shape), whole(orders.shape), whole(basis.shape), col(0), col(1)],
        out_specs=[whole(terms.shape), whole(terms.shape), col(0), col(0)],
        out_shape=[terms, terms, face, face],
        compiler_params=params(),
        cost_estimate=FREE,
        name="first_stage",
    )(weights, orders, basis, x, x)


def cut_kernel(fs, basis, x_one, x_two, one, two):
    nc = basis.shape[0]
    for face, x, out in ((2, x_one, one), (3, x_two, two)):
        out[0:fs, :] = x[...]

        @pl.when(pl.program_id(0) == 0)
        def _():
            out[fs:, :] = jnp.zeros((ROWS, out.shape[1]), BF16)
            out[fs : fs + nc, 0:fs] = basis[:, face * fs : (face + 1) * fs]


def cut(x, basis):
    nb, m = x.shape
    fs, width = nb // 4, m // 2
    col = lambda n, k: spec((n, width), lambda i: (k, i))
    face = jax.ShapeDtypeStruct((fs + ROWS, m), BF16)
    return pl.pallas_call(
        functools.partial(cut_kernel, fs),
        grid=(2,),
        in_specs=[whole(basis.shape), col(fs, 2), col(fs, 3)],
        out_specs=[col(fs + ROWS, 0), col(fs + ROWS, 0)],
        out_shape=[face, face],
        compiler_params=params(),
        cost_estimate=FREE,
        name="cut",
    )(basis, x, x)


def on_lanes(rows, offset):
    n = rows.shape[1]
    parts = [jnp.zeros((offset, n), F32)] if offset else []
    parts += [rows, jnp.zeros((LANES - offset - SLOT, n), F32)]
    return jnp.concatenate(parts, axis=0).T.astype(BF16)


def near_kernel(fs, weights, orders, basis, low_qb, high_qb, x, own_out, rest, picks, w_col, basis_t):
    nc = basis.shape[0]
    half = 2 * fs

    @pl.when(pl.program_id(0) == 0)
    def _():
        w_col[...] = jnp.broadcast_to(weights[...], (8, 4 * fs)).T[:, 0:1]
        for face in range(4):
            picks[face] = one_hot_lanes(fs, orders[face : face + 1, :]).T.astype(BF16)
        tall = jnp.concatenate([basis[...].astype(F32), jnp.zeros((LANES - nc, 4 * fs), F32)], axis=0)
        basis_t[...] = tall.T.astype(BF16)

    own = (w_col[...] * x[...].astype(F32)).astype(BF16)
    own_out[...] = own
    rest[...] = jnp.zeros_like(rest)
    rest[0:nc, :] = dot(basis[...], own)
    rest[SLOT : 2 * SLOT, :] = dot(low_qb[0:ROWS, :], x[0:fs])[0:SLOT]
    rest[2 * SLOT : 3 * SLOT, :] = dot(high_qb[0:ROWS, :], x[fs:half])[0:SLOT]


def near_stage(weights, orders, basis, low_qb, high_qb, x, width):
    nb, m = x.shape
    fs = nb // 4
    col = lambda n: pl.BlockSpec((n, width), lambda i: (0, i))
    return pl.pallas_call(
        functools.partial(near_kernel, fs),
        grid=(m // width,),
        in_specs=[whole(a.shape) for a in (weights, orders, basis, low_qb, high_qb)] + [col(nb)],
        out_specs=[col(nb), col(LANES), whole((4, fs, fs)), whole((nb, 1)), whole((nb, LANES))],
        out_shape=[
            jax.ShapeDtypeStruct((nb, m), BF16),
            jax.ShapeDtypeStruct((LANES, m), F32),
            jax.ShapeDtypeStruct((4, fs, fs), BF16),
            jax.ShapeDtypeStruct((nb, 1), F32),
            jax.ShapeDtypeStruct((nb, LANES), BF16),
        ],
        compiler_params=params(),
        cost_estimate=FREE,
        name="near_stage",
    )(weights, orders, basis, low_qb, high_qb, x)


def met(picks, w_col, faces):
    fs = picks.shape[1]
    each = [
        (w_col[i * fs : (i + 1) * fs, :] * dot(picks[i], face)).astype(BF16) for i, face in enumerate(faces)
    ]
    return jnp.concatenate(each, axis=0)


def load_kernel(cols, basis, ids, picks, w_col, rest, from_left, from_right, other_out, load, digits):
    nc, nb = basis.shape
    fs = nb // 4

    @pl.when(pl.program_id(0) == 0)
    def _():
        digits[...] = jnp.zeros_like(digits)
        high = jnp.right_shift(ids[...], 4)
        digits[0:1, 0:nc] = high.astype(F32)
        digits[1:2, 0:nc] = (ids[...] - high * BASE).astype(F32)

    other = met(picks, w_col, (from_left[0:fs, :], from_right[0:fs, :]))
    other_out[...] = other
    mine = dot(basis[:, nb // 2 :], other)
    mine = jnp.concatenate([mine, jnp.zeros((LANES - nc, mine.shape[1]), F32)], axis=0)
    turned = (rest[...] + mine).T.astype(BF16)
    for block in range(load.shape[0]):
        load[block, 0:cols, :] = turned[block * cols : (block + 1) * cols]
        load[block, cols:, :] = digits[...].astype(BF16)


def load_stage(basis, ids, picks, w_col, rest, from_left, from_right, subs, width):
    m = rest.shape[1]
    nb = w_col.shape[0]
    fs = nb // 4
    cols = m // subs
    col = lambda n: pl.BlockSpec((n, width), lambda i: (0, i))
    return pl.pallas_call(
        functools.partial(load_kernel, cols),
        grid=(m // width,),
        in_specs=[
            whole(basis.shape),
            whole(ids.shape),
            pl.BlockSpec((2, fs, fs), lambda i: (1, 0, 0)),
            pl.BlockSpec((2 * fs, 1), lambda i: (1, 0)),
            col(LANES),
            col(fs + ROWS),
            col(fs + ROWS),
        ],
        out_specs=[col(2 * fs), pl.BlockSpec((width // cols, cols + 16, LANES), lambda i: (i, 0, 0))],
        out_shape=[
            jax.ShapeDtypeStruct((2 * fs, m), BF16),
            jax.ShapeDtypeStruct((subs, cols + 16, LANES), BF16),
        ],
        scratch_shapes=[pltpu.VMEM((16, LANES), F32)],
        compiler_params=params(),
        cost_estimate=FREE,
        name="load_stage",
    )(basis, ids, picks, w_col, rest, from_left, from_right)


def acc_kernel(half, inverse, own, other, acc):
    acc[...] = dot(inverse[...], own[...]) + dot(inverse[:, half:], other[...])


def acc_stage(inverse, own, other, tall):
    nb, m = own.shape
    row = lambda n: pl.BlockSpec((tall, n), lambda i: (i, 0))
    return pl.pallas_call(
        functools.partial(acc_kernel, nb // 2),
        grid=(nb // tall,),
        in_specs=[row(nb), whole(own.shape), whole(other.shape)],
        out_specs=row(m),
        out_shape=jax.ShapeDtypeStruct((nb, m), F32),
        compiler_params=params(),
        cost_estimate=FREE,
        name="acc_stage",
    )(inverse, own, other)


def coded(values, q_ref):
    fs = values.shape[0]
    top = jnp.max(jnp.abs(values), axis=0, keepdims=True)
    power = jnp.floor(jnp.log2(jnp.maximum(top, 1e-30))) - 13.0
    q_ref[0:fs, :] = jnp.round(values * jnp.exp2(-power)).astype(I32).astype(I16)
    q_ref[fs:, :] = jnp.broadcast_to(power.astype(I32), (EXTRA, values.shape[1])).astype(I16)


def part_kernel(fs, picks, w_col, inverse, low, high, acc, part, q_one, q_two, other_out, other):
    @pl.when(pl.program_id(0) == 0)
    def _():
        other[...] = met(picks, w_col, (low[...], high[...]))
        other_out[...] = other[...]

    total = acc[...] + dot(inverse[...], other[...])
    part[...] = total
    for face, q in enumerate((q_one, q_two)):
        pl.when(pl.program_id(0) == face)(functools.partial(coded, total, q))


def part_stage(picks, w_col, inverse, low, high, acc):
    nb, m = acc.shape
    fs, half = nb // 4, nb // 2
    row = lambda n: spec((fs, n), lambda i: (i, 0))
    code = jax.ShapeDtypeStruct((fs + EXTRA, m), I16)
    return pl.pallas_call(
        functools.partial(part_kernel, fs),
        grid=(2,),
        in_specs=[
            spec((2, fs, fs), lambda i: (0, 0, 0)),
            spec((half, 1), lambda i: (0, 0)),
            row(half),
            whole(low.shape),
            whole(high.shape),
            row(m),
        ],
        out_specs=[row(m), whole(code.shape), whole(code.shape), whole((half, m))],
        out_shape=[jax.ShapeDtypeStruct((half, m), F32), code, code, jax.ShapeDtypeStruct((half, m), BF16)],
        scratch_shapes=[pltpu.VMEM((half, m), BF16)],
        compiler_params=params(),
        cost_estimate=FREE,
        name="part_stage",
    )(picks, w_col, inverse, low, high, acc)


def part_grp_kernel(inverse, other, acc, part, q_one, q_two):
    total = acc[...] + dot(inverse[...], other[...])
    part[...] = total
    for face, q in enumerate((q_one, q_two)):
        pl.when(pl.program_id(0) == face)(functools.partial(coded, total, q))


def part_grp_stage(inverse, other, acc):
    nb, m = acc.shape
    fs, half = nb // 4, nb // 2
    code = jax.ShapeDtypeStruct((fs + EXTRA, m), I16)
    return pl.pallas_call(
        part_grp_kernel,
        grid=(2,),
        in_specs=[
            spec((fs, half), lambda i: (2 + i, 0)),
            whole(other.shape),
            spec((fs, m), lambda i: (2 + i, 0)),
        ],
        out_specs=[spec((fs, m), lambda i: (i, 0)), whole(code.shape), whole(code.shape)],
        out_shape=[jax.ShapeDtypeStruct((half, m), F32), code, code],
        compiler_params=params(),
        cost_estimate=FREE,
        name="part_grp_stage",
    )(inverse, other, acc)


def widened(basis_in, slots, basis, slot_row):
    nc2 = basis_in.shape[0]
    basis[...] = jnp.zeros_like(basis)
    basis[0:nc2, :] = basis_in[...]
    slot_row[...] = jnp.full_like(slot_row, -1.0)
    slot_row[0:1, 0:nc2] = slots[...].astype(F32)


def group_kernel(nc, loads, inverse, basis_in, slots, local_out, send, index_out, basis, slot_row):
    widened(basis_in, slots, basis, slot_row)
    subs, rows, _ = loads.shape
    cols = rows - 16
    size = inverse.shape[0]
    digits = jnp.stack([loads[s, cols : cols + 8, :].astype(F32) for s in range(subs)])
    own = (digits[:, 0, :] * BASE + digits[:, 1, :]).astype(I32)
    before = pltpu.roll(jnp.concatenate([own[0:1], own[: subs - 1]], axis=0), SLOT, 1)
    after = pltpu.roll(jnp.concatenate([own[1:], own[subs - 1 :]], axis=0), 2 * SLOT, 1)
    in_zero = lanes_between(own.shape, 0, nc)
    in_one = lanes_between(own.shape, SLOT, SLOT + nc)
    in_two = lanes_between(own.shape, 2 * SLOT, 2 * SLOT + nc)
    index = jnp.where(in_zero, own, jnp.where(in_one, before, jnp.where(in_two, after, -1)))
    index_out[...] = index
    total = jnp.zeros((cols, size), F32)
    for s in range(0, subs, 2):
        pair = jnp.concatenate([loads[s, 0:cols, :], loads[s + 1, 0:cols, :]], axis=1)
        row = jnp.concatenate([index[s : s + 1], index[s + 1 : s + 2]], axis=1)
        total = total + dot(pair, one_hot_lanes(size, row).astype(BF16), ((1,), (1,)))
    exact = lax.Precision.HIGHEST
    local_out[...] = dot(total, inverse[...], ((1,), (1,)), exact)
    coarse = dot(total, basis[...], ((1,), (1,)), exact)
    for g in range(send.shape[0]):
        send[g, 0:cols, :] = coarse
        send[g, cols:, :] = jnp.broadcast_to(slot_row[...], (8, LANES))


def group_stage(loads, inverse, basis, slots, nc, groups):
    subs, rows, _ = loads.shape
    cols = rows - 16
    size = inverse.shape[0]
    return pl.pallas_call(
        functools.partial(group_kernel, nc),
        out_shape=[
            jax.ShapeDtypeStruct((cols, size), F32),
            jax.ShapeDtypeStruct((groups, cols + 8, LANES), F32),
            jax.ShapeDtypeStruct((subs, LANES), I32),
        ],
        scratch_shapes=[pltpu.VMEM((LANES, size), F32), pltpu.VMEM((1, LANES), F32)],
        compiler_params=params(),
        cost_estimate=FREE,
        name="group_stage",
    )(loads, inverse, basis, slots)


def coarse_kernel(received, local_in, basis_in, slots, coarse_in, index, send, basis, slot_row, coarse_inverse):
    widened(basis_in, slots, basis, slot_row)
    n3 = coarse_in.shape[0]
    coarse_inverse[...] = jnp.zeros_like(coarse_inverse)
    coarse_inverse[0:n3, 0:n3] = coarse_in[...]
    groups = received.shape[0]
    cols, size = local_in.shape
    exact = lax.Precision.HIGHEST
    wide = coarse_inverse.shape[0]
    rhs = jnp.zeros((cols, wide), F32)
    for g in range(groups):
        theirs = received[g, cols : cols + 1, :].astype(I32)
        rhs = rhs + dot(received[g, 0:cols, :], one_hot_lanes(wide, theirs), ((1,), (1,)), exact)
    sol = dot(rhs, coarse_inverse[...], ((1,), (1,)), exact)
    here = dot(sol, one_hot_lanes(wide, slot_row[...].astype(I32)), ((1,), (0,)), exact)
    group_sol = local_in[...] + dot(here, basis[...], ((1,), (0,)), exact)
    rounded = group_sol.astype(BF16)
    for s in range(0, send.shape[0], 2):
        row = jnp.concatenate([index[s : s + 1, :], index[s + 1 : s + 2, :]], axis=1)
        both = dot(rounded, one_hot_lanes(size, row).astype(BF16)).astype(BF16)
        send[s] = both[:, 0:LANES]
        send[s + 1] = both[:, LANES:]


def coarse_stage(received, local_in, basis, slots, coarse_inverse, index):
    subs = index.shape[0]
    cols, size = local_in.shape
    wide = -(-coarse_inverse.shape[0] // LANES) * LANES
    return pl.pallas_call(
        coarse_kernel,
        out_shape=jax.ShapeDtypeStruct((subs, cols, LANES), BF16),
        scratch_shapes=[pltpu.VMEM((LANES, size), F32), pltpu.VMEM((1, LANES), F32), pltpu.VMEM((wide, wide), F32)],
        compiler_params=params(),
        cost_estimate=FREE,
        name="coarse_stage",
    )(received, local_in, basis, slots, coarse_inverse, index)


def into(kernel, target, args, in_specs):
    if target is None:
        return kernel, args, in_specs
    return (lambda _, *refs: kernel(*refs)), [target] + args, [pl.BlockSpec(memory_space=pl.ANY)] + in_specs


def last_kernel(fs, offsets, *refs):
    picks, w_col, basis_t, part, primal, near, far, near_p, far_p, near_q, far_q, out, lifts = refs

    @pl.when(pl.program_id(0) == 0)
    def _():
        for face, rows in enumerate((near, far)):
            lifts[face] = on_lanes(rows[0:SLOT, 0:fs].astype(F32), offsets[face])

    nt = ((1,), (1,))
    for face, (primal_n, q) in enumerate(((near_p, near_q), (far_p, far_q))):
        at = slice(face * fs, (face + 1) * fs)
        mine = (part[at] + dot(basis_t[at], primal[...], nt)).astype(BF16)
        scale = jnp.exp2(q[fs:, :].astype(I32).astype(F32)[0:1])
        theirs = q[0:fs, :].astype(I32).astype(F32) * scale
        theirs = (theirs + dot(lifts[face], primal_n[...], nt)).astype(BF16)
        arrived = dot(picks[face], theirs)
        out[at] = (w_col[at] * (mine.astype(F32) + arrived)).astype(BF16)


def last_stage(place, offsets, row, picks, w_col, basis_t, part, primal, near, far, near_p, far_p, codes, target=None):
    half, m = part.shape
    fs = half // 2
    width = m // 2
    lane = pl.BlockSpec((width, LANES), lambda i: (i, 0))
    mine = lambda k: pl.BlockSpec((half, k), lambda i: (place, 0))
    rows = spec((ROWS, fs), lambda i: (row // ROWS, 0))
    in_specs = [pl.BlockSpec((2, fs, fs), lambda i: (place, 0, 0)), mine(1), mine(LANES), spec((half, width), lambda i: (0, i)), lane, rows, rows, lane, lane]
    in_specs += [pl.BlockSpec((fs + EXTRA, width), lambda i: (0, i))] * 2
    args = [picks, w_col, basis_t, part, primal, near, far, near_p, far_p, *codes]
    kernel, args, in_specs = into(functools.partial(last_kernel, fs, offsets), target, args, in_specs)
    return pl.pallas_call(
        kernel,
        grid=(2,),
        in_specs=in_specs,
        out_specs=spec((half, width), lambda i: (place, i)),
        out_shape=jax.ShapeDtypeStruct((2 * half, m), BF16),
        scratch_shapes=[pltpu.VMEM((2, fs, LANES), BF16)],
        input_output_aliases={} if target is None else {0: 0},
        compiler_params=params(),
        cost_estimate=FREE,
        name="last_stage",
    )(*args)


def exchange(faces, axis):
    size = lax.axis_size(axis)
    up = [(i, i + 1) for i in range(size - 1)]
    down = [(j, i) for i, j in up]
    return lax.ppermute(faces[1], axis, up), lax.ppermute(faces[0], axis, down)


def together(*values):
    return lax.optimization_barrier(values)


def local(
    residual,
    weights,
    face_map,
    local_inverse,
    basis,
    primal_index,
    group_inverse,
    group_basis,
    group_index,
    coarse_inverse,
):
    x = residual[0, 0]
    nb, m = x.shape
    nc = basis.shape[2]
    subs, groups = lax.axis_size("sub"), lax.axis_size("grp")
    inverse = local_inverse[0, 0]
    w_row = weights[0]
    orders = face_map[0, 0]
    coarse_rows = basis[0, 0]

    low_out, high_out, face_one, face_two = first_stage(x, w_row, orders, coarse_rows)
    low_qb, high_qb = exchange((low_out, high_out), "sub")
    low, high = exchange((face_one, face_two), "sub")
    left, right = exchange(cut(x, coarse_rows), "grp")

    own, rest, picks, w_col, basis_t = near_stage(w_row, orders, coarse_rows, low_qb, high_qb, x, min(512, m))
    other_grp, load = load_stage(coarse_rows, primal_index[0], picks, w_col, rest, left, right, subs, min(512, m))
    loads = lax.all_to_all(load, "sub", 0, 0, tiled=True)
    acc = acc_stage(inverse, own, other_grp, nb // 4)
    low, high, acc = together(low, high, acc)
    part_sub, q_one, q_two, other_sub = part_stage(picks, w_col, inverse, low, high, acc)
    q_low, q_high = exchange((q_one, q_two), "sub")

    loads, part_sub = together(loads, part_sub)
    group_local, send, index = group_stage(loads, group_inverse[0], group_basis[0], group_index, nc, groups)
    received = lax.all_to_all(send, "grp", 0, 0, tiled=True)
    other_sub, send = together(other_sub, send)
    part_grp, q_three, q_four = part_grp_stage(inverse, other_sub, acc)
    q_left, q_right = exchange((q_three, q_four), "grp")
    received, part_grp = together(received, part_grp)
    picked = coarse_stage(received, group_local, group_basis[0], group_index, coarse_inverse, index)
    primal = lax.all_to_all(picked, "sub", 0, 0, tiled=True).reshape(m, LANES)
    primal, q_low, q_high = together(primal, q_low, q_high)
    primal_left, primal_right = exchange((primal, primal), "grp")

    mine = (picks, w_col, basis_t)
    out = last_stage(0, (SLOT, 2 * SLOT), ROWS, *mine, part_sub, primal, low_qb, high_qb, primal, primal, (q_low, q_high))
    out = last_stage(
        1, (0, 0), nb // 4, *mine, part_grp, primal, left, right, primal_left, primal_right, (q_left, q_right), out
    )
    return out[None, None]


def solution(mesh):
    placed = (
        P("sub", "grp", None, None),
        P("sub", "grp", None),
        P("sub", "grp", None, None),
        P("sub", "grp", None, None),
        P("sub", "grp", None, None),
        P("sub", "grp", None),
        P("grp", None, None),
        P("grp", None, None),
        P("grp", None),
        P(),
    )
    return jax.shard_map(
        local, mesh=mesh, in_specs=placed, out_specs=P("sub", "grp", None, None), check_vma=False
    )
```

time: 749 us -> 178 us (0.24)
  the two profiles are of different devices: /device:TPU:15 before, /device:TPU:1 now
where the time goes in v1:
time: 178 us; the launch traced here: 177 us
  starting transfers between devices  101 us (57%)
  Pallas kernels  62.1 us (35%)
  waiting for transfers between devices  11.9 us (7%)
    all_to_all x1, starting transfers between devices, local(): primal = lax.all_to_all(picked, 'sub', 0, 0, tiled=True).reshape(m, LANES)  35.7 us
    ppermute x6, starting transfers between devices, exchange(): lax.ppermute(faces[1], axis, up)  23 us
    all_to_all x1, starting transfers between devices, local(): loads = lax.all_to_all(load, 'sub', 0, 0, tiled=True)  21.9 us
    ppermute x6, starting transfers between devices, exchange(): lax.ppermute(faces[0], axis, down)  12.4 us
    pallas_call x1, Pallas kernels, acc_stage(): pl.pallas_call(functools.partial(acc_kernel, nb // 2), grid=(nb // tall,)...  11.9 us
    all_to_all x1, waiting for transfers between devices, local(): primal = lax.all_to_all(picked, 'sub', 0, 0, tiled=True).reshape(m, LANES)  11.9 us
    pallas_call x2, Pallas kernels, last_stage(): pl.pallas_call(kernel, grid=(2,), in_specs=in_specs, out_specs=spec((half...  11.5 us
    all_to_all x1, starting transfers between devices, local(): received = lax.all_to_all(send, 'grp', 0, 0, tiled=True)  8.22 us
  transfers between devices with their start and end apart: 15, of which 1 were waited for; matrix products, arithmetic and copies ran while one was open for 1% of the time, Pallas kernels for 30%

profile of v1, /device:TPU:1, one launch (start us, length us, event | category | flops | bytes accessed | tf_op | source)
XLA Modules:
  0.0 176.9 jit_solution(4248529472673589806)
XLA Ops:
  0.0 2.5 %cut.1 = (bf16[432,1024]{1,0:T(8,128)(2,1)}, bf16[432,1024]{1,0:T(8,128)(2,1)}) custom-call(bf16[37,1536]{1,0:T(8,128)(2,1)} %bitcast.20, bf16[1536,1024]{1,0:T(8,128)(2,1)} %bitcast.12, bf16[1536,1024]{1,0:T(8,128)(2,1)} %bitcast.13), custom_call_target="tpu_custom_call" | custom-call | tf_op jit(solution)/shard_map/cut/pallas_call | solution.py:97
  2.5 4.9 %collective-permute-start.2 = (bf16[432,1024]{1,0:T(8,128)(2,1)}, bf16[432,1024]{1,0:T(8,128)(2,1)}, u32[]{:S(2)}, u32[]{:S(2)}) collective-permute-start(bf16[432,1024]{1,0:T(8,128)(2,1)} %get-tuple-element.45), channel_id=1, source_target_pairs={{0,1},{1,2},{2,3},{3,4},{4,5},{5,6},{6,7},{8,9},{9,10},{10,11},{11... | collective-permute-start | bytes 2654216 | tf_op jit(solution)/shard_map/ppermute | solution.py:453
  7.4 2.4 %collective-permute-start.3 = (bf16[432,1024]{1,0:T(8,128)(2,1)}, bf16[432,1024]{1,0:T(8,128)(2,1)}, u32[]{:S(2)}, u32[]{:S(2)}) collective-permute-start(bf16[432,1024]{1,0:T(8,128)(2,1)} %get-tuple-element.46), channel_id=1, source_target_pairs={{1,0},{2,1},{3,2},{4,3},{5,4},{6,5},{7,6},{9,8},{10,9},{11,10},{12... | collective-permute-start | bytes 2654216 | tf_op jit(solution)/shard_map/ppermute | solution.py:453
  9.8 2.8 %first_stage.1 = (bf16[96,384]{1,0:T(8,128)(2,1)}, bf16[96,384]{1,0:T(8,128)(2,1)}, bf16[384,1024]{1,0:T(8,128)(2,1)}, bf16[384,1024]{1,0:T(8,128)(2,1)}) custom-call(f32[1,1536]{1,0:T(1,128)} %bitcast.27, s32[4,384]{1,0:T(4,128)} %bitcast.29, bf16[37,1536]{1,0:T(8,128)(2,1)} %bitcast.21, bf16[1536,1024]{1,0:T(8,128)(2,1)} %bitcast.14, ...), custom_call_target="tpu_custom_call" | custom-call | tf_op jit(solution)/shard_map/first_stage/pallas_call | solution.py:69
  12.7 3.2 %collective-permute-start = (bf16[96,384]{1,0:T(8,128)(2,1)}, bf16[96,384]{1,0:T(8,128)(2,1)}, u32[]{:S(2)}, u32[]{:S(2)}) collective-permute-start(bf16[96,384]{1,0:T(8,128)(2,1)} %get-tuple-element.39), channel_id=1, source_target_pairs={{0,8},{8,16},{16,24},{24,32},{32,40},{40,48},{48,56},{56,64},{64,7... | collective-permute-start | bytes 221192 | tf_op jit(solution)/shard_map/ppermute | solution.py:453
  15.9 1.3 collective-permute-start.1
  17.2 4.9 %collective-permute-start.4 = (bf16[384,1024]{1,0:T(8,128)(2,1)}, bf16[384,1024]{1,0:T(8,128)(2,1)}, u32[]{:S(2)}, u32[]{:S(2)}) collective-permute-start(bf16[384,1024]{1,0:T(8,128)(2,1)} %get-tuple-element.48), channel_id=1, source_target_pairs={{0,8},{8,16},{16,24},{24,32},{32,40},{40,48},{48,56},{56,64},{64,7... | collective-permute-start | bytes 2359304 | tf_op jit(solution)/shard_map/ppermute | solution.py:453
  22.1 0.0 collective-permute-done.low_qb.refs_5_
  22.1 1.3 collective-permute-start.5
  23.4 0.0 collective-permute-done.1.high_qb.refs_6_
  23.4 5.3 %near_stage.1 = (bf16[1536,1024]{1,0:T(8,128)(2,1)}, f32[128,1024]{1,0:T(8,128)}, bf16[4,384,384]{2,1,0:T(8,128)(2,1)}, f32[1536,1]{1,0:T(8,128)}, bf16[1536,128]{1,0:T(8,128)(2,1)}) custom-call(f32[1,1536]{1,0:T(1,128)} %bitcast.28, s32[4,384]{1,0:T(4,128)} %bitcast.30, bf16[37,1536]{1,0:T(8,128)(2,1)} %bitcast.22, ...), custom_call_target="tpu_custom_call" | custom-call | tf_op jit(solution)/shard_map/near_stage/pallas_call | solution.py:140
  28.7 0.0 collective-permute-done.2.from_left.refs_5_
  28.7 0.0 collective-permute-done.3.from_right.refs_6_
  28.8 4.2 %load_stage.1 = (bf16[768,1024]{1,0:T(8,128)(2,1)}, bf16[32,48,128]{2,1,0:T(8,128)(2,1)}) custom-call(bf16[37,1536]{1,0:T(8,128)(2,1)} %bitcast.23, s32[1,37]{1,0:T(1,128)} %bitcast.31, bf16[4,384,384]{2,1,0:T(8,128)(2,1)} %get-tuple-element.41.picks.refs_0_, f32[1536,1]{1,0:T(8,128)} %get-tuple-element.42.w_col.refs_1_, ...), custom_call_target="tpu_custom_call" | custom-call | tf_op jit(solution)/shard_map/load_stage/pallas_call | solution.py:193
  32.9 21.9 %all-to-all-start = ((bf16[32,48,128]{2,1,0:T(8,128)(2,1)}), bf16[32,48,128]{2,1,0:T(8,128)(2,1)}, u32[]{:S(2)}, u32[]{:S(2)}) async-start(bf16[32,48,128]{2,1,0:T(8,128)(2,1)} %get-tuple-element.47), calls=%async_computation | async-start | bytes 786432 | tf_op jit(solution)/shard_map/all_to_all | solution.py:488
  54.9 11.9 %acc_stage.1.acc = f32[1536,1024]{1,0:T(8,128)} custom-call(bf16[1536,1536]{1,0:T(8,128)(2,1)} %bitcast.17, bf16[1536,1024]{1,0:T(8,128)(2,1)} %get-tuple-element.50.own, bf16[768,1024]{1,0:T(8,128)(2,1)} %get-tuple-element.51.other), custom_call_target="tpu_custom_call" | custom-call | tf_op jit(solution)/shard_map/acc_stage/pallas_call | solution.py:224
  66.8 0.0 collective-permute-done.4.low
  66.8 0.0 collective-permute-done.5.high
  66.8 7.8 %part_stage.1 = (f32[768,1024]{1,0:T(8,128)}, s16[400,1024]{1,0:T(8,128)(2,1)}, s16[400,1024]{1,0:T(8,128)(2,1)}, bf16[768,1024]{1,0:T(8,128)(2,1)}) custom-call(bf16[4,384,384]{2,1,0:T(8,128)(2,1)} %get-tuple-element.41.picks.refs_0_, f32[1536,1]{1,0:T(8,128)} %get-tuple-element.42.w_col.refs_1_, bf16[1536,1536]{1,0:T(8,128)(2,1)} %bitcast.18, ...), custom_call_target="tpu_custom_call" | custom-call | tf_op jit(solution)/shard_map/part_stage/pallas_call | solution.py:261
  74.6 4.0 %collective-permute-start.6 = (s16[400,1024]{1,0:T(8,128)(2,1)}, s16[400,1024]{1,0:T(8,128)(2,1)}, u32[]{:S(2)}, u32[]{:S(2)}) collective-permute-start(s16[400,1024]{1,0:T(8,128)(2,1)} %get-tuple-element.65), channel_id=1, source_target_pairs={{0,8},{8,16},{16,24},{24,32},{32,40},{40,48},{48,56},{56,64},{64,7... | collective-permute-start | bytes 2457608 | tf_op jit(solution)/shard_map/ppermute | solution.py:453
  78.6 1.3 collective-permute-start.7
  79.9 1.5 copy.14
  81.4 0.0 all-to-all-done.loads
  81.4 4.5 %group_stage.1 = (f32[32,512]{1,0:T(8,128)}, f32[8,40,128]{2,1,0:T(8,128)}, s32[32,128]{1,0:T(8,128)}) custom-call(bf16[32,48,128]{2,1,0:T(8,128)(2,1)} %all-to-all-done.loads, f32[512,512]{1,0:T(8,128)} %bitcast.24, f32[37,512]{1,0:T(8,128)} %bitcast.25, s32[1,37]{1,0:T(1,128)} %slots.3), custom_call_target="tpu_custom_call" | custom-call | tf_op jit(solution)/shard_map/group_stage/pallas_call | solution.py:347
  85.9 8.2 %all-to-all-start.1 = ((f32[8,40,128]{2,1,0:T(8,128)}), f32[8,40,128]{2,1,0:T(8,128)}, u32[]{:S(2)}, u32[]{:S(2)}) async-start(f32[8,40,128]{2,1,0:T(8,128)} %get-tuple-element.58), calls=%async_computation.1 | async-start | bytes 327680 | tf_op jit(solution)/shard_map/all_to_all | solution.py:496
  94.1 6.0 %part_grp_stage.1 = (f32[768,1024]{1,0:T(8,128)}, s16[400,1024]{1,0:T(8,128)(2,1)}, s16[400,1024]{1,0:T(8,128)(2,1)}) custom-call(bf16[1536,1536]{1,0:T(8,128)(2,1)} %bitcast.19, bf16[768,1024]{1,0:T(8,128)(2,1)} %get-tuple-element.60.other, f32[1536,1024]{1,0:T(8,128)} %acc_stage.1.acc), custom_call_target="tpu_custom_call" | custom-call | tf_op jit(solution)/shard_map/part_grp_stage/pallas_call | solution.py:292
  100.1 3.5 %collective-permute-start.10 = (s16[400,1024]{1,0:T(8,128)(2,1)}, s16[400,1024]{1,0:T(8,128)(2,1)}, u32[]{:S(2)}, u32[]{:S(2)}) collective-permute-start(s16[400,1024]{1,0:T(8,128)(2,1)} %get-tuple-element.71), channel_id=1, source_target_pairs={{0,1},{1,2},{2,3},{3,4},{4,5},{5,6},{6,7},{8,9},{9,10},{10,11},{11... | collective-permute-start | bytes 2457608 | tf_op jit(solution)/shard_map/ppermute | solution.py:453
  103.7 2.1 %collective-permute-start.11 = (s16[400,1024]{1,0:T(8,128)(2,1)}, s16[400,1024]{1,0:T(8,128)(2,1)}, u32[]{:S(2)}, u32[]{:S(2)}) collective-permute-start(s16[400,1024]{1,0:T(8,128)(2,1)} %get-tuple-element.72), channel_id=1, source_target_pairs={{1,0},{2,1},{3,2},{4,3},{5,4},{6,5},{7,6},{9,8},{10,9},{11,10},{12... | collective-permute-start | bytes 2457608 | tf_op jit(solution)/shard_map/ppermute | solution.py:453
  105.8 0.0 all-to-all-done.1.received
  105.8 5.6 %coarse_stage.1 = bf16[32,32,128]{2,1,0:T(8,128)(2,1)} custom-call(f32[8,40,128]{2,1,0:T(8,128)} %all-to-all-done.1.received, f32[32,512]{1,0:T(8,128)} %get-tuple-element.63.local_in, f32[37,512]{1,0:T(8,128)} %bitcast.26, s32[1,37]{1,0:T(1,128)} %slots.3, f32[148,148]{1,0:T(8,128)} %coarse_in.1, s32[32,128]{1,0:T(8,128)} %get-tuple-element.64.index), custom_call_target="tpu_custom_call" | custom-call | tf_op jit(solution)/shard_map/coarse_stage/pallas_call | solution.py:389
  111.4 35.7 %all-to-all-start.2 = ((bf16[32,32,128]{2,1,0:T(8,128)(2,1)}), bf16[32,32,128]{2,1,0:T(8,128)(2,1)}, u32[]{:S(2)}, u32[]{:S(2)}) async-start(bf16[32,32,128]{2,1,0:T(8,128)(2,1)} %coarse_stage.1), calls=%async_computation.2 | async-start | bytes 524288 | tf_op jit(solution)/shard_map/all_to_all | solution.py:502
  147.0 0.0 collective-permute-done.6.refs_9_
  147.1 0.0 collective-permute-done.7.refs_10_
  147.1 11.9 %all-to-all-done.2 = bf16[32,32,128]{2,1,0:T(8,128)(2,1)} async-done(((bf16[32,32,128]{2,1,0:T(8,128)(2,1)}), bf16[32,32,128]{2,1,0:T(8,128)(2,1)}, u32[]{:S(2)}, u32[]{:S(2)}) %all-to-all-start.2) | async-done | bytes 262176 | tf_op jit(solution)/shard_map/all_to_all | solution.py:502
  158.9 4.0 %collective-permute-start.9 = (bf16[1024,128]{1,0:T(8,128)(2,1)}, bf16[1024,128]{1,0:T(8,128)(2,1)}, u32[]{:S(2)}, u32[]{:S(2)}) collective-permute-start(bf16[1024,128]{1,0:T(8,128)(2,1)} %bitcast.7.refs_4_.refs_7_.refs_8_), channel_id=1, source_target_pairs={{1,0},{2,1},{3,2},{4,3},{5,4},{6,5},{7,6},{9,8},{10,9},{11,10},{12... | collective-permute-start | bytes 786440 | tf_op jit(solution)/shard_map/ppermute | solution.py:453
  162.9 2.4 %collective-permute-start.8 = (bf16[1024,128]{1,0:T(8,128)(2,1)}, bf16[1024,128]{1,0:T(8,128)(2,1)}, u32[]{:S(2)}, u32[]{:S(2)}) collective-permute-start(bf16[1024,128]{1,0:T(8,128)(2,1)} %bitcast.7.refs_4_.refs_7_.refs_8_), channel_id=1, source_target_pairs={{0,1},{1,2},{2,3},{3,4},{4,5},{5,6},{6,7},{8,9},{9,10},{10,11},{11... | collective-permute-start | bytes 786440 | tf_op jit(solution)/shard_map/ppermute | solution.py:453
  165.3 5.8 %last_stage.2._ = bf16[1536,1024]{1,0:T(8,128)(2,1)} custom-call(bf16[4,384,384]{2,1,0:T(8,128)(2,1)} %get-tuple-element.41.picks.refs_0_, f32[1536,1]{1,0:T(8,128)} %get-tuple-element.42.w_col.refs_1_, bf16[1536,128]{1,0:T(8,128)(2,1)} %get-tuple-element.43.refs_2_, f32[768,1024]{1,0:T(8,128)} %get-tuple-element.56.refs_3_, ...), custom_call_target="tpu_custom_call" | custom-call | tf_op jit(solution)/shard_map/last_stage/pallas_call | solution.py:435
  171.1 0.0 collective-permute-done.10.refs_9_
  171.1 0.0 collective-permute-done.11.refs_10_
  171.1 0.0 collective-permute-done.9.refs_8_
  171.1 0.0 collective-permute-done.8.refs_7_
  171.1 5.8 %last_stage.3 = bf16[1536,1024]{1,0:T(8,128)(2,1)} custom-call(bf16[1536,1024]{1,0:T(8,128)(2,1)} %last_stage.2._, bf16[4,384,384]{2,1,0:T(8,128)(2,1)} %get-tuple-element.41.picks.refs_0_, f32[1536,1]{1,0:T(8,128)} %get-tuple-element.42.w_col.refs_1_, bf16[1536,128]{1,0:T(8,128)(2,1)} %get-tuple-element.43.refs_2_, ...), custom_call_target="tpu_custom_call", output_to_operand_aliasing={{}: (0, {})} | custom-call | tf_op jit(solution)/shard_map/last_stage/pallas_call | solution.py:435
Async XLA Ops:
  2.5 26.3 %collective-permute-start.2 = (bf16[432,1024]{1,0:T(8,128)(2,1)}, bf16[432,1024]{1,0:T(8,128)(2,1)}, u32[]{:S(2)}, u32[]{:S(2)}) collective-permute-start(bf16[432,1024]{1,0:T(8,128)(2,1)} %get-tuple-element.45), channel_id=1, source_target_pairs={{0,1},{1,2},{2,3},{3,4},{4,5},{5,6},{6,7},{8,9},{9,10},{10,11},{11... | collective-permute-start | bytes 2654216 | tf_op jit(solution)/shard_map/ppermute | solution.py:453
  7.4 21.3 %collective-permute-start.3 = (bf16[432,1024]{1,0:T(8,128)(2,1)}, bf16[432,1024]{1,0:T(8,128)(2,1)}, u32[]{:S(2)}, u32[]{:S(2)}) collective-permute-start(bf16[432,1024]{1,0:T(8,128)(2,1)} %get-tuple-element.46), channel_id=1, source_target_pairs={{1,0},{2,1},{3,2},{4,3},{5,4},{6,5},{7,6},{9,8},{10,9},{11,10},{12... | collective-permute-start | bytes 2654216 | tf_op jit(solution)/shard_map/ppermute | solution.py:453
  12.7 9.4 %collective-permute-start = (bf16[96,384]{1,0:T(8,128)(2,1)}, bf16[96,384]{1,0:T(8,128)(2,1)}, u32[]{:S(2)}, u32[]{:S(2)}) collective-permute-start(bf16[96,384]{1,0:T(8,128)(2,1)} %get-tuple-element.39), channel_id=1, source_target_pairs={{0,8},{8,16},{16,24},{24,32},{32,40},{40,48},{48,56},{56,64},{64,7... | collective-permute-start | bytes 221192 | tf_op jit(solution)/shard_map/ppermute | solution.py:453
  15.9 7.5 %collective-permute-start.1 = (bf16[96,384]{1,0:T(8,128)(2,1)}, bf16[96,384]{1,0:T(8,128)(2,1)}, u32[]{:S(2)}, u32[]{:S(2)}) collective-permute-start(bf16[96,384]{1,0:T(8,128)(2,1)} %get-tuple-element.40), channel_id=1, source_target_pairs={{8,0},{16,8},{24,16},{32,24},{40,32},{48,40},{56,48},{64,56},{72,6... | collective-permute-start | bytes 221192 | tf_op jit(solution)/shard_map/ppermute | solution.py:453
  17.2 49.6 %collective-permute-start.4 = (bf16[384,1024]{1,0:T(8,128)(2,1)}, bf16[384,1024]{1,0:T(8,128)(2,1)}, u32[]{:S(2)}, u32[]{:S(2)}) collective-permute-start(bf16[384,1024]{1,0:T(8,128)(2,1)} %get-tuple-element.48), channel_id=1, source_target_pairs={{0,8},{8,16},{16,24},{24,32},{32,40},{40,48},{48,56},{56,64},{64,7... | collective-permute-start | bytes 2359304 | tf_op jit(solution)/shard_map/ppermute | solution.py:453
  22.1 44.7 %collective-permute-start.5 = (bf16[384,1024]{1,0:T(8,128)(2,1)}, bf16[384,1024]{1,0:T(8,128)(2,1)}, u32[]{:S(2)}, u32[]{:S(2)}) collective-permute-start(bf16[384,1024]{1,0:T(8,128)(2,1)} %get-tuple-element.49), channel_id=1, source_target_pairs={{8,0},{16,8},{24,16},{32,24},{40,32},{48,40},{56,48},{64,56},{72,6... | collective-permute-start | bytes 2359304 | tf_op jit(solution)/shard_map/ppermute | solution.py:453
  32.9 48.5 %all-to-all-start = ((bf16[32,48,128]{2,1,0:T(8,128)(2,1)}), bf16[32,48,128]{2,1,0:T(8,128)(2,1)}, u32[]{:S(2)}, u32[]{:S(2)}) async-start(bf16[32,48,128]{2,1,0:T(8,128)(2,1)} %get-tuple-element.47), calls=%async_computation | async-start | bytes 786432 | tf_op jit(solution)/shard_map/all_to_all | solution.py:488
  74.6 72.5 %collective-permute-start.6 = (s16[400,1024]{1,0:T(8,128)(2,1)}, s16[400,1024]{1,0:T(8,128)(2,1)}, u32[]{:S(2)}, u32[]{:S(2)}) collective-permute-start(s16[400,1024]{1,0:T(8,128)(2,1)} %get-tuple-element.65), channel_id=1, source_target_pairs={{0,8},{8,16},{16,24},{24,32},{32,40},{40,48},{48,56},{56,64},{64,7... | collective-permute-start | bytes 2457608 | tf_op jit(solution)/shard_map/ppermute | solution.py:453
  78.6 68.5 %collective-permute-start.7 = (s16[400,1024]{1,0:T(8,128)(2,1)}, s16[400,1024]{1,0:T(8,128)(2,1)}, u32[]{:S(2)}, u32[]{:S(2)}) collective-permute-start(s16[400,1024]{1,0:T(8,128)(2,1)} %get-tuple-element.66), channel_id=1, source_target_pairs={{8,0},{16,8},{24,16},{32,24},{40,32},{48,40},{56,48},{64,56},{72,6... | collective-permute-start | bytes 2457608 | tf_op jit(solution)/shard_map/ppermute | solution.py:453
  85.9 19.9 %all-to-all-start.1 = ((f32[8,40,128]{2,1,0:T(8,128)}), f32[8,40,128]{2,1,0:T(8,128)}, u32[]{:S(2)}, u32[]{:S(2)}) async-start(f32[8,40,128]{2,1,0:T(8,128)} %get-tuple-element.58), calls=%async_computation.1 | async-start | bytes 327680 | tf_op jit(solution)/shard_map/all_to_all | solution.py:496
  100.1 71.0 %collective-permute-start.10 = (s16[400,1024]{1,0:T(8,128)(2,1)}, s16[400,1024]{1,0:T(8,128)(2,1)}, u32[]{:S(2)}, u32[]{:S(2)}) collective-permute-start(s16[400,1024]{1,0:T(8,128)(2,1)} %get-tuple-element.71), channel_id=1, source_target_pairs={{0,1},{1,2},{2,3},{3,4},{4,5},{5,6},{6,7},{8,9},{9,10},{10,11},{11... | collective-permute-start | bytes 2457608 | tf_op jit(solution)/shard_map/ppermute | solution.py:453
  103.7 67.4 %collective-permute-start.11 = (s16[400,1024]{1,0:T(8,128)(2,1)}, s16[400,1024]{1,0:T(8,128)(2,1)}, u32[]{:S(2)}, u32[]{:S(2)}) collective-permute-start(s16[400,1024]{1,0:T(8,128)(2,1)} %get-tuple-element.72), channel_id=1, source_target_pairs={{1,0},{2,1},{3,2},{4,3},{5,4},{6,5},{7,6},{9,8},{10,9},{11,10},{12... | collective-permute-start | bytes 2457608 | tf_op jit(solution)/shard_map/ppermute | solution.py:453
  111.4 47.5 %all-to-all-start.2 = ((bf16[32,32,128]{2,1,0:T(8,128)(2,1)}), bf16[32,32,128]{2,1,0:T(8,128)(2,1)}, u32[]{:S(2)}, u32[]{:S(2)}) async-start(bf16[32,32,128]{2,1,0:T(8,128)(2,1)} %coarse_stage.1), calls=%async_computation.2 | async-start | bytes 524288 | tf_op jit(solution)/shard_map/all_to_all | solution.py:502
  158.9 12.2 %collective-permute-start.9 = (bf16[1024,128]{1,0:T(8,128)(2,1)}, bf16[1024,128]{1,0:T(8,128)(2,1)}, u32[]{:S(2)}, u32[]{:S(2)}) collective-permute-start(bf16[1024,128]{1,0:T(8,128)(2,1)} %bitcast.7.refs_4_.refs_7_.refs_8_), channel_id=1, source_target_pairs={{1,0},{2,1},{3,2},{4,3},{5,4},{6,5},{7,6},{9,8},{10,9},{11,10},{12... | collective-permute-start | bytes 786440 | tf_op jit(solution)/shard_map/ppermute | solution.py:453
  162.9 8.2 %collective-permute-start.8 = (bf16[1024,128]{1,0:T(8,128)(2,1)}, bf16[1024,128]{1,0:T(8,128)(2,1)}, u32[]{:S(2)}, u32[]{:S(2)}) collective-permute-start(bf16[1024,128]{1,0:T(8,128)(2,1)} %bitcast.7.refs_4_.refs_7_.refs_8_), channel_id=1, source_target_pairs={{0,1},{1,2},{2,3},{3,4},{4,5},{5,6},{6,7},{8,9},{9,10},{10,11},{11... | collective-permute-start | bytes 786440 | tf_op jit(solution)/shard_map/ppermute | solution.py:453

commit v2 on v1

v2 whole, which is shorter than its diff:
```python
import functools
import jax
import jax.numpy as jnp
from jax import lax
from jax.experimental import pallas as pl
from jax.experimental.pallas import tpu as pltpu
from jax.sharding import PartitionSpec as P

F32, BF16, I16, I32 = jnp.float32, jnp.bfloat16, jnp.int16, jnp.int32
LANES = 128
SLOT = 40
ROWS = 48
EARLY = 32
EXTRA = 16
BASE = 16
VMEM = 64 * 1024 * 1024
FREE = pl.CostEstimate(flops=0, bytes_accessed=0, transcendentals=0)
LONG = pl.CostEstimate(flops=10**12, bytes_accessed=0, transcendentals=0)


def dot(a, b, dims=((1,), (0,)), precision=None):
    return lax.dot_general(a, b, (dims, ((), ())), precision=precision, preferred_element_type=F32)


def whole(shape):
    return pl.BlockSpec(shape, lambda i: (0,) * len(shape))


def params():
    return pltpu.CompilerParams(vmem_limit_bytes=VMEM)


SIDE = pl.BlockSpec(memory_space=pltpu.SMEM)


def by_side(side, even, odd):
    pl.when(side[0] == 0)(even)
    pl.when(side[0] != 0)(odd)


def spec(shape, place):
    return pl.BlockSpec(shape, lambda i: place(i))


def lanes_between(shape, low, high):
    lane = lax.broadcasted_iota(I32, shape, len(shape) - 1)
    return (lane >= low) & (lane < high)


def one_hot_lanes(size, index_row):
    ids = lax.broadcasted_iota(I32, (size, index_row.shape[1]), 0)
    return jnp.where(ids == index_row, 1.0, 0.0)


def first_kernel(fs, side, weights, orders, basis, x, far_a, far_b, near_a, near_b):
    nc = basis.shape[0]

    def fill(face, ahead, behind):
        at = slice(face * fs, (face + 1) * fs)
        ahead[ROWS:, :] = x[face * fs : face * fs + EARLY, :]
        behind[...] = x[face * fs + EARLY : (face + 1) * fs, :]
        part = basis[:, at]
        scaled = (part.astype(F32) * weights[:, at]).astype(BF16)
        turned = dot(scaled, one_hot_lanes(fs, orders[face : face + 1, :]).astype(BF16), ((1,), (1,)))
        ahead[0:ROWS, :] = jnp.zeros((ROWS, ahead.shape[1]), BF16)
        ahead[0:nc, 0:fs] = turned.astype(BF16)
        ahead[0:nc, fs : 2 * fs] = part

    def even():
        fill(0, far_a, far_b)
        fill(1, near_a, near_b)

    def odd():
        fill(1, far_a, far_b)
        fill(0, near_a, near_b)

    by_side(side, even, odd)


def first_stage(side, x, weights, orders, basis):
    nb, m = x.shape
    fs = nb // 4
    ahead = jax.ShapeDtypeStruct((EARLY + ROWS, m), BF16)
    behind = jax.ShapeDtypeStruct((fs - EARLY, m), BF16)
    return pl.pallas_call(
        functools.partial(first_kernel, fs),
        grid=(1,),
        in_specs=[SIDE, whole(weights.shape), whole(orders.shape), whole(basis.shape), whole((2 * fs, m))],
        out_specs=[whole(ahead.shape), whole(behind.shape)] * 2,
        out_shape=[ahead, behind] * 2,
        compiler_params=params(),
        cost_estimate=FREE,
        name="first_stage",
    )(side, weights, orders, basis, x)


def cut_kernel(fs, basis, x_one, x_two, one, two):
    nc = basis.shape[0]
    for face, x, out in ((2, x_one, one), (3, x_two, two)):
        out[ROWS:, :] = x[...]

        @pl.when(pl.program_id(0) == 0)
        def _():
            out[0:ROWS, :] = jnp.zeros((ROWS, out.shape[1]), BF16)
            out[0:nc, 0:fs] = basis[:, face * fs : (face + 1) * fs]


def cut(x, basis):
    nb, m = x.shape
    fs, width = nb // 4, m // 2
    col = lambda n, k: spec((n, width), lambda i: (k, i))
    face = jax.ShapeDtypeStruct((fs + ROWS, m), BF16)
    return pl.pallas_call(
        functools.partial(cut_kernel, fs),
        grid=(2,),
        in_specs=[whole(basis.shape), col(fs, 2), col(fs, 3)],
        out_specs=[col(fs + ROWS, 0), col(fs + ROWS, 0)],
        out_shape=[face, face],
        compiler_params=params(),
        cost_estimate=FREE,
        name="cut",
    )(basis, x, x)


def on_lanes(rows, offset):
    n = rows.shape[1]
    parts = [jnp.zeros((offset, n), F32)] if offset else []
    parts += [rows, jnp.zeros((LANES - offset - SLOT, n), F32)]
    return jnp.concatenate(parts, axis=0).T.astype(BF16)


def base_kernel(fs, weights, orders, basis, x, own_out, rest, picks, w_col, basis_t):
    nc = basis.shape[0]

    @pl.when(pl.program_id(0) == 0)
    def _():
        w_col[...] = jnp.broadcast_to(weights[...], (8, 4 * fs)).T[:, 0:1]
        for face in range(4):
            picks[face] = one_hot_lanes(fs, orders[face : face + 1, :]).T.astype(BF16)
        tall = jnp.concatenate([basis[...].astype(F32), jnp.zeros((LANES - nc, 4 * fs), F32)], axis=0)
        basis_t[...] = tall.T.astype(BF16)

    own = (w_col[...] * x[...].astype(F32)).astype(BF16)
    own_out[...] = own
    rest[...] = jnp.zeros_like(rest)
    rest[0:nc, :] = dot(basis[...], own)


def base_stage(weights, orders, basis, x):
    nb, m = x.shape
    fs, width = nb // 4, m // 2
    col = lambda n: spec((n, width), lambda i: (0, i))
    return pl.pallas_call(
        functools.partial(base_kernel, fs),
        grid=(2,),
        in_specs=[whole(a.shape) for a in (weights, orders, basis)] + [col(nb)],
        out_specs=[col(nb), col(SLOT), whole((4, fs, fs)), whole((nb, 1)), whole((nb, LANES))],
        out_shape=[
            jax.ShapeDtypeStruct((nb, m), BF16),
            jax.ShapeDtypeStruct((SLOT, m), F32),
            jax.ShapeDtypeStruct((4, fs, fs), BF16),
            jax.ShapeDtypeStruct((nb, 1), F32),
            jax.ShapeDtypeStruct((nb, LANES), BF16),
        ],
        compiler_params=params(),
        cost_estimate=FREE,
        name="base_stage",
    )(weights, orders, basis, x)


def met(picks, w_col, faces):
    fs = picks.shape[1]
    each = [
        (w_col[i * fs : (i + 1) * fs, :] * dot(picks[i], face)).astype(BF16) for i, face in enumerate(faces)
    ]
    return jnp.concatenate(each, axis=0)


def far_kernel(basis, picks, w_col, rest, left, right, other_out, rest_out):
    nc, nb = basis.shape
    fs = nb // 4
    other = met(picks, w_col, (left[ROWS:, :], right[ROWS:, :]))
    other_out[...] = other
    rest_out[...] = rest[...]
    rest_out[0:nc, :] += dot(basis[:, nb // 2 :], other)


def far_stage(basis, picks, w_col, rest, left, right):
    m = rest.shape[1]
    nb = w_col.shape[0]
    fs, half, width = nb // 4, nb // 2, m // 2
    col = lambda n: spec((n, width), lambda i: (0, i))
    return pl.pallas_call(
        far_kernel,
        grid=(2,),
        in_specs=[
            whole(basis.shape),
            spec((2, fs, fs), lambda i: (1, 0, 0)),
            spec((half, 1), lambda i: (1, 0)),
            col(SLOT),
            col(left.shape[0]),
            col(right.shape[0]),
        ],
        out_specs=[col(half), col(SLOT)],
        out_shape=[jax.ShapeDtypeStruct((half, m), BF16), jax.ShapeDtypeStruct((SLOT, m), F32)],
        compiler_params=params(),
        cost_estimate=FREE,
        name="far_stage",
    )(basis, picks, w_col, rest, left, right)


def load_kernel(nc, cols, side, ids, rest, x, far, near, load, digits, shares):
    fs = x.shape[0] // 2

    @pl.when(pl.program_id(0) == 0)
    def _():
        digits[...] = jnp.zeros_like(digits)
        top = jnp.right_shift(ids[...], 4)
        digits[0:1, 0:nc] = top.astype(F32)
        digits[1:2, 0:nc] = (ids[...] - top * BASE).astype(F32)

    def share(low, high):
        shares[0:SLOT, :] = dot(low[0:ROWS, 0:fs], x[0:fs])[0:SLOT]
        shares[SLOT:, :] = dot(high[0:ROWS, 0:fs], x[fs:])[0:SLOT]

    by_side(side, lambda: share(far, near), lambda: share(near, far))
    none = jnp.zeros((LANES - 3 * SLOT, rest.shape[1]), F32)
    turned = jnp.concatenate([rest[...], shares[...], none], axis=0).T.astype(BF16)
    for block in range(load.shape[0]):
        load[block, 0:cols, :] = turned[block * cols : (block + 1) * cols]
        load[block, cols:, :] = digits[...].astype(BF16)


def load_stage(nc, side, ids, rest, x, far, near, subs):
    nb, m = x.shape
    half, width = nb // 2, m // 2
    cols = m // subs
    col = lambda n: spec((n, width), lambda i: (0, i))
    return pl.pallas_call(
        functools.partial(load_kernel, nc, cols),
        grid=(2,),
        in_specs=[SIDE, whole(ids.shape), col(SLOT), col(half), whole((ROWS, m)), whole((ROWS, m))],
        out_specs=spec((width // cols, cols + 16, LANES), lambda i: (i, 0, 0)),
        out_shape=jax.ShapeDtypeStruct((subs, cols + 16, LANES), BF16),
        scratch_shapes=[pltpu.VMEM((16, LANES), F32), pltpu.VMEM((2 * SLOT, width), F32)],
        compiler_params=params(),
        cost_estimate=FREE,
        name="load_stage",
    )(side, ids, rest, x, far, near)


def acc_kernel(half, inverse, own, other, acc):
    acc[...] = dot(inverse[...], own[...]) + dot(inverse[:, half:], other[...])


def acc_stage(place, inverse, own, other, cost):
    nb, m = own.shape
    tall = nb // 4
    return pl.pallas_call(
        functools.partial(acc_kernel, nb // 2),
        grid=(2,),
        in_specs=[spec((tall, nb), lambda i: (2 * place + i, 0)), whole(own.shape), whole(other.shape)],
        out_specs=spec((tall, m), lambda i: (i, 0)),
        out_shape=jax.ShapeDtypeStruct((nb // 2, m), F32),
        compiler_params=params(),
        cost_estimate=cost,
        name="acc_stage",
    )(inverse, own, other)


def coded(values, q_ref):
    fs = values.shape[0]
    top = jnp.max(jnp.abs(values), axis=0, keepdims=True)
    power = jnp.floor(jnp.log2(jnp.maximum(top, 1e-30))) - 13.0
    q_ref[0:fs, :] = jnp.round(values * jnp.exp2(-power)).astype(I32).astype(I16)
    q_ref[fs:, :] = jnp.broadcast_to(power.astype(I32), (EXTRA, values.shape[1])).astype(I16)


def part_kernel(side, picks, w_col, inverse, far_a, far_b, near_a, near_b, acc, part, q_far, q_near, other_out, other):
    @pl.when(pl.program_id(0) == 0)
    def _():
        far = jnp.concatenate([far_a[ROWS:, :], far_b[...]], axis=0)
        near = jnp.concatenate([near_a[ROWS:, :], near_b[...]], axis=0)

        def arrived(faces):
            other[...] = met(picks, w_col, faces)

        by_side(side, lambda: arrived((far, near)), lambda: arrived((near, far)))
        other_out[...] = other[...]

    total = acc[...] + dot(inverse[...], other[...])
    part[...] = total
    is_far = pl.program_id(0) == side[0]
    pl.when(is_far)(lambda: coded(total, q_far))
    pl.when(jnp.logical_not(is_far))(lambda: coded(total, q_near))


def part_stage(side, picks, w_col, inverse, far, near, acc):
    half, m = acc.shape
    fs = half // 2
    row = lambda n: spec((fs, n), lambda i: (i, 0))
    code = jax.ShapeDtypeStruct((fs + EXTRA, m), I16)
    return pl.pallas_call(
        part_kernel,
        grid=(2,),
        in_specs=[
            SIDE,
            spec((2, fs, fs), lambda i: (0, 0, 0)),
            spec((half, 1), lambda i: (0, 0)),
            row(half),
            whole(far[0].shape),
            whole(far[1].shape),
            whole(near[0].shape),
            whole(near[1].shape),
            row(m),
        ],
        out_specs=[row(m), whole(code.shape), whole(code.shape), whole((half, m))],
        out_shape=[jax.ShapeDtypeStruct((half, m), F32), code, code, jax.ShapeDtypeStruct((half, m), BF16)],
        scratch_shapes=[pltpu.VMEM((half, m), BF16)],
        compiler_params=params(),
        cost_estimate=FREE,
        name="part_stage",
    )(side, picks, w_col, inverse, *far, *near, acc)


def part_grp_kernel(inverse, other, acc, part, q_one, q_two):
    total = acc[...] + dot(inverse[...], other[...])
    part[...] = total
    for face, q in enumerate((q_one, q_two)):
        pl.when(pl.program_id(0) == face)(functools.partial(coded, total, q))


def part_grp_stage(inverse, other, acc):
    half, m = acc.shape
    fs = half // 2
    code = jax.ShapeDtypeStruct((fs + EXTRA, m), I16)
    return pl.pallas_call(
        part_grp_kernel,
        grid=(2,),
        in_specs=[
            spec((fs, half), lambda i: (2 + i, 0)),
            whole(other.shape),
            spec((fs, m), lambda i: (i, 0)),
        ],
        out_specs=[spec((fs, m), lambda i: (i, 0)), whole(code.shape), whole(code.shape)],
        out_shape=[jax.ShapeDtypeStruct((half, m), F32), code, code],
        compiler_params=params(),
        cost_estimate=FREE,
        name="part_grp_stage",
    )(inverse, other, acc)


def static_kernel(basis_in, slots_in, coarse_in, basis, slots, up, coarse):
    exact = lax.Precision.HIGHEST
    nc2, n3 = basis_in.shape[0], coarse_in.shape[0]
    basis[...] = jnp.zeros_like(basis)
    basis[0:nc2, :] = basis_in[...]
    slots[...] = jnp.full_like(slots, -1.0)
    slots[0:1, 0:nc2] = slots_in[...].astype(F32)
    coarse[...] = jnp.zeros_like(coarse)
    coarse[0:n3, 0:n3] = coarse_in[...]
    chosen = dot(one_hot_lanes(coarse.shape[0], slots[...].astype(I32)), coarse[...], ((0,), (0,)), exact)
    up[...] = dot(chosen, basis[...], ((0,), (0,)), exact)


def static_stage(basis, slots, coarse_inverse):
    nc2, size = basis.shape
    wide = -(-coarse_inverse.shape[0] // LANES) * LANES
    return pl.pallas_call(
        static_kernel,
        out_shape=[
            jax.ShapeDtypeStruct((LANES, size), F32),
            jax.ShapeDtypeStruct((1, LANES), F32),
            jax.ShapeDtypeStruct((wide, size), F32),
        ],
        scratch_shapes=[pltpu.VMEM((wide, wide), F32)],
        compiler_params=params(),
        cost_estimate=FREE,
        name="static_stage",
    )(basis, slots, coarse_inverse)


def group_kernel(nc, loads, inverse, basis, slots, local_out, send, index_out):
    subs, rows, _ = loads.shape
    cols = rows - 16
    size = inverse.shape[0]
    digits = jnp.stack([loads[s, cols : cols + 8, :].astype(F32) for s in range(subs)])
    own = (digits[:, 0, :] * BASE + digits[:, 1, :]).astype(I32)
    before = pltpu.roll(jnp.concatenate([own[0:1], own[: subs - 1]], axis=0), SLOT, 1)
    after = pltpu.roll(jnp.concatenate([own[1:], own[subs - 1 :]], axis=0), 2 * SLOT, 1)
    in_zero = lanes_between(own.shape, 0, nc)
    in_one = lanes_between(own.shape, SLOT, SLOT + nc)
    in_two = lanes_between(own.shape, 2 * SLOT, 2 * SLOT + nc)
    index = jnp.where(in_zero, own, jnp.where(in_one, before, jnp.where(in_two, after, -1)))
    index_out[...] = index
    total = jnp.zeros((cols, size), F32)
    for s in range(0, subs, 2):
        pair = jnp.concatenate([loads[s, 0:cols, :], loads[s + 1, 0:cols, :]], axis=1)
        row = jnp.concatenate([index[s : s + 1], index[s + 1 : s + 2]], axis=1)
        total = total + dot(pair, one_hot_lanes(size, row).astype(BF16), ((1,), (1,)))
    exact = lax.Precision.HIGHEST
    local_out[...] = dot(total, inverse[...], ((1,), (1,)), exact)
    coarse = dot(total, basis[...], ((1,), (1,)), exact)
    for g in range(send.shape[0]):
        send[g, 0:cols, :] = coarse
        send[g, cols:, :] = jnp.broadcast_to(slots[...], (8, LANES))


def group_stage(loads, inverse, basis, slots, nc, groups):
    subs, rows, _ = loads.shape
    cols = rows - 16
    size = inverse.shape[0]
    return pl.pallas_call(
        functools.partial(group_kernel, nc),
        out_shape=[
            jax.ShapeDtypeStruct((cols, size), F32),
            jax.ShapeDtypeStruct((groups, cols + 8, LANES), F32),
            jax.ShapeDtypeStruct((subs, LANES), I32),
        ],
        compiler_params=params(),
        cost_estimate=FREE,
        name="group_stage",
    )(loads, inverse, basis, slots)


def coarse_kernel(received, local_in, up, index, send):
    cols, size = local_in.shape
    wide = up.shape[0]
    spread = jnp.zeros((3 * cols, wide), F32)
    for g in range(received.shape[0]):
        whole_part = received[g, 0:cols, :]
        top = whole_part.astype(BF16).astype(F32)
        middle = (whole_part - top).astype(BF16).astype(F32)
        terms = jnp.concatenate([top, middle, whole_part - top - middle], axis=0).astype(BF16)
        slots = received[g, cols : cols + 1, :].astype(I32)
        spread = spread + dot(terms, one_hot_lanes(wide, slots).astype(BF16), ((1,), (1,)))
    rhs = spread[0:cols] + spread[cols : 2 * cols] + spread[2 * cols :]
    group_sol = local_in[...] + dot(rhs, up[...], precision=lax.Precision.HIGHEST)
    rounded = group_sol.astype(BF16)
    for s in range(0, send.shape[0], 2):
        row = jnp.concatenate([index[s : s + 1, :], index[s + 1 : s + 2, :]], axis=1)
        both = dot(rounded, one_hot_lanes(size, row).astype(BF16)).astype(BF16)
        send[s] = both[:, 0:LANES]
        send[s + 1] = both[:, LANES:]


def coarse_stage(received, local_in, up, index):
    subs = index.shape[0]
    cols = local_in.shape[0]
    return pl.pallas_call(
        coarse_kernel,
        out_shape=jax.ShapeDtypeStruct((subs, cols, LANES), BF16),
        compiler_params=params(),
        cost_estimate=FREE,
        name="coarse_stage",
    )(received, local_in, up, index)


def into(kernel, target, args, in_specs):
    if target is None:
        return kernel, args, in_specs
    return (lambda _, *refs: kernel(*refs)), [target] + args, [pl.BlockSpec(memory_space=pl.ANY)] + in_specs


def last_kernel(fs, offsets, lane, side, picks, w_col, basis_t, part, primal, far, near, far_p, near_p, far_q, near_q, out, lifts):
    nt = ((1,), (1,))

    def finish(faces):
        @pl.when(pl.program_id(0) == 0)
        def _():
            for face, (rows, _, _) in enumerate(faces):
                lifts[face] = on_lanes(rows[0:SLOT, lane : lane + fs].astype(F32), offsets[face])

        for face, (_, primal_n, q) in enumerate(faces):
            at = slice(face * fs, (face + 1) * fs)
            mine = (part[at] + dot(basis_t[at], primal[...], nt)).astype(BF16)
            scale = jnp.exp2(q[fs:, :].astype(I32).astype(F32)[0:1])
            theirs = q[0:fs, :].astype(I32).astype(F32) * scale
            theirs = (theirs + dot(lifts[face], primal_n[...], nt)).astype(BF16)
            arrived = dot(picks[face], theirs)
            out[at] = (w_col[at] * (mine.astype(F32) + arrived)).astype(BF16)

    one, two = (far, far_p, far_q), (near, near_p, near_q)
    if side is None:
        finish((one, two))
    else:
        by_side(side, lambda: finish((one, two)), lambda: finish((two, one)))


def last_stage(place, offsets, lane, side, picks, w_col, basis_t, part, primal, far, near, far_p, near_p, codes, target=None):
    half, m = part.shape
    fs = half // 2
    width = m // 2
    mine = lambda k: spec((half, k), lambda i: (place, 0))
    primal_spec = spec((width, LANES), lambda i: (i, 0))
    basis_spec = whole((ROWS, far.shape[1]))
    in_specs = [spec((2, fs, fs), lambda i: (place, 0, 0)), mine(1), mine(LANES), spec((half, width), lambda i: (0, i))]
    in_specs += [primal_spec, basis_spec, basis_spec, primal_spec, primal_spec]
    in_specs += [spec((fs + EXTRA, width), lambda i: (0, i))] * 2
    args = [picks, w_col, basis_t, part, primal, far, near, far_p, near_p, *codes]
    kernel = functools.partial(last_kernel, fs, offsets, lane)
    if side is None:
        kernel = functools.partial(kernel, None)
    else:
        args, in_specs = [side] + args, [SIDE] + in_specs
    kernel, args, in_specs = into(kernel, target, args, in_specs)
    return pl.pallas_call(
        kernel,
        grid=(2,),
        in_specs=in_specs,
        out_specs=spec((half, width), lambda i: (place, i)),
        out_shape=jax.ShapeDtypeStruct((2 * half, m), BF16),
        scratch_shapes=[pltpu.VMEM((2, fs, LANES), BF16)],
        input_output_aliases={} if target is None else {0: 0},
        compiler_params=params(),
        cost_estimate=FREE,
        name="last_stage",
    )(*args)


def exchange(faces, axis):
    size = lax.axis_size(axis)
    up = [(i, i + 1) for i in range(size - 1)]
    down = [(j, i) for i, j in up]
    return lax.ppermute(faces[1], axis, up), lax.ppermute(faces[0], axis, down)


def swap(far_out, near_out):
    size = lax.axis_size("sub")
    near = [(i, i ^ 1) for i in range(size)]
    far = [(i, i + 1) for i in range(1, size - 1, 2)]
    far += [(j, i) for i, j in far]
    return lax.ppermute(far_out, "sub", far), lax.ppermute(near_out, "sub", near)


def together(*values):
    return lax.optimization_barrier(values)


def local(
    residual,
    weights,
    face_map,
    local_inverse,
    basis,
    primal_index,
    group_inverse,
    group_basis,
    group_index,
    coarse_inverse,
):
    x = residual[0, 0]
    nb, m = x.shape
    nc = basis.shape[2]
    subs, groups = lax.axis_size("sub"), lax.axis_size("grp")
    inverse = local_inverse[0, 0]
    w_row = weights[0]
    orders = face_map[0, 0]
    coarse_rows = basis[0, 0]

    side = lax.rem(lax.axis_index("sub"), 2).astype(I32).reshape(1)
    fs = nb // 4
    far_a, far_b, near_a, near_b = first_stage(side, x, w_row, orders, coarse_rows)
    far_a, near_a = swap(far_a, near_a)
    far_b, near_b = swap(far_b, near_b)
    left, right = exchange(cut(x, coarse_rows), "grp")

    w_row, left = together(w_row, left)
    own, rest, picks, w_col, basis_t = base_stage(w_row, orders, coarse_rows, x)
    other_grp, rest = far_stage(coarse_rows, picks, w_col, rest, left, right)
    g_basis, slots, up = static_stage(group_basis[0], group_index, coarse_inverse)
    rest, g_basis, slots, up = together(rest, g_basis, slots, up)
    load = load_stage(nc, side, primal_index[0], rest, x, far_a, near_a, subs)
    loads = lax.all_to_all(load, "sub", 0, 0, tiled=True)
    other_grp, load = together(other_grp, load)
    acc_sub = acc_stage(0, inverse, own, other_grp, LONG)
    far_b, near_b, acc_sub = together(far_b, near_b, acc_sub)
    part_sub, q_far, q_near, other_sub = part_stage(side, picks, w_col, inverse, (far_a, far_b), (near_a, near_b), acc_sub)
    q_far, q_near = swap(q_far, q_near)

    loads, part_sub = together(loads, part_sub)
    group_local, send, index = group_stage(loads, group_inverse[0], g_basis, slots, nc, groups)
    received = lax.all_to_all(send, "grp", 0, 0, tiled=True)
    other_sub, other_grp, send = together(other_sub, other_grp, send)
    acc_grp = acc_stage(1, inverse, own, other_grp, FREE)
    part_grp, q_three, q_four = part_grp_stage(inverse, other_sub, acc_grp)
    q_left, q_right = exchange((q_three, q_four), "grp")
    received, part_grp = together(received, part_grp)
    picked = coarse_stage(received, group_local, up, index)
    primal = lax.all_to_all(picked, "sub", 0, 0, tiled=True).reshape(m, LANES)
    primal, q_far, q_near = together(primal, q_far, q_near)
    primal_left, primal_right = exchange((primal, primal), "grp")

    mine = (picks, w_col, basis_t)
    out = last_stage(
        0, (SLOT, 2 * SLOT), fs, side, *mine, part_sub, primal, far_a, near_a, primal, primal, (q_far, q_near)
    )
    out = last_stage(
        1, (0, 0), 0, None, *mine, part_grp, primal, left, right, primal_left, primal_right, (q_left, q_right), out
    )
    return out[None, None]


def solution(mesh):
    placed = (
        P("sub", "grp", None, None),
        P("sub", "grp", None),
        P("sub", "grp", None, None),
        P("sub", "grp", None, None),
        P("sub", "grp", None, None),
        P("sub", "grp", None),
        P("grp", None, None),
        P("grp", None, None),
        P("grp", None),
        P(),
    )
    return jax.shard_map(
        local, mesh=mesh, in_specs=placed, out_specs=P("sub", "grp", None, None), check_vma=False
    )
```

time: 178 us -> 167 us (0.938)
  starting transfers between devices: 101 us -> 83.3 us
  Pallas kernels: 62.1 us -> 69.7 us
    ppermute x0 -> x6, starting transfers between devices: none -> 17.1 us  [the longest x3 12.5 us: swap(): lax.ppermute(near_out, 'sub', near)]
    all_to_all x1, starting transfers between devices: 35.7 us -> 21.4 us  [local(): primal = lax.all_to_all(picked, 'sub', 0, 0, tiled=True).reshape(m, LANES)]
    pallas_call x5 -> x8, Pallas kernels: 32.1 us -> 41.5 us  [the longest x2 15.8 us: acc_stage(): pl.pallas_call(functools.partial(acc_kernel, nb // 2), grid=(2,), in_spec...]
    ppermute x6 -> x3, starting transfers between devices: 23 us -> 14.2 us  [exchange(): lax.ppermute(faces[1], axis, up)]
    all_to_all x1, starting transfers between devices: 21.9 us -> 16.3 us  [local(): loads = lax.all_to_all(load, 'sub', 0, 0, tiled=True)]
    ppermute x6 -> x3, starting transfers between devices: 12.4 us -> 8.43 us  [exchange(): lax.ppermute(faces[0], axis, down)]
    all_to_all x1, starting transfers between devices: 8.22 us -> 5.88 us  [local(): received = lax.all_to_all(send, 'grp', 0, 0, tiled=True)]
    pallas_call x1, Pallas kernels: 5.58 us -> 3.6 us  [coarse_stage(): pl.pallas_call(coarse_kernel, out_shape=jax.ShapeDtypeStruct((subs, cols,...]
  transfers between devices with their start and end apart: 15 -> 15, of which waited for: 1 -> 1; matrix products, arithmetic and copies ran while one was open for 1% -> 1% of each run, Pallas kernels for 30% -> 37%
where the time goes in v2:
time: 167 us
  starting transfers between devices  83.3 us (50%)
  Pallas kernels  69.7 us (42%)
  waiting for transfers between devices  11.9 us (7%)
    all_to_all x1, starting transfers between devices, local(): primal = lax.all_to_all(picked, 'sub', 0, 0, tiled=True).reshape(m, LANES)  21.4 us
    all_to_all x1, starting transfers between devices, local(): loads = lax.all_to_all(load, 'sub', 0, 0, tiled=True)  16.3 us
    pallas_call x2, Pallas kernels, acc_stage(): pl.pallas_call(functools.partial(acc_kernel, nb // 2), grid=(2,), in_spec...  15.8 us
    ppermute x3, starting transfers between devices, exchange(): lax.ppermute(faces[1], axis, up)  14.2 us
    ppermute x3, starting transfers between devices, swap(): lax.ppermute(near_out, 'sub', near)  12.5 us
    all_to_all x1, waiting for transfers between devices, local(): primal = lax.all_to_all(picked, 'sub', 0, 0, tiled=True).reshape(m, LANES)  11.9 us
    pallas_call x2, Pallas kernels, last_stage(): pl.pallas_call(kernel, grid=(2,), in_specs=in_specs, out_specs=spec((half...  11.6 us
    ppermute x3, starting transfers between devices, exchange(): lax.ppermute(faces[0], axis, down)  8.43 us
  transfers between devices with their start and end apart: 15, of which 1 were waited for; matrix products, arithmetic and copies ran while one was open for 1% of the time, Pallas kernels for 37%

profile of v2, /device:TPU:1, one launch (start us, length us, event | category | flops | bytes accessed | tf_op | source)
XLA Modules:
  0.0 166.5 jit_solution(16812070959435638947)
XLA Ops:
  0.0 2.4 %cut.1 = (bf16[432,1024]{1,0:T(8,128)(2,1)}, bf16[432,1024]{1,0:T(8,128)(2,1)}) custom-call(bf16[37,1536]{1,0:T(8,128)(2,1)} %bitcast.22, bf16[1536,1024]{1,0:T(8,128)(2,1)} %bitcast.13, bf16[1536,1024]{1,0:T(8,128)(2,1)} %bitcast.14), custom_call_target="tpu_custom_call" | custom-call | tf_op jit(solution)/shard_map/cut/pallas_call | solution.py:113
  2.4 4.9 %collective-permute-start = (bf16[432,1024]{1,0:T(8,128)(2,1)}, bf16[432,1024]{1,0:T(8,128)(2,1)}, u32[]{:S(2)}, u32[]{:S(2)}) collective-permute-start(bf16[432,1024]{1,0:T(8,128)(2,1)} %get-tuple-element.50), channel_id=1, source_target_pairs={{0,1},{1,2},{2,3},{3,4},{4,5},{5,6},{6,7},{8,9},{9,10},{10,11},{11... | collective-permute-start | bytes 2654216 | tf_op jit(solution)/shard_map/ppermute | solution.py:525
  7.4 2.4 %collective-permute-start.1 = (bf16[432,1024]{1,0:T(8,128)(2,1)}, bf16[432,1024]{1,0:T(8,128)(2,1)}, u32[]{:S(2)}, u32[]{:S(2)}) collective-permute-start(bf16[432,1024]{1,0:T(8,128)(2,1)} %get-tuple-element.57), channel_id=1, source_target_pairs={{1,0},{2,1},{3,2},{4,3},{5,4},{6,5},{7,6},{9,8},{10,9},{11,10},{12... | collective-permute-start | bytes 2654216 | tf_op jit(solution)/shard_map/ppermute | solution.py:525
  9.8 3.2 %first_stage.1 = (bf16[80,1024]{1,0:T(8,128)(2,1)}, bf16[352,1024]{1,0:T(8,128)(2,1)}, bf16[80,1024]{1,0:T(8,128)(2,1)}, bf16[352,1024]{1,0:T(8,128)(2,1)}) custom-call(s32[1]{0:T(128)} %bitcast.side, f32[1,1536]{1,0:T(1,128)} %bitcast.28, s32[4,384]{1,0:T(4,128)} %bitcast.30, bf16[37,1536]{1,0:T(8,128)(2,1)} %bitcast.23, bf16[1536,1024]{1,0:T(8,128)(2,1)} %bitcast.15), custom_call_target="tpu_custom_call" | custom-call | tf_op jit(solution)/shard_map/first_stage/pallas_call | solution.py:85
  13.0 1.3 collective-permute-start.2
  14.3 2.6 %collective-permute-start.3 = (bf16[80,1024]{1,0:T(8,128)(2,1)}, bf16[80,1024]{1,0:T(8,128)(2,1)}, u32[]{:S(2)}, u32[]{:S(2)}) collective-permute-start(bf16[80,1024]{1,0:T(8,128)(2,1)} %get-tuple-element.64), channel_id=1, source_target_pairs={{0,8},{8,0},{16,24},{24,16},{32,40},{40,32},{48,56},{56,48},{64,72... | collective-permute-start | bytes 491528 | tf_op jit(solution)/shard_map/ppermute | solution.py:533
  16.9 1.6 collective-permute-start.4
  18.5 1.5 copy.14
  20.0 2.9 %static_stage.1 = (f32[128,512]{1,0:T(8,128)}, f32[1,128]{1,0:T(1,128)}, f32[256,512]{1,0:T(8,128)}) custom-call(f32[37,512]{1,0:T(8,128)} %bitcast.27, s32[1,37]{1,0:T(1,128)} %slots_in.1, f32[148,148]{1,0:T(8,128)} %coarse_in.1), custom_call_target="tpu_custom_call" | custom-call | tf_op jit(solution)/shard_map/static_stage/pallas_call | solution.py:369
  22.9 0.0 collective-permute-done.left.refs_5_
  22.9 7.3 %collective-permute-start.5 = (bf16[352,1024]{1,0:T(8,128)(2,1)}, bf16[352,1024]{1,0:T(8,128)(2,1)}, u32[]{:S(2)}, u32[]{:S(2)}) collective-permute-start(bf16[352,1024]{1,0:T(8,128)(2,1)} %get-tuple-element.66), channel_id=1, source_target_pairs={{0,8},{8,0},{16,24},{24,16},{32,40},{40,32},{48,56},{56,48},{64,72... | collective-permute-start | bytes 2162696 | tf_op jit(solution)/shard_map/ppermute | solution.py:533
  30.1 5.1 %base_stage.1 = (bf16[1536,1024]{1,0:T(8,128)(2,1)}, f32[40,1024]{1,0:T(8,128)}, bf16[4,384,384]{2,1,0:T(8,128)(2,1)}, f32[1536,1]{1,0:T(8,128)}, bf16[1536,128]{1,0:T(8,128)(2,1)}) custom-call(f32[1,1536]{1,0:T(1,128)} %bitcast.29, s32[4,384]{1,0:T(4,128)} %bitcast.31, bf16[37,1536]{1,0:T(8,128)(2,1)} %bitcast.24, bf16[1536,1024]{1,0:T(8,128)(2,1)} %bitcast.16), custom_call_target="tpu_custom_call" | custom-call | tf_op jit(solution)/shard_map/base_stage/pallas_call | solution.py:153
  35.2 0.0 collective-permute-done.1.right.refs_6_
  35.2 4.0 %far_stage.1 = (bf16[768,1024]{1,0:T(8,128)(2,1)}, f32[40,1024]{1,0:T(8,128)}) custom-call(bf16[37,1536]{1,0:T(8,128)(2,1)} %bitcast.25, bf16[4,384,384]{2,1,0:T(8,128)(2,1)} %get-tuple-element.52.picks.refs_0_, f32[1536,1]{1,0:T(8,128)} %get-tuple-element.53.w_col.refs_1_, f32[40,1024]{1,0:T(8,128)} %get-tuple-element.55.rest, ...), custom_call_target="tpu_custom_call" | custom-call | tf_op jit(solution)/shard_map/far_stage/pallas_call | solution.py:193
  39.2 0.0 collective-permute-done.2.far.far_a
  39.2 0.0 collective-permute-done.3.near.near_a
  39.2 2.7 %load_stage.1 = bf16[32,48,128]{2,1,0:T(8,128)(2,1)} custom-call(s32[1]{0:T(128)} %bitcast.side, s32[1,37]{1,0:T(1,128)} %bitcast.32, f32[40,1024]{1,0:T(8,128)} %get-tuple-element.62.rest, bf16[1536,1024]{1,0:T(8,128)(2,1)} %bitcast.17, bf16[80,1024]{1,0:T(8,128)(2,1)} %collective-permute-done.2.far.far_a, bf16[80,1024]{1,0:T(8,128)(2,1)} %collective-permute-done.3.near.near_a), custom_call_target="tpu_custom_call" | custom-call | tf_op jit(solution)/shard_map/load_stage/pallas_call | solution.py:239
  41.9 16.3 %all-to-all-start = ((bf16[32,48,128]{2,1,0:T(8,128)(2,1)}), bf16[32,48,128]{2,1,0:T(8,128)(2,1)}, u32[]{:S(2)}, u32[]{:S(2)}) async-start(bf16[32,48,128]{2,1,0:T(8,128)(2,1)} %load_stage.1), calls=%async_computation | async-start | bytes 786432 | tf_op jit(solution)/shard_map/all_to_all | solution.py:574
  58.2 7.9 %acc_stage.2.acc = f32[768,1024]{1,0:T(8,128)} custom-call(bf16[1536,1536]{1,0:T(8,128)(2,1)} %bitcast.18, bf16[1536,1024]{1,0:T(8,128)(2,1)} %get-tuple-element.67.own, bf16[768,1024]{1,0:T(8,128)(2,1)} %get-tuple-element.81.other), custom_call_target="tpu_custom_call" | custom-call | flops 999999995904 | tf_op jit(solution)/shard_map/acc_stage/pallas_call | solution.py:259
  66.1 0.0 collective-permute-done.4.far_b
  66.1 0.0 collective-permute-done.5.near_b
  66.1 7.9 %part_stage.1 = (f32[768,1024]{1,0:T(8,128)}, s16[400,1024]{1,0:T(8,128)(2,1)}, s16[400,1024]{1,0:T(8,128)(2,1)}, bf16[768,1024]{1,0:T(8,128)(2,1)}) custom-call(s32[1]{0:T(128)} %bitcast.side, bf16[4,384,384]{2,1,0:T(8,128)(2,1)} %get-tuple-element.52.picks.refs_0_, f32[1536,1]{1,0:T(8,128)} %get-tuple-element.53.w_col.refs_1_, ...), custom_call_target="tpu_custom_call" | custom-call | tf_op jit(solution)/shard_map/part_stage/pallas_call | solution.py:303
  74.0 1.7 collective-permute-start.6
  75.7 2.7 %collective-permute-start.7 = (s16[400,1024]{1,0:T(8,128)(2,1)}, s16[400,1024]{1,0:T(8,128)(2,1)}, u32[]{:S(2)}, u32[]{:S(2)}) collective-permute-start(s16[400,1024]{1,0:T(8,128)(2,1)} %get-tuple-element.88), channel_id=1, source_target_pairs={{0,8},{8,0},{16,24},{24,16},{32,40},{40,32},{48,56},{56,48},{64,72... | collective-permute-start | bytes 2457608 | tf_op jit(solution)/shard_map/ppermute | solution.py:533
  78.4 0.0 all-to-all-done.loads
  78.4 4.5 %group_stage.1 = (f32[32,512]{1,0:T(8,128)}, f32[8,40,128]{2,1,0:T(8,128)}, s32[32,128]{1,0:T(8,128)}) custom-call(bf16[32,48,128]{2,1,0:T(8,128)(2,1)} %all-to-all-done.loads, f32[512,512]{1,0:T(8,128)} %bitcast.26, f32[128,512]{1,0:T(8,128)} %get-tuple-element.76.basis, f32[1,128]{1,0:T(1,128)} %get-tuple-element.77.slots), custom_call_target="tpu_custom_call" | custom-call | tf_op jit(solution)/shard_map/group_stage/pallas_call | solution.py:413
  82.9 5.9 %all-to-all-start.1 = ((f32[8,40,128]{2,1,0:T(8,128)}), f32[8,40,128]{2,1,0:T(8,128)}, u32[]{:S(2)}, u32[]{:S(2)}) async-start(f32[8,40,128]{2,1,0:T(8,128)} %get-tuple-element.78), calls=%async_computation.1 | async-start | bytes 327680 | tf_op jit(solution)/shard_map/all_to_all | solution.py:583
  88.8 7.9 %acc_stage.3.acc = f32[768,1024]{1,0:T(8,128)} custom-call(bf16[1536,1536]{1,0:T(8,128)(2,1)} %bitcast.20, bf16[1536,1024]{1,0:T(8,128)(2,1)} %get-tuple-element.67.own, bf16[768,1024]{1,0:T(8,128)(2,1)} %get-tuple-element.81.other), custom_call_target="tpu_custom_call" | custom-call | tf_op jit(solution)/shard_map/acc_stage/pallas_call | solution.py:259
  96.7 6.0 %part_grp_stage.1 = (f32[768,1024]{1,0:T(8,128)}, s16[400,1024]{1,0:T(8,128)(2,1)}, s16[400,1024]{1,0:T(8,128)(2,1)}) custom-call(bf16[1536,1536]{1,0:T(8,128)(2,1)} %bitcast.21, bf16[768,1024]{1,0:T(8,128)(2,1)} %get-tuple-element.80.other, f32[768,1024]{1,0:T(8,128)} %acc_stage.3.acc), custom_call_target="tpu_custom_call" | custom-call | tf_op jit(solution)/shard_map/part_grp_stage/pallas_call | solution.py:337
  102.7 3.8 %collective-permute-start.10 = (s16[400,1024]{1,0:T(8,128)(2,1)}, s16[400,1024]{1,0:T(8,128)(2,1)}, u32[]{:S(2)}, u32[]{:S(2)}) collective-permute-start(s16[400,1024]{1,0:T(8,128)(2,1)} %get-tuple-element.93), channel_id=1, source_target_pairs={{0,1},{1,2},{2,3},{3,4},{4,5},{5,6},{6,7},{8,9},{9,10},{10,11},{11... | collective-permute-start | bytes 2457608 | tf_op jit(solution)/shard_map/ppermute | solution.py:525
  106.5 1.9 %collective-permute-start.11 = (s16[400,1024]{1,0:T(8,128)(2,1)}, s16[400,1024]{1,0:T(8,128)(2,1)}, u32[]{:S(2)}, u32[]{:S(2)}) collective-permute-start(s16[400,1024]{1,0:T(8,128)(2,1)} %get-tuple-element.94), channel_id=1, source_target_pairs={{1,0},{2,1},{3,2},{4,3},{5,4},{6,5},{7,6},{9,8},{10,9},{11,10},{12... | collective-permute-start | bytes 2457608 | tf_op jit(solution)/shard_map/ppermute | solution.py:525
  108.4 0.0 all-to-all-done.1.received
  108.4 3.6 %coarse_stage.1 = bf16[32,32,128]{2,1,0:T(8,128)(2,1)} custom-call(f32[8,40,128]{2,1,0:T(8,128)} %all-to-all-done.1.received, f32[32,512]{1,0:T(8,128)} %get-tuple-element.84.local_in, f32[256,512]{1,0:T(8,128)} %get-tuple-element.85.up, s32[32,128]{1,0:T(8,128)} %get-tuple-element.86.index), custom_call_target="tpu_custom_call" | custom-call | tf_op jit(solution)/shard_map/coarse_stage/pallas_call | solution.py:450
  112.0 21.4 %all-to-all-start.2 = ((bf16[32,32,128]{2,1,0:T(8,128)(2,1)}), bf16[32,32,128]{2,1,0:T(8,128)(2,1)}, u32[]{:S(2)}, u32[]{:S(2)}) async-start(bf16[32,32,128]{2,1,0:T(8,128)(2,1)} %coarse_stage.1), calls=%async_computation.2 | async-start | bytes 524288 | tf_op jit(solution)/shard_map/all_to_all | solution.py:590
  133.4 0.0 collective-permute-done.6.far_q
  133.5 0.0 collective-permute-done.7.near_q
  133.5 11.9 %all-to-all-done.2 = bf16[32,32,128]{2,1,0:T(8,128)(2,1)} async-done(((bf16[32,32,128]{2,1,0:T(8,128)(2,1)}), bf16[32,32,128]{2,1,0:T(8,128)(2,1)}, u32[]{:S(2)}, u32[]{:S(2)}) %all-to-all-start.2) | async-done | bytes 262176 | tf_op jit(solution)/shard_map/all_to_all | solution.py:590
  145.3 4.1 %collective-permute-start.9 = (bf16[1024,128]{1,0:T(8,128)(2,1)}, bf16[1024,128]{1,0:T(8,128)(2,1)}, u32[]{:S(2)}, u32[]{:S(2)}) collective-permute-start(bf16[1024,128]{1,0:T(8,128)(2,1)} %bitcast.8.primal.far_p.near_p.refs_4_), channel_id=1, source_target_pairs={{1,0},{2,1},{3,2},{4,3},{5,4},{6,5},{7,6},{9,8},{10,9},{11,10},{12... | collective-permute-start | bytes 786440 | tf_op jit(solution)/shard_map/ppermute | solution.py:525
  149.4 5.4 %collective-permute-start.8 = (bf16[1024,128]{1,0:T(8,128)(2,1)}, bf16[1024,128]{1,0:T(8,128)(2,1)}, u32[]{:S(2)}, u32[]{:S(2)}) collective-permute-start(bf16[1024,128]{1,0:T(8,128)(2,1)} %bitcast.8.primal.far_p.near_p.refs_4_), channel_id=1, source_target_pairs={{0,1},{1,2},{2,3},{3,4},{4,5},{5,6},{6,7},{8,9},{9,10},{10,11},{11... | collective-permute-start | bytes 786440 | tf_op jit(solution)/shard_map/ppermute | solution.py:525
  154.9 5.8 %last_stage.2._ = bf16[1536,1024]{1,0:T(8,128)(2,1)} custom-call(s32[1]{0:T(128)} %bitcast.side, bf16[4,384,384]{2,1,0:T(8,128)(2,1)} %get-tuple-element.52.picks.refs_0_, f32[1536,1]{1,0:T(8,128)} %get-tuple-element.53.w_col.refs_1_, bf16[1536,128]{1,0:T(8,128)(2,1)} %get-tuple-element.54.basis_t.refs_2_, f32[768,1024]{1,0:T(8,128)} %get-tuple-element.74.part, ...), custom_call_target="tpu_custom_call" | custom-call | tf_op jit(solution)/shard_map/last_stage/pallas_call | solution.py:507
  160.7 0.0 collective-permute-done.10.refs_9_
  160.7 0.0 collective-permute-done.11.refs_10_
  160.7 0.0 collective-permute-done.9.refs_8_
  160.7 0.0 collective-permute-done.8.refs_7_
  160.7 5.8 %last_stage.3 = bf16[1536,1024]{1,0:T(8,128)(2,1)} custom-call(bf16[1536,1024]{1,0:T(8,128)(2,1)} %last_stage.2._, bf16[4,384,384]{2,1,0:T(8,128)(2,1)} %get-tuple-element.52.picks.refs_0_, f32[1536,1]{1,0:T(8,128)} %get-tuple-element.53.w_col.refs_1_, bf16[1536,128]{1,0:T(8,128)(2,1)} %get-tuple-element.54.basis_t.refs_2_, ...), custom_call_target="tpu_custom_call", output_to_operand_aliasing={{}: (0, {})} | custom-call | tf_op jit(solution)/shard_map/last_stage/pallas_call | solution.py:507
Async XLA Ops:
  2.4 20.5 %collective-permute-start = (bf16[432,1024]{1,0:T(8,128)(2,1)}, bf16[432,1024]{1,0:T(8,128)(2,1)}, u32[]{:S(2)}, u32[]{:S(2)}) collective-permute-start(bf16[432,1024]{1,0:T(8,128)(2,1)} %get-tuple-element.50), channel_id=1, source_target_pairs={{0,1},{1,2},{2,3},{3,4},{4,5},{5,6},{6,7},{8,9},{9,10},{10,11},{11... | collective-permute-start | bytes 2654216 | tf_op jit(solution)/shard_map/ppermute | solution.py:525
  7.4 27.9 %collective-permute-start.1 = (bf16[432,1024]{1,0:T(8,128)(2,1)}, bf16[432,1024]{1,0:T(8,128)(2,1)}, u32[]{:S(2)}, u32[]{:S(2)}) collective-permute-start(bf16[432,1024]{1,0:T(8,128)(2,1)} %get-tuple-element.57), channel_id=1, source_target_pairs={{1,0},{2,1},{3,2},{4,3},{5,4},{6,5},{7,6},{9,8},{10,9},{11,10},{12... | collective-permute-start | bytes 2654216 | tf_op jit(solution)/shard_map/ppermute | solution.py:525
  13.0 26.3 %collective-permute-start.2 = (bf16[80,1024]{1,0:T(8,128)(2,1)}, bf16[80,1024]{1,0:T(8,128)(2,1)}, u32[]{:S(2)}, u32[]{:S(2)}) collective-permute-start(bf16[80,1024]{1,0:T(8,128)(2,1)} %get-tuple-element.63), channel_id=1, source_target_pairs={{8,16},{24,32},{40,48},{56,64},{72,80},{88,96},{104,112},{120,128}... | collective-permute-start | bytes 491528 | tf_op jit(solution)/shard_map/ppermute | solution.py:533
  14.3 24.9 %collective-permute-start.3 = (bf16[80,1024]{1,0:T(8,128)(2,1)}, bf16[80,1024]{1,0:T(8,128)(2,1)}, u32[]{:S(2)}, u32[]{:S(2)}) collective-permute-start(bf16[80,1024]{1,0:T(8,128)(2,1)} %get-tuple-element.64), channel_id=1, source_target_pairs={{0,8},{8,0},{16,24},{24,16},{32,40},{40,32},{48,56},{56,48},{64,72... | collective-permute-start | bytes 491528 | tf_op jit(solution)/shard_map/ppermute | solution.py:533
  16.9 49.2 %collective-permute-start.4 = (bf16[352,1024]{1,0:T(8,128)(2,1)}, bf16[352,1024]{1,0:T(8,128)(2,1)}, u32[]{:S(2)}, u32[]{:S(2)}) collective-permute-start(bf16[352,1024]{1,0:T(8,128)(2,1)} %get-tuple-element.65), channel_id=1, source_target_pairs={{8,16},{24,32},{40,48},{56,64},{72,80},{88,96},{104,112},{120,128}... | collective-permute-start | bytes 2162696 | tf_op jit(solution)/shard_map/ppermute | solution.py:533
  22.9 43.2 %collective-permute-start.5 = (bf16[352,1024]{1,0:T(8,128)(2,1)}, bf16[352,1024]{1,0:T(8,128)(2,1)}, u32[]{:S(2)}, u32[]{:S(2)}) collective-permute-start(bf16[352,1024]{1,0:T(8,128)(2,1)} %get-tuple-element.66), channel_id=1, source_target_pairs={{0,8},{8,0},{16,24},{24,16},{32,40},{40,32},{48,56},{56,48},{64,72... | collective-permute-start | bytes 2162696 | tf_op jit(solution)/shard_map/ppermute | solution.py:533
  41.9 36.5 %all-to-all-start = ((bf16[32,48,128]{2,1,0:T(8,128)(2,1)}), bf16[32,48,128]{2,1,0:T(8,128)(2,1)}, u32[]{:S(2)}, u32[]{:S(2)}) async-start(bf16[32,48,128]{2,1,0:T(8,128)(2,1)} %load_stage.1), calls=%async_computation | async-start | bytes 786432 | tf_op jit(solution)/shard_map/all_to_all | solution.py:574
  74.0 59.4 %collective-permute-start.6 = (s16[400,1024]{1,0:T(8,128)(2,1)}, s16[400,1024]{1,0:T(8,128)(2,1)}, u32[]{:S(2)}, u32[]{:S(2)}) collective-permute-start(s16[400,1024]{1,0:T(8,128)(2,1)} %get-tuple-element.87), channel_id=1, source_target_pairs={{8,16},{24,32},{40,48},{56,64},{72,80},{88,96},{104,112},{120,128}... | collective-permute-start | bytes 2457608 | tf_op jit(solution)/shard_map/ppermute | solution.py:533
  75.7 57.8 %collective-permute-start.7 = (s16[400,1024]{1,0:T(8,128)(2,1)}, s16[400,1024]{1,0:T(8,128)(2,1)}, u32[]{:S(2)}, u32[]{:S(2)}) collective-permute-start(s16[400,1024]{1,0:T(8,128)(2,1)} %get-tuple-element.88), channel_id=1, source_target_pairs={{0,8},{8,0},{16,24},{24,16},{32,40},{40,32},{48,56},{56,48},{64,72... | collective-permute-start | bytes 2457608 | tf_op jit(solution)/shard_map/ppermute | solution.py:533
  82.9 25.5 %all-to-all-start.1 = ((f32[8,40,128]{2,1,0:T(8,128)}), f32[8,40,128]{2,1,0:T(8,128)}, u32[]{:S(2)}, u32[]{:S(2)}) async-start(f32[8,40,128]{2,1,0:T(8,128)} %get-tuple-element.78), calls=%async_computation.1 | async-start | bytes 327680 | tf_op jit(solution)/shard_map/all_to_all | solution.py:583
  102.7 58.0 %collective-permute-start.10 = (s16[400,1024]{1,0:T(8,128)(2,1)}, s16[400,1024]{1,0:T(8,128)(2,1)}, u32[]{:S(2)}, u32[]{:S(2)}) collective-permute-start(s16[400,1024]{1,0:T(8,128)(2,1)} %get-tuple-element.93), channel_id=1, source_target_pairs={{0,1},{1,2},{2,3},{3,4},{4,5},{5,6},{6,7},{8,9},{9,10},{10,11},{11... | collective-permute-start | bytes 2457608 | tf_op jit(solution)/shard_map/ppermute | solution.py:525
  106.5 54.2 %collective-permute-start.11 = (s16[400,1024]{1,0:T(8,128)(2,1)}, s16[400,1024]{1,0:T(8,128)(2,1)}, u32[]{:S(2)}, u32[]{:S(2)}) collective-permute-start(s16[400,1024]{1,0:T(8,128)(2,1)} %get-tuple-element.94), channel_id=1, source_target_pairs={{1,0},{2,1},{3,2},{4,3},{5,4},{6,5},{7,6},{9,8},{10,9},{11,10},{12... | collective-permute-start | bytes 2457608 | tf_op jit(solution)/shard_map/ppermute | solution.py:525
  112.0 33.3 %all-to-all-start.2 = ((bf16[32,32,128]{2,1,0:T(8,128)(2,1)}), bf16[32,32,128]{2,1,0:T(8,128)(2,1)}, u32[]{:S(2)}, u32[]{:S(2)}) async-start(bf16[32,32,128]{2,1,0:T(8,128)(2,1)} %coarse_stage.1), calls=%async_computation.2 | async-start | bytes 524288 | tf_op jit(solution)/shard_map/all_to_all | solution.py:590
  145.3 15.4 %collective-permute-start.9 = (bf16[1024,128]{1,0:T(8,128)(2,1)}, bf16[1024,128]{1,0:T(8,128)(2,1)}, u32[]{:S(2)}, u32[]{:S(2)}) collective-permute-start(bf16[1024,128]{1,0:T(8,128)(2,1)} %bitcast.8.primal.far_p.near_p.refs_4_), channel_id=1, source_target_pairs={{1,0},{2,1},{3,2},{4,3},{5,4},{6,5},{7,6},{9,8},{10,9},{11,10},{12... | collective-permute-start | bytes 786440 | tf_op jit(solution)/shard_map/ppermute | solution.py:525
  149.4 11.3 %collective-permute-start.8 = (bf16[1024,128]{1,0:T(8,128)(2,1)}, bf16[1024,128]{1,0:T(8,128)(2,1)}, u32[]{:S(2)}, u32[]{:S(2)}) collective-permute-start(bf16[1024,128]{1,0:T(8,128)(2,1)} %bitcast.8.primal.far_p.near_p.refs_4_), channel_id=1, source_target_pairs={{0,1},{1,2},{2,3},{3,4},{4,5},{5,6},{6,7},{8,9},{9,10},{10,11},{11... | collective-permute-start | bytes 786440 | tf_op jit(solution)/shard_map/ppermute | solution.py:525

commit v3 on v2

--- a/solution.py
+++ b/solution.py
@@ -9,7 +9,7 @@
 F32, BF16, I16, I32 = jnp.float32, jnp.bfloat16, jnp.int16, jnp.int32
 LANES = 128
 SLOT = 40
-ROWS = 48
+PACK = 16
 EARLY = 32
 EXTRA = 16
 BASE = 16
@@ -52,74 +52,66 @@
     return jnp.where(ids == index_row, 1.0, 0.0)
 
 
-def first_kernel(fs, side, weights, orders, basis, x, far_a, far_b, near_a, near_b):
-    nc = basis.shape[0]
-
-    def fill(face, ahead, behind):
+def pack(out, row, block):
+    nc, fs = block.shape
+    spare = out.shape[1] - 2 * fs
+    out[row : row + PACK, :] = jnp.zeros((PACK, out.shape[1]), BF16)
+    out[row : row + PACK, 0:fs] = block[0:PACK]
+    out[row : row + PACK, fs : 2 * fs] = block[PACK : 2 * PACK]
+    last = block[2 * PACK : nc]
+    out[row : row + nc - 2 * PACK, 2 * fs :] = last[:, 0:spare]
+    out[row + 8 : row + 8 + nc - 2 * PACK, 2 * fs : 3 * fs - spare] = last[:, spare:]
+
+
+def unpacked(rows, fs):
+    rows = rows.astype(F32)
+    spare = rows.shape[1] - 2 * fs
+    last = jnp.concatenate([rows[0:8, 2 * fs :], rows[8:16, 2 * fs : 3 * fs - spare]], axis=1)
+    return jnp.concatenate([rows[:, 0:fs], rows[:, fs : 2 * fs], last], axis=0)
+
+
+def first_kernel(fs, side, grp_side, weights, orders, basis, x, far_g, near_g, far_a, far_b, near_a, near_b):
+    def grp_face(face, out):
+        pack(out, 0, basis[:, face * fs : (face + 1) * fs])
+        out[PACK:, :] = x[face * fs : (face + 1) * fs, :]
+
+    def grp_faces(one, two):
+        grp_face(one, far_g)
+        grp_face(two, near_g)
+
+    by_side(grp_side, lambda: grp_faces(2, 3), lambda: grp_faces(3, 2))
+
+    def sub_face(face, ahead, behind):
         at = slice(face * fs, (face + 1) * fs)
-        ahead[ROWS:, :] = x[face * fs : face * fs + EARLY, :]
+        ahead[2 * PACK :, :] = x[face * fs : face * fs + EARLY, :]
         behind[...] = x[face * fs + EARLY : (face + 1) * fs, :]
         part = basis[:, at]
         scaled = (part.astype(F32) * weights[:, at]).astype(BF16)
         turned = dot(scaled, one_hot_lanes(fs, orders[face : face + 1, :]).astype(BF16), ((1,), (1,)))
-        ahead[0:ROWS, :] = jnp.zeros((ROWS, ahead.shape[1]), BF16)
-        ahead[0:nc, 0:fs] = turned.astype(BF16)
-        ahead[0:nc, fs : 2 * fs] = part
-
-    def even():
-        fill(0, far_a, far_b)
-        fill(1, near_a, near_b)
-
-    def odd():
-        fill(1, far_a, far_b)
-        fill(0, near_a, near_b)
-
-    by_side(side, even, odd)
-
-
-def first_stage(side, x, weights, orders, basis):
+        pack(ahead, 0, turned.astype(BF16))
+        pack(ahead, PACK, part)
+
+    def sub_faces(one, two):
+        sub_face(one, far_a, far_b)
+        sub_face(two, near_a, near_b)
+
+    by_side(side, lambda: sub_faces(0, 1), lambda: sub_faces(1, 0))
+
+
+def first_stage(side, grp_side, x, weights, orders, basis):
     nb, m = x.shape
     fs = nb // 4
-    ahead = jax.ShapeDtypeStruct((EARLY + ROWS, m), BF16)
+    face = jax.ShapeDtypeStruct((fs + PACK, m), BF16)
+    ahead = jax.ShapeDtypeStruct((EARLY + 2 * PACK, m), BF16)
     behind = jax.ShapeDtypeStruct((fs - EARLY, m), BF16)
     return pl.pallas_call(
         functools.partial(first_kernel, fs),
-        grid=(1,),
-        in_specs=[SIDE, whole(weights.shape), whole(orders.shape), whole(basis.shape), whole((2 * fs, m))],
-        out_specs=[whole(ahead.shape), whole(behind.shape)] * 2,
-        out_shape=[ahead, behind] * 2,
+        in_specs=[SIDE, SIDE] + [pl.BlockSpec(memory_space=pltpu.VMEM)] * 4,
+        out_shape=[face, face] + [ahead, behind] * 2,
         compiler_params=params(),
         cost_estimate=FREE,
         name="first_stage",
-    )(side, weights, orders, basis, x)
-
-
-def cut_kernel(fs, basis, x_one, x_two, one, two):
-    nc = basis.shape[0]
-    for face, x, out in ((2, x_one, one), (3, x_two, two)):
-        out[ROWS:, :] = x[...]
-
-        @pl.when(pl.program_id(0) == 0)
-        def _():
-            out[0:ROWS, :] = jnp.zeros((ROWS, out.shape[1]), BF16)
-            out[0:nc, 0:fs] = basis[:, face * fs : (face + 1) * fs]
-
-
-def cut(x, basis):
-    nb, m = x.shape
-    fs, width = nb // 4, m // 2
-    col = lambda n, k: spec((n, width), lambda i: (k, i))
-    face = jax.ShapeDtypeStruct((fs + ROWS, m), BF16)
-    return pl.pallas_call(
-        functools.partial(cut_kernel, fs),
-        grid=(2,),
-        in_specs=[whole(basis.shape), col(fs, 2), col(fs, 3)],
-        out_specs=[col(fs + ROWS, 0), col(fs + ROWS, 0)],
-        out_shape=[face, face],
-        compiler_params=params(),
-        cost_estimate=FREE,
-        name="cut",
-    )(basis, x, x)
+    )(side, grp_side, weights, orders, basis, x)
 
 
 def on_lanes(rows, offset):
@@ -176,16 +168,18 @@
     return jnp.concatenate(each, axis=0)
 
 
-def far_kernel(basis, picks, w_col, rest, left, right, other_out, rest_out):
+def far_kernel(side, basis, picks, w_col, rest, far, near, other_out, rest_out):
     nc, nb = basis.shape
-    fs = nb // 4
-    other = met(picks, w_col, (left[ROWS:, :], right[ROWS:, :]))
-    other_out[...] = other
+
+    def arrived(left, right):
+        other_out[...] = met(picks, w_col, (left[PACK:, :], right[PACK:, :]))
+
+    by_side(side, lambda: arrived(far, near), lambda: arrived(near, far))
     rest_out[...] = rest[...]
-    rest_out[0:nc, :] += dot(basis[:, nb // 2 :], other)
-
-
-def far_stage(basis, picks, w_col, rest, left, right):
+    rest_out[0:nc, :] += dot(basis[:, nb // 2 :], other_out[...])
+
+
+def far_stage(side, basis, picks, w_col, rest, far, near):
     m = rest.shape[1]
     nb = w_col.shape[0]
     fs, half, width = nb // 4, nb // 2, m // 2
@@ -194,19 +188,20 @@
         far_kernel,
         grid=(2,),
         in_specs=[
+            SIDE,
             whole(basis.shape),
             spec((2, fs, fs), lambda i: (1, 0, 0)),
             spec((half, 1), lambda i: (1, 0)),
             col(SLOT),
-            col(left.shape[0]),
-            col(right.shape[0]),
+            col(far.shape[0]),
+            col(near.shape[0]),
         ],
         out_specs=[col(half), col(SLOT)],
         out_shape=[jax.ShapeDtypeStruct((half, m), BF16), jax.ShapeDtypeStruct((SLOT, m), F32)],
         compiler_params=params(),
         cost_estimate=FREE,
         name="far_stage",
-    )(basis, picks, w_col, rest, left, right)
+    )(side, basis, picks, w_col, rest, far, near)
 
 
 def load_kernel(nc, cols, side, ids, rest, x, far, near, load, digits, shares):
@@ -220,8 +215,8 @@
         digits[1:2, 0:nc] = (ids[...] - top * BASE).astype(F32)
 
     def share(low, high):
-        shares[0:SLOT, :] = dot(low[0:ROWS, 0:fs], x[0:fs])[0:SLOT]
-        shares[SLOT:, :] = dot(high[0:ROWS, 0:fs], x[fs:])[0:SLOT]
+        shares[0:SLOT, :] = dot(unpacked(low[...], fs).astype(BF16), x[0:fs])
+        shares[SLOT:, :] = dot(unpacked(high[...], fs).astype(BF16), x[fs:])
 
     by_side(side, lambda: share(far, near), lambda: share(near, far))
     none = jnp.zeros((LANES - 3 * SLOT, rest.shape[1]), F32)
@@ -239,7 +234,7 @@
     return pl.pallas_call(
         functools.partial(load_kernel, nc, cols),
         grid=(2,),
-        in_specs=[SIDE, whole(ids.shape), col(SLOT), col(half), whole((ROWS, m)), whole((ROWS, m))],
+        in_specs=[SIDE, whole(ids.shape), col(SLOT), col(half), whole((PACK, m)), whole((PACK, m))],
         out_specs=spec((width // cols, cols + 16, LANES), lambda i: (i, 0, 0)),
         out_shape=jax.ShapeDtypeStruct((subs, cols + 16, LANES), BF16),
         scratch_shapes=[pltpu.VMEM((16, LANES), F32), pltpu.VMEM((2 * SLOT, width), F32)],
@@ -249,21 +244,40 @@
     )(side, ids, rest, x, far, near)
 
 
+def own_kernel(inverse, own, acc):
+    acc[...] = dot(inverse[...], own[...])
+
+
+def own_stage(inverse, own):
+    nb, m = own.shape
+    tall = nb // 4
+    return pl.pallas_call(
+        own_kernel,
+        grid=(2,),
+        in_specs=[spec((tall, nb), lambda i: (2 + i, 0)), whole(own.shape)],
+        out_specs=spec((tall, m), lambda i: (i, 0)),
+        out_shape=jax.ShapeDtypeStruct((nb // 2, m), F32),
+        compiler_params=params(),
+        cost_estimate=FREE,
+        name="own_stage",
+    )(inverse, own)
+
+
 def acc_kernel(half, inverse, own, other, acc):
     acc[...] = dot(inverse[...], own[...]) + dot(inverse[:, half:], other[...])
 
 
-def acc_stage(place, inverse, own, other, cost):
+def acc_stage(inverse, own, other):
     nb, m = own.shape
     tall = nb // 4
     return pl.pallas_call(
         functools.partial(acc_kernel, nb // 2),
         grid=(2,),
-        in_specs=[spec((tall, nb), lambda i: (2 * place + i, 0)), whole(own.shape), whole(other.shape)],
+        in_specs=[spec((tall, nb), lambda i: (i, 0)), whole(own.shape), whole(other.shape)],
         out_specs=spec((tall, m), lambda i: (i, 0)),
         out_shape=jax.ShapeDtypeStruct((nb // 2, m), F32),
         compiler_params=params(),
-        cost_estimate=cost,
+        cost_estimate=LONG,
         name="acc_stage",
     )(inverse, own, other)
 
@@ -276,78 +290,99 @@
     q_ref[fs:, :] = jnp.broadcast_to(power.astype(I32), (EXTRA, values.shape[1])).astype(I16)
 
 
-def part_kernel(side, picks, w_col, inverse, far_a, far_b, near_a, near_b, acc, part, q_far, q_near, other_out, other):
-    @pl.when(pl.program_id(0) == 0)
-    def _():
-        far = jnp.concatenate([far_a[ROWS:, :], far_b[...]], axis=0)
-        near = jnp.concatenate([near_a[ROWS:, :], near_b[...]], axis=0)
-
-        def arrived(faces):
-            other[...] = met(picks, w_col, faces)
-
-        by_side(side, lambda: arrived((far, near)), lambda: arrived((near, far)))
-        other_out[...] = other[...]
-
+def part_far_kernel(side, picks, w_col, inverse, far_a, far_b, near_a, near_b, acc, part, q, other_out, other):
+    far = jnp.concatenate([far_a[2 * PACK :, :], far_b[...]], axis=0)
+    near = jnp.concatenate([near_a[2 * PACK :, :], near_b[...]], axis=0)
+
+    def arrived(faces):
+        other[...] = met(picks, w_col, faces)
+
+    by_side(side, lambda: arrived((far, near)), lambda: arrived((near, far)))
+    other_out[...] = other[...]
     total = acc[...] + dot(inverse[...], other[...])
     part[...] = total
+    coded(total, q)
+
+
+def part_near_kernel(side, inverse, other, acc, part, q):
+    total = acc[...] + dot(inverse[...], other[...])
+    part[...] = total
+    coded(total, q)
+
+
+def part_stage(side, inverse, acc, faces, other=None):
+    half, m = acc.shape
+    fs, width = half // 2, m // 2
+    far = other is None
+    face = lambda side: side[0] if far else 1 - side[0]
+    col = lambda n: pl.BlockSpec((n, width), lambda i, side: (0, i))
+    outs = [jax.ShapeDtypeStruct((fs, m), F32), jax.ShapeDtypeStruct((fs + EXTRA, m), I16)]
+    rows = [
+        pl.BlockSpec((fs, half), lambda i, side: (face(side), 0)),
+        pl.BlockSpec((fs, width), lambda i, side: (face(side), i)),
+    ]
+    if far:
+        picks, w_col, *pieces = faces
+        args = [picks, w_col, inverse, *pieces, acc]
+        in_specs = [
+            pl.BlockSpec((2, fs, fs), lambda i, side: (0, 0, 0)),
+            pl.BlockSpec((half, 1), lambda i, side: (0, 0)),
+            rows[0],
+            *[col(piece.shape[0]) for piece in pieces],
+            rows[1],
+        ]
+        outs.append(jax.ShapeDtypeStruct((half, m), BF16))
+    else:
+        args = [inverse, other, acc]
+        in_specs = [rows[0], col(half), rows[1]]
+    return pl.pallas_call(
+        part_far_kernel if far else part_near_kernel,
+        grid_spec=pltpu.PrefetchScalarGridSpec(
+            num_scalar_prefetch=1,
+            grid=(2,),
+            in_specs=in_specs,
+            out_specs=[col(out.shape[0]) for out in outs],
+            scratch_shapes=[pltpu.VMEM((half, width), BF16)] if far else [],
+        ),
+        out_shape=outs,
+        compiler_params=params(),
+        cost_estimate=FREE,
+        name="part_stage",
+    )(side, *args)
+
+
+def part_grp_kernel(half, side, inverse, other_sub, other_grp, acc, far_part, near_part, q_far, q_near):
+    total = acc[...] + dot(inverse[:, 0:half], other_sub[...]) + dot(inverse[:, half:], other_grp[...])
+
+    def keep(part, q):
+        part[...] = total
+        coded(total, q)
+
     is_far = pl.program_id(0) == side[0]
-    pl.when(is_far)(lambda: coded(total, q_far))
-    pl.when(jnp.logical_not(is_far))(lambda: coded(total, q_near))
-
-
-def part_stage(side, picks, w_col, inverse, far, near, acc):
+    pl.when(is_far)(lambda: keep(far_part, q_far))
+    pl.when(jnp.logical_not(is_far))(lambda: keep(near_part, q_near))
+
+
+def part_grp_stage(side, inverse, other_sub, other_grp, acc):
     half, m = acc.shape
     fs = half // 2
-    row = lambda n: spec((fs, n), lambda i: (i, 0))
     code = jax.ShapeDtypeStruct((fs + EXTRA, m), I16)
     return pl.pallas_call(
-        part_kernel,
+        functools.partial(part_grp_kernel, half),
         grid=(2,),
         in_specs=[
             SIDE,
-            spec((2, fs, fs), lambda i: (0, 0, 0)),
-            spec((half, 1), lambda i: (0, 0)),
-            row(half),
-            whole(far[0].shape),
-            whole(far[1].shape),
-            whole(near[0].shape),
-            whole(near[1].shape),
-            row(m),
-        ],
-        out_specs=[row(m), whole(code.shape), whole(code.shape), whole((half, m))],
-        out_shape=[jax.ShapeDtypeStruct((half, m), F32), code, code, jax.ShapeDtypeStruct((half, m), BF16)],
-        scratch_shapes=[pltpu.VMEM((half, m), BF16)],
-        compiler_params=params(),
-        cost_estimate=FREE,
-        name="part_stage",
-    )(side, picks, w_col, inverse, *far, *near, acc)
-
-
-def part_grp_kernel(inverse, other, acc, part, q_one, q_two):
-    total = acc[...] + dot(inverse[...], other[...])
-    part[...] = total
-    for face, q in enumerate((q_one, q_two)):
-        pl.when(pl.program_id(0) == face)(functools.partial(coded, total, q))
-
-
-def part_grp_stage(inverse, other, acc):
-    half, m = acc.shape
-    fs = half // 2
-    code = jax.ShapeDtypeStruct((fs + EXTRA, m), I16)
-    return pl.pallas_call(
-        part_grp_kernel,
-        grid=(2,),
-        in_specs=[
-            spec((fs, half), lambda i: (2 + i, 0)),
-            whole(other.shape),
+            spec((fs, 2 * half), lambda i: (2 + i, 0)),
+            whole(other_sub.shape),
+            whole(other_grp.shape),
             spec((fs, m), lambda i: (i, 0)),
         ],
-        out_specs=[spec((fs, m), lambda i: (i, 0)), whole(code.shape), whole(code.shape)],
-        out_shape=[jax.ShapeDtypeStruct((half, m), F32), code, code],
+        out_specs=[whole((fs, m))] * 2 + [whole(code.shape)] * 2,
+        out_shape=[jax.ShapeDtypeStruct((fs, m), F32)] * 2 + [code, code],
         compiler_params=params(),
         cost_estimate=FREE,
         name="part_grp_stage",
-    )(inverse, other, acc)
+    )(side, inverse, other_sub, other_grp, acc)
 
 
 def static_kernel(basis_in, slots_in, coarse_in, basis, slots, up, coarse):
@@ -462,48 +497,41 @@
     return (lambda _, *refs: kernel(*refs)), [target] + args, [pl.BlockSpec(memory_space=pl.ANY)] + in_specs
 
 
-def last_kernel(fs, offsets, lane, side, picks, w_col, basis_t, part, primal, far, near, far_p, near_p, far_q, near_q, out, lifts):
+def last_kernel(fs, offsets, side, picks, w_col, basis_t, far_part, near_part, primal, far, near, far_p, near_p, far_q, near_q, out, lifts):
     nt = ((1,), (1,))
 
     def finish(faces):
         @pl.when(pl.program_id(0) == 0)
         def _():
-            for face, (rows, _, _) in enumerate(faces):
-                lifts[face] = on_lanes(rows[0:SLOT, lane : lane + fs].astype(F32), offsets[face])
-
-        for face, (_, primal_n, q) in enumerate(faces):
+            for face, (rows, _, _, _) in enumerate(faces):
+                lifts[face] = on_lanes(unpacked(rows[...], fs), offsets[face])
+
+        for face, (_, part, primal_n, q) in enumerate(faces):
             at = slice(face * fs, (face + 1) * fs)
-            mine = (part[at] + dot(basis_t[at], primal[...], nt)).astype(BF16)
+            mine = (part[...] + dot(basis_t[at], primal[...], nt)).astype(BF16)
             scale = jnp.exp2(q[fs:, :].astype(I32).astype(F32)[0:1])
             theirs = q[0:fs, :].astype(I32).astype(F32) * scale
             theirs = (theirs + dot(lifts[face], primal_n[...], nt)).astype(BF16)
             arrived = dot(picks[face], theirs)
             out[at] = (w_col[at] * (mine.astype(F32) + arrived)).astype(BF16)
 
-    one, two = (far, far_p, far_q), (near, near_p, near_q)
-    if side is None:
-        finish((one, two))
-    else:
-        by_side(side, lambda: finish((one, two)), lambda: finish((two, one)))
-
-
-def last_stage(place, offsets, lane, side, picks, w_col, basis_t, part, primal, far, near, far_p, near_p, codes, target=None):
-    half, m = part.shape
-    fs = half // 2
-    width = m // 2
+    one, two = (far, far_part, far_p, far_q), (near, near_part, near_p, near_q)
+    by_side(side, lambda: finish((one, two)), lambda: finish((two, one)))
+
+
+def last_stage(place, offsets, block, side, picks, w_col, basis_t, parts, primal, far, near, far_p, near_p, codes, target=None):
+    fs, m = parts[0].shape
+    half, width = 2 * fs, m // 2
     mine = lambda k: spec((half, k), lambda i: (place, 0))
+    part = spec((fs, width), lambda i: (0, i))
     primal_spec = spec((width, LANES), lambda i: (i, 0))
-    basis_spec = whole((ROWS, far.shape[1]))
-    in_specs = [spec((2, fs, fs), lambda i: (place, 0, 0)), mine(1), mine(LANES), spec((half, width), lambda i: (0, i))]
+    basis_spec = spec((PACK, m), lambda i: (block, 0))
+    in_specs = [spec((2, fs, fs), lambda i: (place, 0, 0)), mine(1), mine(LANES), part, part]
     in_specs += [primal_spec, basis_spec, basis_spec, primal_spec, primal_spec]
     in_specs += [spec((fs + EXTRA, width), lambda i: (0, i))] * 2
-    args = [picks, w_col, basis_t, part, primal, far, near, far_p, near_p, *codes]
-    kernel = functools.partial(last_kernel, fs, offsets, lane)
-    if side is None:
-        kernel = functools.partial(kernel, None)
-    else:
-        args, in_specs = [side] + args, [SIDE] + in_specs
-    kernel, args, in_specs = into(kernel, target, args, in_specs)
+    args = [picks, w_col, basis_t, *parts, primal, far, near, far_p, near_p, *codes]
+    args, in_specs = [side] + args, [SIDE] + in_specs
+    kernel, args, in_specs = into(functools.partial(last_kernel, fs, offsets), target, args, in_specs)
     return pl.pallas_call(
         kernel,
         grid=(2,),
@@ -518,19 +546,16 @@
     )(*args)
 
 
-def exchange(faces, axis):
+def swap(far_out, near_out, axis):
     size = lax.axis_size(axis)
-    up = [(i, i + 1) for i in range(size - 1)]
-    down = [(j, i) for i, j in up]
-    return lax.ppermute(faces[1], axis, up), lax.ppermute(faces[0], axis, down)
-
-
-def swap(far_out, near_out):
-    size = lax.axis_size("sub")
     near = [(i, i ^ 1) for i in range(size)]
     far = [(i, i + 1) for i in range(1, size - 1, 2)]
     far += [(j, i) for i, j in far]
-    return lax.ppermute(far_out, "sub", far), lax.ppermute(near_out, "sub", near)
+    return lax.ppermute(far_out, axis, far), lax.ppermute(near_out, axis, near)
+
+
+def side_of(axis):
+    return lax.rem(lax.axis_index(axis), 2).astype(I32).reshape(1)
 
 
 def together(*values):
@@ -558,45 +583,46 @@
     orders = face_map[0, 0]
     coarse_rows = basis[0, 0]
 
-    side = lax.rem(lax.axis_index("sub"), 2).astype(I32).reshape(1)
-    fs = nb // 4
-    far_a, far_b, near_a, near_b = first_stage(side, x, w_row, orders, coarse_rows)
-    far_a, near_a = swap(far_a, near_a)
-    far_b, near_b = swap(far_b, near_b)
-    left, right = exchange(cut(x, coarse_rows), "grp")
-
-    w_row, left = together(w_row, left)
+    side, grp_side = side_of("sub"), side_of("grp")
+    far_g, near_g, far_a, far_b, near_a, near_b = first_stage(side, grp_side, x, w_row, orders, coarse_rows)
+    far_a, near_a = swap(far_a, near_a, "sub")
+    far_b, near_b = swap(far_b, near_b, "sub")
+    far_g, near_g = swap(far_g, near_g, "grp")
+
+    w_row, near_g = together(w_row, near_g)
     own, rest, picks, w_col, basis_t = base_stage(w_row, orders, coarse_rows, x)
-    other_grp, rest = far_stage(coarse_rows, picks, w_col, rest, left, right)
-    g_basis, slots, up = static_stage(group_basis[0], group_index, coarse_inverse)
-    rest, g_basis, slots, up = together(rest, g_basis, slots, up)
+    acc_grp = own_stage(inverse, own)
+    rest, acc_grp = together(rest, acc_grp)
+    other_grp, rest = far_stage(grp_side, coarse_rows, picks, w_col, rest, far_g, near_g)
     load = load_stage(nc, side, primal_index[0], rest, x, far_a, near_a, subs)
     loads = lax.all_to_all(load, "sub", 0, 0, tiled=True)
-    other_grp, load = together(other_grp, load)
-    acc_sub = acc_stage(0, inverse, own, other_grp, LONG)
-    far_b, near_b, acc_sub = together(far_b, near_b, acc_sub)
-    part_sub, q_far, q_near, other_sub = part_stage(side, picks, w_col, inverse, (far_a, far_b), (near_a, near_b), acc_sub)
-    q_far, q_near = swap(q_far, q_near)
-
-    loads, part_sub = together(loads, part_sub)
+    other_grp, group_index, load = together(other_grp, group_index, load)
+    g_basis, slots, up = static_stage(group_basis[0], group_index, coarse_inverse)
+    acc_sub = acc_stage(inverse, own, other_grp)
+    far_b, near_b, acc_sub, up = together(far_b, near_b, acc_sub, up)
+    faces = (picks, w_col, far_a, far_b, near_a, near_b)
+    part_far, q_far, other_sub = part_stage(side, inverse, acc_sub, faces)
+    loads, part_far = together(loads, part_far)
     group_local, send, index = group_stage(loads, group_inverse[0], g_basis, slots, nc, groups)
     received = lax.all_to_all(send, "grp", 0, 0, tiled=True)
-    other_sub, other_grp, send = together(other_sub, other_grp, send)
-    acc_grp = acc_stage(1, inverse, own, other_grp, FREE)
-    part_grp, q_three, q_four = part_grp_stage(inverse, other_sub, acc_grp)
-    q_left, q_right = exchange((q_three, q_four), "grp")
-    received, part_grp = together(received, part_grp)
+    other_sub, send = together(other_sub, send)
+    part_near, q_near = part_stage(side, inverse, acc_sub, None, other_sub)
+    q_far, q_near = swap(q_far, q_near, "sub")
+    other_sub, part_near = together(other_sub, part_near)
+    far_grp, near_grp, q_far_g, q_near_g = part_grp_stage(grp_side, inverse, other_sub, other_grp, acc_grp)
+    q_far_g, q_near_g = swap(q_far_g, q_near_g, "grp")
+    received, far_grp = together(received, far_grp)
     picked = coarse_stage(received, group_local, up, index)
     primal = lax.all_to_all(picked, "sub", 0, 0, tiled=True).reshape(m, LANES)
     primal, q_far, q_near = together(primal, q_far, q_near)
-    primal_left, primal_right = exchange((primal, primal), "grp")
+    far_p, near_p = swap(primal, primal, "grp")
 
     mine = (picks, w_col, basis_t)
     out = last_stage(
-        0, (SLOT, 2 * SLOT), fs, side, *mine, part_sub, primal, far_a, near_a, primal, primal, (q_far, q_near)
+        0, (SLOT, 2 * SLOT), 1, side, *mine, (part_far, part_near), primal, far_a, near_a, primal, primal, (q_far, q_near)
     )
     out = last_stage(
-        1, (0, 0), 0, None, *mine, part_grp, primal, left, right, primal_left, primal_right, (q_left, q_right), out
+        1, (0, 0), 0, grp_side, *mine, (far_grp, near_grp), primal, far_g, near_g, far_p, near_p, (q_far_g, q_near_g), out
     )
     return out[None, None]
 

time: 167 us -> 160 us (0.958)
  starting transfers between devices: 83.3 us -> 72.8 us
  Pallas kernels: 69.7 us -> 71.4 us
    ppermute x12, starting transfers between devices: 39.7 us -> 30.1 us  [the longest x6 18.2 us: swap(): lax.ppermute(near_out, axis, near)]
    pallas_call x5 -> x6, Pallas kernels: 23.5 us -> 32.7 us  [the longest x2 9.61 us: part_stage(): pl.pallas_call(part_far_kernel if far else part_near_kernel, grid_spec=pl...]
    pallas_call x2 -> x1, Pallas kernels: 15.8 us -> 7.93 us  [acc_stage(): pl.pallas_call(functools.partial(acc_kernel, nb // 2), grid=(2,), in_spec...]
    all_to_all x1, starting transfers between devices: 16.3 us -> 14 us  [local(): loads = lax.all_to_all(load, 'sub', 0, 0, tiled=True)]
  transfers between devices with their start and end apart: 15 -> 15, of which waited for: 1 -> 1; matrix products, arithmetic and copies ran while one was open for 1% -> 1% of each run, Pallas kernels for 37% -> 39%
where the time goes in v3:
time: 160 us; the launch traced here: 158 us
  starting transfers between devices  72.8 us (46%)
  Pallas kernels  71.4 us (45%)
  waiting for transfers between devices  12.1 us (8%)
    all_to_all x1, starting transfers between devices, local(): primal = lax.all_to_all(picked, 'sub', 0, 0, tiled=True).reshape(m, LANES)  22.8 us
    ppermute x6, starting transfers between devices, swap(): lax.ppermute(near_out, axis, near)  18.2 us
    all_to_all x1, starting transfers between devices, local(): loads = lax.all_to_all(load, 'sub', 0, 0, tiled=True)  14 us
    pallas_call x2, Pallas kernels, last_stage(): pl.pallas_call(kernel, grid=(2,), in_specs=in_specs, out_specs=spec((half...  12.1 us
    all_to_all x1, waiting for transfers between devices, local(): primal = lax.all_to_all(picked, 'sub', 0, 0, tiled=True).reshape(m, LANES)  12.1 us
    ppermute x6, starting transfers between devices, swap(): lax.ppermute(far_out, axis, far)  12 us
    pallas_call x2, Pallas kernels, part_stage(): pl.pallas_call(part_far_kernel if far else part_near_kernel, grid_spec=pl...  9.61 us
    pallas_call x1, Pallas kernels, part_grp_stage(): pl.pallas_call(functools.partial(part_grp_kernel, half), grid=(2,), in_sp...  8.53 us
  transfers between devices with their start and end apart: 15, of which 1 were waited for; matrix products, arithmetic and copies ran while one was open for 1% of the time, Pallas kernels for 39%

profile of v3, /device:TPU:1, one launch (start us, length us, event | category | flops | bytes accessed | tf_op | source)
XLA Modules:
  0.0 157.9 jit_solution(10790648015936492834)
XLA Ops:
  0.0 4.2 %first_stage.1 = (bf16[400,1024]{1,0:T(8,128)(2,1)}, bf16[400,1024]{1,0:T(8,128)(2,1)}, bf16[64,1024]{1,0:T(8,128)(2,1)}, bf16[352,1024]{1,0:T(8,128)(2,1)}, bf1...) custom-call(s32[1]{0:T(128)} %bitcast.side, s32[1]{0:T(128)} %bitcast.2.grp_side.side.refs_0_, f32[1,1536]{1,0:T(1,128)} %bitcast.27, ...), custom_call_target="tpu_custom_call" | custom-call | tf_op jit(solution)/shard_map/first_stage/pallas_call | solution.py:107
  4.2 3.2 %collective-permute-start = (bf16[400,1024]{1,0:T(8,128)(2,1)}, bf16[400,1024]{1,0:T(8,128)(2,1)}, u32[]{:S(2)}, u32[]{:S(2)}) collective-permute-start(bf16[400,1024]{1,0:T(8,128)(2,1)} %get-tuple-element.53), channel_id=1, source_target_pairs={{0,1},{1,0},{2,3},{3,2},{4,5},{5,4},{6,7},{7,6},{8,9},{9,8},{10,11... | collective-permute-start | bytes 2457608 | tf_op jit(solution)/shard_map/ppermute | solution.py:554
  7.5 1.9 %collective-permute-start.1 = (bf16[400,1024]{1,0:T(8,128)(2,1)}, bf16[400,1024]{1,0:T(8,128)(2,1)}, u32[]{:S(2)}, u32[]{:S(2)}) collective-permute-start(bf16[400,1024]{1,0:T(8,128)(2,1)} %get-tuple-element.61), channel_id=1, source_target_pairs={{1,2},{3,4},{5,6},{2,1},{4,3},{6,5},{9,10},{11,12},{13,14},{10,9},... | collective-permute-start | bytes 2457608 | tf_op jit(solution)/shard_map/ppermute | solution.py:554
  9.4 1.3 collective-permute-start.2
  10.7 2.9 %collective-permute-start.3 = (bf16[64,1024]{1,0:T(8,128)(2,1)}, bf16[64,1024]{1,0:T(8,128)(2,1)}, u32[]{:S(2)}, u32[]{:S(2)}) collective-permute-start(bf16[64,1024]{1,0:T(8,128)(2,1)} %get-tuple-element.65), channel_id=1, source_target_pairs={{0,8},{8,0},{16,24},{24,16},{32,40},{40,32},{48,56},{56,48},{64,72... | collective-permute-start | bytes 393224 | tf_op jit(solution)/shard_map/ppermute | solution.py:554
  13.6 1.5 collective-permute-start.4
  15.1 1.5 copy.14
  16.6 0.0 collective-permute-done.near.refs_8_
  16.6 7.2 %collective-permute-start.5 = (bf16[352,1024]{1,0:T(8,128)(2,1)}, bf16[352,1024]{1,0:T(8,128)(2,1)}, u32[]{:S(2)}, u32[]{:S(2)}) collective-permute-start(bf16[352,1024]{1,0:T(8,128)(2,1)} %get-tuple-element.67), channel_id=1, source_target_pairs={{0,8},{8,0},{16,24},{24,16},{32,40},{40,32},{48,56},{56,48},{64,72... | collective-permute-start | bytes 2162696 | tf_op jit(solution)/shard_map/ppermute | solution.py:554
  23.9 5.0 %base_stage.1 = (bf16[1536,1024]{1,0:T(8,128)(2,1)}, f32[40,1024]{1,0:T(8,128)}, bf16[4,384,384]{2,1,0:T(8,128)(2,1)}, f32[1536,1]{1,0:T(8,128)}, bf16[1536,128]{1,0:T(8,128)(2,1)}) custom-call(f32[1,1536]{1,0:T(1,128)} %bitcast.28, s32[4,384]{1,0:T(4,128)} %bitcast.30, bf16[37,1536]{1,0:T(8,128)(2,1)} %bitcast.23, bf16[1536,1024]{1,0:T(8,128)(2,1)} %bitcast.20), custom_call_target="tpu_custom_call" | custom-call | tf_op jit(solution)/shard_map/base_stage/pallas_call | solution.py:145
  28.9 6.2 %own_stage.1.acc = f32[768,1024]{1,0:T(8,128)} custom-call(bf16[1536,1536]{1,0:T(8,128)(2,1)} %bitcast.14, bf16[1536,1024]{1,0:T(8,128)(2,1)} %get-tuple-element.59.own), custom_call_target="tpu_custom_call" | custom-call | tf_op jit(solution)/shard_map/own_stage/pallas_call | solution.py:254
  35.1 0.0 collective-permute-done.1.far.refs_7_
  35.1 4.1 %far_stage.1 = (bf16[768,1024]{1,0:T(8,128)(2,1)}, f32[40,1024]{1,0:T(8,128)}) custom-call(s32[1]{0:T(128)} %bitcast.2.grp_side.side.refs_0_, bf16[37,1536]{1,0:T(8,128)(2,1)} %bitcast.24, bf16[4,384,384]{2,1,0:T(8,128)(2,1)} %get-tuple-element.55.picks.refs_1_, f32[1536,1]{1,0:T(8,128)} %get-tuple-element.56.w_col.refs_2_, ...), custom_call_target="tpu_custom_call" | custom-call | tf_op jit(solution)/shard_map/far_stage/pallas_call | solution.py:187
  39.2 0.0 collective-permute-done.2.far.far_a
  39.2 0.0 collective-permute-done.3.near.near_a
  39.2 2.6 %load_stage.1 = bf16[32,48,128]{2,1,0:T(8,128)(2,1)} custom-call(s32[1]{0:T(128)} %bitcast.side, s32[1,37]{1,0:T(1,128)} %bitcast.31, f32[40,1024]{1,0:T(8,128)} %get-tuple-element.63.rest, bf16[1536,1024]{1,0:T(8,128)(2,1)} %bitcast.21, bf16[64,1024]{1,0:T(8,128)(2,1)} %collective-permute-done.2.far.far_a, bf16[64,1024]{1,0:T(8,128)(2,1)} %collective-permute-done.3.near.near_a), custom_call_target="tpu_custom_call" | custom-call | tf_op jit(solution)/shard_map/load_stage/pallas_call | solution.py:234
  41.9 14.0 %all-to-all-start = ((bf16[32,48,128]{2,1,0:T(8,128)(2,1)}), bf16[32,48,128]{2,1,0:T(8,128)(2,1)}, u32[]{:S(2)}, u32[]{:S(2)}) async-start(bf16[32,48,128]{2,1,0:T(8,128)(2,1)} %load_stage.1), calls=%async_computation | async-start | bytes 786432 | tf_op jit(solution)/shard_map/all_to_all | solution.py:598
  55.9 7.9 %acc_stage.1.acc = f32[768,1024]{1,0:T(8,128)} custom-call(bf16[1536,1536]{1,0:T(8,128)(2,1)} %bitcast.15, bf16[1536,1024]{1,0:T(8,128)(2,1)} %get-tuple-element.59.own, bf16[768,1024]{1,0:T(8,128)(2,1)} %get-tuple-element.69.other.other_grp), custom_call_target="tpu_custom_call" | custom-call | flops 999999995904 | tf_op jit(solution)/shard_map/acc_stage/pallas_call | solution.py:273
  63.8 2.9 %static_stage.1 = (f32[128,512]{1,0:T(8,128)}, f32[1,128]{1,0:T(1,128)}, f32[256,512]{1,0:T(8,128)}) custom-call(f32[37,512]{1,0:T(8,128)} %bitcast.26, s32[1,37]{1,0:T(1,128)} %slots_in, f32[148,148]{1,0:T(8,128)} %coarse_in.1), custom_call_target="tpu_custom_call" | custom-call | tf_op jit(solution)/shard_map/static_stage/pallas_call | solution.py:404
  66.7 0.0 collective-permute-done.4.far_b
  66.7 0.0 collective-permute-done.5.near_b
  66.7 5.8 %part_stage.2 = (f32[384,1024]{1,0:T(8,128)}, s16[400,1024]{1,0:T(8,128)(2,1)}, bf16[768,1024]{1,0:T(8,128)(2,1)}) custom-call(s32[1]{0:T(128)} %bitcast.side, bf16[4,384,384]{2,1,0:T(8,128)(2,1)} %get-tuple-element.55.picks.refs_1_, f32[1536,1]{1,0:T(8,128)} %get-tuple-element.56.w_col.refs_2_, bf16[1536,1536]{1,0:T(8,128)(2,1)} %bitcast.16, ...), custom_call_target="tpu_custom_call" | custom-call | tf_op jit(solution)/shard_map/part_stage/pallas_call | solution.py:338
  72.5 1.6 %collective-permute-start.6 = (s16[400,1024]{1,0:T(8,128)(2,1)}, s16[400,1024]{1,0:T(8,128)(2,1)}, u32[]{:S(2)}, u32[]{:S(2)}) collective-permute-start(s16[400,1024]{1,0:T(8,128)(2,1)} %get-tuple-element.92), channel_id=1, source_target_pairs={{8,16},{24,32},{40,48},{56,64},{72,80},{88,96},{104,112},{120,128}... | collective-permute-start | bytes 2457608 | tf_op jit(solution)/shard_map/ppermute | solution.py:554
  74.1 0.0 all-to-all-done.loads
  74.1 4.5 %group_stage.1 = (f32[32,512]{1,0:T(8,128)}, f32[8,40,128]{2,1,0:T(8,128)}, s32[32,128]{1,0:T(8,128)}) custom-call(bf16[32,48,128]{2,1,0:T(8,128)(2,1)} %all-to-all-done.loads, f32[512,512]{1,0:T(8,128)} %bitcast.25, f32[128,512]{1,0:T(8,128)} %get-tuple-element.79.basis, f32[1,128]{1,0:T(1,128)} %get-tuple-element.80.slots), custom_call_target="tpu_custom_call" | custom-call | tf_op jit(solution)/shard_map/group_stage/pallas_call | solution.py:448
  78.6 3.8 %part_stage.3 = (f32[384,1024]{1,0:T(8,128)}, s16[400,1024]{1,0:T(8,128)(2,1)}) custom-call(s32[1]{0:T(128)} %bitcast.side, bf16[1536,1536]{1,0:T(8,128)(2,1)} %bitcast.17, bf16[768,1024]{1,0:T(8,128)(2,1)} %get-tuple-element.85.other.other_sub, f32[768,1024]{1,0:T(8,128)} %acc_stage.1.acc), custom_call_target="tpu_custom_call" | custom-call | tf_op jit(solution)/shard_map/part_stage/pallas_call | solution.py:338
  82.4 2.6 %collective-permute-start.7 = (s16[400,1024]{1,0:T(8,128)(2,1)}, s16[400,1024]{1,0:T(8,128)(2,1)}, u32[]{:S(2)}, u32[]{:S(2)}) collective-permute-start(s16[400,1024]{1,0:T(8,128)(2,1)} %get-tuple-element.93), channel_id=1, source_target_pairs={{0,8},{8,0},{16,24},{24,16},{32,40},{40,32},{48,56},{56,48},{64,72... | collective-permute-start | bytes 2457608 | tf_op jit(solution)/shard_map/ppermute | solution.py:554
  85.0 5.9 %all-to-all-start.1 = ((f32[8,40,128]{2,1,0:T(8,128)}), f32[8,40,128]{2,1,0:T(8,128)}, u32[]{:S(2)}, u32[]{:S(2)}) async-start(f32[8,40,128]{2,1,0:T(8,128)} %get-tuple-element.81), calls=%async_computation.1 | async-start | bytes 327680 | tf_op jit(solution)/shard_map/all_to_all | solution.py:607
  90.9 8.5 %part_grp_stage.1 = (f32[384,1024]{1,0:T(8,128)}, f32[384,1024]{1,0:T(8,128)}, s16[400,1024]{1,0:T(8,128)(2,1)}, s16[400,1024]{1,0:T(8,128)(2,1)}) custom-call(s32[1]{0:T(128)} %bitcast.2.grp_side.side.refs_0_, bf16[1536,1536]{1,0:T(8,128)(2,1)} %bitcast.18, bf16[768,1024]{1,0:T(8,128)(2,1)} %get-tuple-element.85.other.other_sub, ...), custom_call_target="tpu_custom_call" | custom-call | tf_op jit(solution)/shard_map/part_grp_stage/pallas_call | solution.py:370
  99.4 3.5 %collective-permute-start.10 = (s16[400,1024]{1,0:T(8,128)(2,1)}, s16[400,1024]{1,0:T(8,128)(2,1)}, u32[]{:S(2)}, u32[]{:S(2)}) collective-permute-start(s16[400,1024]{1,0:T(8,128)(2,1)} %get-tuple-element.99), channel_id=1, source_target_pairs={{1,2},{3,4},{5,6},{2,1},{4,3},{6,5},{9,10},{11,12},{13,14},{10,9},... | collective-permute-start | bytes 2457608 | tf_op jit(solution)/shard_map/ppermute | solution.py:554
  103.0 0.1 collective-permute-start.11
  103.1 0.0 all-to-all-done.1.received
  103.1 3.6 %coarse_stage.1 = bf16[32,32,128]{2,1,0:T(8,128)(2,1)} custom-call(f32[8,40,128]{2,1,0:T(8,128)} %all-to-all-done.1.received, f32[32,512]{1,0:T(8,128)} %get-tuple-element.89.local_in, f32[256,512]{1,0:T(8,128)} %get-tuple-element.90.up, s32[32,128]{1,0:T(8,128)} %get-tuple-element.91.index), custom_call_target="tpu_custom_call" | custom-call | tf_op jit(solution)/shard_map/coarse_stage/pallas_call | solution.py:485
  106.7 22.8 %all-to-all-start.2 = ((bf16[32,32,128]{2,1,0:T(8,128)(2,1)}), bf16[32,32,128]{2,1,0:T(8,128)(2,1)}, u32[]{:S(2)}, u32[]{:S(2)}) async-start(bf16[32,32,128]{2,1,0:T(8,128)(2,1)} %coarse_stage.1), calls=%async_computation.2 | async-start | bytes 524288 | tf_op jit(solution)/shard_map/all_to_all | solution.py:616
  129.4 0.0 collective-permute-done.6.far_q
  129.5 12.1 %all-to-all-done.2 = bf16[32,32,128]{2,1,0:T(8,128)(2,1)} async-done(((bf16[32,32,128]{2,1,0:T(8,128)(2,1)}), bf16[32,32,128]{2,1,0:T(8,128)(2,1)}, u32[]{:S(2)}, u32[]{:S(2)}) %all-to-all-start.2) | async-done | bytes 262176 | tf_op jit(solution)/shard_map/all_to_all | solution.py:616
  141.5 0.0 collective-permute-done.7.near_q
  141.5 2.1 %collective-permute-start.9 = (bf16[1024,128]{1,0:T(8,128)(2,1)}, bf16[1024,128]{1,0:T(8,128)(2,1)}, u32[]{:S(2)}, u32[]{:S(2)}) collective-permute-start(bf16[1024,128]{1,0:T(8,128)(2,1)} %bitcast.9.primal.far_p.near_p.refs_6_), channel_id=1, source_target_pairs={{0,1},{1,0},{2,3},{3,2},{4,5},{5,4},{6,7},{7,6},{8,9},{9,8},{10,11... | collective-permute-start | bytes 786440 | tf_op jit(solution)/shard_map/ppermute | solution.py:554
  143.6 2.1 %collective-permute-start.8 = (bf16[1024,128]{1,0:T(8,128)(2,1)}, bf16[1024,128]{1,0:T(8,128)(2,1)}, u32[]{:S(2)}, u32[]{:S(2)}) collective-permute-start(bf16[1024,128]{1,0:T(8,128)(2,1)} %bitcast.9.primal.far_p.near_p.refs_6_), channel_id=1, source_target_pairs={{1,2},{3,4},{5,6},{2,1},{4,3},{6,5},{9,10},{11,12},{13,14},{10,9},... | collective-permute-start | bytes 786440 | tf_op jit(solution)/shard_map/ppermute | solution.py:554
  145.7 6.1 %last_stage.2._ = bf16[1536,1024]{1,0:T(8,128)(2,1)} custom-call(s32[1]{0:T(128)} %bitcast.side, bf16[4,384,384]{2,1,0:T(8,128)(2,1)} %get-tuple-element.55.picks.refs_1_, f32[1536,1]{1,0:T(8,128)} %get-tuple-element.56.w_col.refs_2_, bf16[1536,128]{1,0:T(8,128)(2,1)} %get-tuple-element.57.basis_t.refs_3_, f32[384,1024]{1,0:T(8,128)} %get-tuple-element.76.far_part, ...), custom_call_target="tpu_custom_call" | custom-call | tf_op jit(solution)/shard_map/last_stage/pallas_call | solution.py:535
  151.8 0.0 collective-permute-done.10.refs_11_
  151.8 0.0 collective-permute-done.11.refs_12_
  151.8 0.0 collective-permute-done.9.refs_10_
  151.8 0.0 collective-permute-done.8.refs_9_
  151.8 6.0 %last_stage.3 = bf16[1536,1024]{1,0:T(8,128)(2,1)} custom-call(bf16[1536,1024]{1,0:T(8,128)(2,1)} %last_stage.2._, s32[1]{0:T(128)} %bitcast.2.grp_side.side.refs_0_, bf16[4,384,384]{2,1,0:T(8,128)(2,1)} %get-tuple-element.55.picks.refs_1_, f32[1536,1]{1,0:T(8,128)} %get-tuple-element.56.w_col.refs_2_, ...), custom_call_target="tpu_custom_call", output_to_operand_aliasing={{}: (0, {})} | custom-call | tf_op jit(solution)/shard_map/last_stage/pallas_call | solution.py:535
Async XLA Ops:
  4.2 12.4 %collective-permute-start = (bf16[400,1024]{1,0:T(8,128)(2,1)}, bf16[400,1024]{1,0:T(8,128)(2,1)}, u32[]{:S(2)}, u32[]{:S(2)}) collective-permute-start(bf16[400,1024]{1,0:T(8,128)(2,1)} %get-tuple-element.53), channel_id=1, source_target_pairs={{0,1},{1,0},{2,3},{3,2},{4,5},{5,4},{6,7},{7,6},{8,9},{9,8},{10,11... | collective-permute-start | bytes 2457608 | tf_op jit(solution)/shard_map/ppermute | solution.py:554
  7.5 27.6 %collective-permute-start.1 = (bf16[400,1024]{1,0:T(8,128)(2,1)}, bf16[400,1024]{1,0:T(8,128)(2,1)}, u32[]{:S(2)}, u32[]{:S(2)}) collective-permute-start(bf16[400,1024]{1,0:T(8,128)(2,1)} %get-tuple-element.61), channel_id=1, source_target_pairs={{1,2},{3,4},{5,6},{2,1},{4,3},{6,5},{9,10},{11,12},{13,14},{10,9},... | collective-permute-start | bytes 2457608 | tf_op jit(solution)/shard_map/ppermute | solution.py:554
  9.4 29.8 %collective-permute-start.2 = (bf16[64,1024]{1,0:T(8,128)(2,1)}, bf16[64,1024]{1,0:T(8,128)(2,1)}, u32[]{:S(2)}, u32[]{:S(2)}) collective-permute-start(bf16[64,1024]{1,0:T(8,128)(2,1)} %get-tuple-element.64), channel_id=1, source_target_pairs={{8,16},{24,32},{40,48},{56,64},{72,80},{88,96},{104,112},{120,128}... | collective-permute-start | bytes 393224 | tf_op jit(solution)/shard_map/ppermute | solution.py:554
  10.7 28.5 %collective-permute-start.3 = (bf16[64,1024]{1,0:T(8,128)(2,1)}, bf16[64,1024]{1,0:T(8,128)(2,1)}, u32[]{:S(2)}, u32[]{:S(2)}) collective-permute-start(bf16[64,1024]{1,0:T(8,128)(2,1)} %get-tuple-element.65), channel_id=1, source_target_pairs={{0,8},{8,0},{16,24},{24,16},{32,40},{40,32},{48,56},{56,48},{64,72... | collective-permute-start | bytes 393224 | tf_op jit(solution)/shard_map/ppermute | solution.py:554
  13.6 53.1 %collective-permute-start.4 = (bf16[352,1024]{1,0:T(8,128)(2,1)}, bf16[352,1024]{1,0:T(8,128)(2,1)}, u32[]{:S(2)}, u32[]{:S(2)}) collective-permute-start(bf16[352,1024]{1,0:T(8,128)(2,1)} %get-tuple-element.66), channel_id=1, source_target_pairs={{8,16},{24,32},{40,48},{56,64},{72,80},{88,96},{104,112},{120,128}... | collective-permute-start | bytes 2162696 | tf_op jit(solution)/shard_map/ppermute | solution.py:554
  16.6 50.0 %collective-permute-start.5 = (bf16[352,1024]{1,0:T(8,128)(2,1)}, bf16[352,1024]{1,0:T(8,128)(2,1)}, u32[]{:S(2)}, u32[]{:S(2)}) collective-permute-start(bf16[352,1024]{1,0:T(8,128)(2,1)} %get-tuple-element.67), channel_id=1, source_target_pairs={{0,8},{8,0},{16,24},{24,16},{32,40},{40,32},{48,56},{56,48},{64,72... | collective-permute-start | bytes 2162696 | tf_op jit(solution)/shard_map/ppermute | solution.py:554
  41.9 32.2 %all-to-all-start = ((bf16[32,48,128]{2,1,0:T(8,128)(2,1)}), bf16[32,48,128]{2,1,0:T(8,128)(2,1)}, u32[]{:S(2)}, u32[]{:S(2)}) async-start(bf16[32,48,128]{2,1,0:T(8,128)(2,1)} %load_stage.1), calls=%async_computation | async-start | bytes 786432 | tf_op jit(solution)/shard_map/all_to_all | solution.py:598
  72.5 57.0 %collective-permute-start.6 = (s16[400,1024]{1,0:T(8,128)(2,1)}, s16[400,1024]{1,0:T(8,128)(2,1)}, u32[]{:S(2)}, u32[]{:S(2)}) collective-permute-start(s16[400,1024]{1,0:T(8,128)(2,1)} %get-tuple-element.92), channel_id=1, source_target_pairs={{8,16},{24,32},{40,48},{56,64},{72,80},{88,96},{104,112},{120,128}... | collective-permute-start | bytes 2457608 | tf_op jit(solution)/shard_map/ppermute | solution.py:554
  82.4 59.1 %collective-permute-start.7 = (s16[400,1024]{1,0:T(8,128)(2,1)}, s16[400,1024]{1,0:T(8,128)(2,1)}, u32[]{:S(2)}, u32[]{:S(2)}) collective-permute-start(s16[400,1024]{1,0:T(8,128)(2,1)} %get-tuple-element.93), channel_id=1, source_target_pairs={{0,8},{8,0},{16,24},{24,16},{32,40},{40,32},{48,56},{56,48},{64,72... | collective-permute-start | bytes 2457608 | tf_op jit(solution)/shard_map/ppermute | solution.py:554
  85.0 18.1 %all-to-all-start.1 = ((f32[8,40,128]{2,1,0:T(8,128)}), f32[8,40,128]{2,1,0:T(8,128)}, u32[]{:S(2)}, u32[]{:S(2)}) async-start(f32[8,40,128]{2,1,0:T(8,128)} %get-tuple-element.81), calls=%async_computation.1 | async-start | bytes 327680 | tf_op jit(solution)/shard_map/all_to_all | solution.py:607
  99.4 52.4 %collective-permute-start.10 = (s16[400,1024]{1,0:T(8,128)(2,1)}, s16[400,1024]{1,0:T(8,128)(2,1)}, u32[]{:S(2)}, u32[]{:S(2)}) collective-permute-start(s16[400,1024]{1,0:T(8,128)(2,1)} %get-tuple-element.99), channel_id=1, source_target_pairs={{1,2},{3,4},{5,6},{2,1},{4,3},{6,5},{9,10},{11,12},{13,14},{10,9},... | collective-permute-start | bytes 2457608 | tf_op jit(solution)/shard_map/ppermute | solution.py:554
  103.0 48.8 %collective-permute-start.11 = (s16[400,1024]{1,0:T(8,128)(2,1)}, s16[400,1024]{1,0:T(8,128)(2,1)}, u32[]{:S(2)}, u32[]{:S(2)}) collective-permute-start(s16[400,1024]{1,0:T(8,128)(2,1)} %get-tuple-element.100), channel_id=1, source_target_pairs={{0,1},{1,0},{2,3},{3,2},{4,5},{5,4},{6,7},{7,6},{8,9},{9,8},{10,11... | collective-permute-start | bytes 2457608 | tf_op jit(solution)/shard_map/ppermute | solution.py:554
  106.7 34.8 %all-to-all-start.2 = ((bf16[32,32,128]{2,1,0:T(8,128)(2,1)}), bf16[32,32,128]{2,1,0:T(8,128)(2,1)}, u32[]{:S(2)}, u32[]{:S(2)}) async-start(bf16[32,32,128]{2,1,0:T(8,128)(2,1)} %coarse_stage.1), calls=%async_computation.2 | async-start | bytes 524288 | tf_op jit(solution)/shard_map/all_to_all | solution.py:616
  141.5 10.3 %collective-permute-start.9 = (bf16[1024,128]{1,0:T(8,128)(2,1)}, bf16[1024,128]{1,0:T(8,128)(2,1)}, u32[]{:S(2)}, u32[]{:S(2)}) collective-permute-start(bf16[1024,128]{1,0:T(8,128)(2,1)} %bitcast.9.primal.far_p.near_p.refs_6_), channel_id=1, source_target_pairs={{0,1},{1,0},{2,3},{3,2},{4,5},{5,4},{6,7},{7,6},{8,9},{9,8},{10,11... | collective-permute-start | bytes 786440 | tf_op jit(solution)/shard_map/ppermute | solution.py:554
  143.6 8.2 %collective-permute-start.8 = (bf16[1024,128]{1,0:T(8,128)(2,1)}, bf16[1024,128]{1,0:T(8,128)(2,1)}, u32[]{:S(2)}, u32[]{:S(2)}) collective-permute-start(bf16[1024,128]{1,0:T(8,128)(2,1)} %bitcast.9.primal.far_p.near_p.refs_6_), channel_id=1, source_target_pairs={{1,2},{3,4},{5,6},{2,1},{4,3},{6,5},{9,10},{11,12},{13,14},{10,9},... | collective-permute-start | bytes 786440 | tf_op jit(solution)/shard_map/ppermute | solution.py:554

commit v4 on v3

--- a/solution.py
+++ b/solution.py
@@ -10,7 +10,7 @@
 LANES = 128
 SLOT = 40
 PACK = 16
-EARLY = 32
+EARLY = 16
 EXTRA = 16
 BASE = 16
 VMEM = 64 * 1024 * 1024
@@ -594,12 +594,13 @@
     acc_grp = own_stage(inverse, own)
     rest, acc_grp = together(rest, acc_grp)
     other_grp, rest = far_stage(grp_side, coarse_rows, picks, w_col, rest, far_g, near_g)
+    g_basis, slots, up = static_stage(group_basis[0], group_index, coarse_inverse)
+    rest, g_basis, slots, up = together(rest, g_basis, slots, up)
     load = load_stage(nc, side, primal_index[0], rest, x, far_a, near_a, subs)
     loads = lax.all_to_all(load, "sub", 0, 0, tiled=True)
-    other_grp, group_index, load = together(other_grp, group_index, load)
-    g_basis, slots, up = static_stage(group_basis[0], group_index, coarse_inverse)
+    other_grp, load = together(other_grp, load)
     acc_sub = acc_stage(inverse, own, other_grp)
-    far_b, near_b, acc_sub, up = together(far_b, near_b, acc_sub, up)
+    far_b, near_b, acc_sub = together(far_b, near_b, acc_sub)
     faces = (picks, w_col, far_a, far_b, near_a, near_b)
     part_far, q_far, other_sub = part_stage(side, inverse, acc_sub, faces)
     loads, part_far = together(loads, part_far)

time: 160 us -> 159 us (level)
  no operation moved by 1% of the time
where the time goes in v4:
time: 159 us; the launch traced here: 158 us
  starting transfers between devices  72.6 us (46%)
  Pallas kernels  71.4 us (45%)
  waiting for transfers between devices  12 us (8%)
    all_to_all x1, starting transfers between devices, local(): primal = lax.all_to_all(picked, 'sub', 0, 0, tiled=True).reshape(m, LANES)  24.1 us
    ppermute x6, starting transfers between devices, swap(): lax.ppermute(near_out, axis, near)  18.5 us
    all_to_all x1, starting transfers between devices, local(): loads = lax.all_to_all(load, 'sub', 0, 0, tiled=True)  12.9 us
    pallas_call x2, Pallas kernels, last_stage(): pl.pallas_call(kernel, grid=(2,), in_specs=in_specs, out_specs=spec((half...  12.1 us
    all_to_all x1, waiting for transfers between devices, local(): primal = lax.all_to_all(picked, 'sub', 0, 0, tiled=True).reshape(m, LANES)  12 us
    ppermute x6, starting transfers between devices, swap(): lax.ppermute(far_out, axis, far)  11.8 us
    pallas_call x2, Pallas kernels, part_stage(): pl.pallas_call(part_far_kernel if far else part_near_kernel, grid_spec=pl...  9.63 us
    pallas_call x1, Pallas kernels, part_grp_stage(): pl.pallas_call(functools.partial(part_grp_kernel, half), grid=(2,), in_sp...  8.53 us
  transfers between devices with their start and end apart: 15, of which 1 were waited for; matrix products, arithmetic and copies ran while one was open for 1% of the time, Pallas kernels for 39%

profile of v4, /device:TPU:1, one launch (start us, length us, event | category | flops | bytes accessed | tf_op | source)
XLA Modules:
  0.0 157.6 jit_solution(13332860874801137013)
XLA Ops:
  0.0 4.2 %first_stage.1 = (bf16[400,1024]{1,0:T(8,128)(2,1)}, bf16[400,1024]{1,0:T(8,128)(2,1)}, bf16[48,1024]{1,0:T(8,128)(2,1)}, bf16[368,1024]{1,0:T(8,128)(2,1)}, bf1...) custom-call(s32[1]{0:T(128)} %bitcast.side, s32[1]{0:T(128)} %bitcast.2.grp_side.side.refs_0_, f32[1,1536]{1,0:T(1,128)} %bitcast.27, ...), custom_call_target="tpu_custom_call" | custom-call | tf_op jit(solution)/shard_map/first_stage/pallas_call | solution.py:107
  4.2 3.2 %collective-permute-start = (bf16[400,1024]{1,0:T(8,128)(2,1)}, bf16[400,1024]{1,0:T(8,128)(2,1)}, u32[]{:S(2)}, u32[]{:S(2)}) collective-permute-start(bf16[400,1024]{1,0:T(8,128)(2,1)} %get-tuple-element.55), channel_id=1, source_target_pairs={{0,1},{1,0},{2,3},{3,2},{4,5},{5,4},{6,7},{7,6},{8,9},{9,8},{10,11... | collective-permute-start | bytes 2457608 | tf_op jit(solution)/shard_map/ppermute | solution.py:554
  7.5 1.9 %collective-permute-start.1 = (bf16[400,1024]{1,0:T(8,128)(2,1)}, bf16[400,1024]{1,0:T(8,128)(2,1)}, u32[]{:S(2)}, u32[]{:S(2)}) collective-permute-start(bf16[400,1024]{1,0:T(8,128)(2,1)} %get-tuple-element.63), channel_id=1, source_target_pairs={{1,2},{3,4},{5,6},{2,1},{4,3},{6,5},{9,10},{11,12},{13,14},{10,9},... | collective-permute-start | bytes 2457608 | tf_op jit(solution)/shard_map/ppermute | solution.py:554
  9.4 1.3 collective-permute-start.2
  10.7 2.9 %collective-permute-start.3 = (bf16[48,1024]{1,0:T(8,128)(2,1)}, bf16[48,1024]{1,0:T(8,128)(2,1)}, u32[]{:S(2)}, u32[]{:S(2)}) collective-permute-start(bf16[48,1024]{1,0:T(8,128)(2,1)} %get-tuple-element.71), channel_id=1, source_target_pairs={{0,8},{8,0},{16,24},{24,16},{32,40},{40,32},{48,56},{56,48},{64,72... | collective-permute-start | bytes 294920 | tf_op jit(solution)/shard_map/ppermute | solution.py:554
  13.6 1.5 collective-permute-start.4
  15.1 1.5 copy.14
  16.7 2.9 %static_stage.1 = (f32[128,512]{1,0:T(8,128)}, f32[1,128]{1,0:T(1,128)}, f32[256,512]{1,0:T(8,128)}) custom-call(f32[37,512]{1,0:T(8,128)} %bitcast.26, s32[1,37]{1,0:T(1,128)} %slots_in.1, f32[148,148]{1,0:T(8,128)} %coarse_in.1), custom_call_target="tpu_custom_call" | custom-call | tf_op jit(solution)/shard_map/static_stage/pallas_call | solution.py:404
  19.5 0.0 collective-permute-done.near.refs_8_
  19.5 7.2 %collective-permute-start.5 = (bf16[368,1024]{1,0:T(8,128)(2,1)}, bf16[368,1024]{1,0:T(8,128)(2,1)}, u32[]{:S(2)}, u32[]{:S(2)}) collective-permute-start(bf16[368,1024]{1,0:T(8,128)(2,1)} %get-tuple-element.73), channel_id=1, source_target_pairs={{0,8},{8,0},{16,24},{24,16},{32,40},{40,32},{48,56},{56,48},{64,72... | collective-permute-start | bytes 2261000 | tf_op jit(solution)/shard_map/ppermute | solution.py:554
  26.8 5.0 %base_stage.1 = (bf16[1536,1024]{1,0:T(8,128)(2,1)}, f32[40,1024]{1,0:T(8,128)}, bf16[4,384,384]{2,1,0:T(8,128)(2,1)}, f32[1536,1]{1,0:T(8,128)}, bf16[1536,128]{1,0:T(8,128)(2,1)}) custom-call(f32[1,1536]{1,0:T(1,128)} %bitcast.28, s32[4,384]{1,0:T(4,128)} %bitcast.30, bf16[37,1536]{1,0:T(8,128)(2,1)} %bitcast.23, bf16[1536,1024]{1,0:T(8,128)(2,1)} %bitcast.20), custom_call_target="tpu_custom_call" | custom-call | tf_op jit(solution)/shard_map/base_stage/pallas_call | solution.py:145
  31.8 6.2 %own_stage.1.acc = f32[768,1024]{1,0:T(8,128)} custom-call(bf16[1536,1536]{1,0:T(8,128)(2,1)} %bitcast.14, bf16[1536,1024]{1,0:T(8,128)(2,1)} %get-tuple-element.61.own), custom_call_target="tpu_custom_call" | custom-call | tf_op jit(solution)/shard_map/own_stage/pallas_call | solution.py:254
  38.0 0.0 collective-permute-done.1.far.refs_7_
  38.0 4.1 %far_stage.1 = (bf16[768,1024]{1,0:T(8,128)(2,1)}, f32[40,1024]{1,0:T(8,128)}) custom-call(s32[1]{0:T(128)} %bitcast.2.grp_side.side.refs_0_, bf16[37,1536]{1,0:T(8,128)(2,1)} %bitcast.24, bf16[4,384,384]{2,1,0:T(8,128)(2,1)} %get-tuple-element.57.picks.refs_1_, f32[1536,1]{1,0:T(8,128)} %get-tuple-element.58.w_col.refs_2_, ...), custom_call_target="tpu_custom_call" | custom-call | tf_op jit(solution)/shard_map/far_stage/pallas_call | solution.py:187
  42.1 0.0 collective-permute-done.2.far.far_a
  42.1 0.0 collective-permute-done.3.near.near_a
  42.1 2.6 %load_stage.1 = bf16[32,48,128]{2,1,0:T(8,128)(2,1)} custom-call(s32[1]{0:T(128)} %bitcast.side, s32[1,37]{1,0:T(1,128)} %bitcast.31, f32[40,1024]{1,0:T(8,128)} %get-tuple-element.69.rest, bf16[1536,1024]{1,0:T(8,128)(2,1)} %bitcast.21, bf16[48,1024]{1,0:T(8,128)(2,1)} %collective-permute-done.2.far.far_a, bf16[48,1024]{1,0:T(8,128)(2,1)} %collective-permute-done.3.near.near_a), custom_call_target="tpu_custom_call" | custom-call | tf_op jit(solution)/shard_map/load_stage/pallas_call | solution.py:234
  44.7 12.9 %all-to-all-start = ((bf16[32,48,128]{2,1,0:T(8,128)(2,1)}), bf16[32,48,128]{2,1,0:T(8,128)(2,1)}, u32[]{:S(2)}, u32[]{:S(2)}) async-start(bf16[32,48,128]{2,1,0:T(8,128)(2,1)} %load_stage.1), calls=%async_computation | async-start | bytes 786432 | tf_op jit(solution)/shard_map/all_to_all | solution.py:600
  57.7 7.9 %acc_stage.1.acc = f32[768,1024]{1,0:T(8,128)} custom-call(bf16[1536,1536]{1,0:T(8,128)(2,1)} %bitcast.15, bf16[1536,1024]{1,0:T(8,128)(2,1)} %get-tuple-element.61.own, bf16[768,1024]{1,0:T(8,128)(2,1)} %get-tuple-element.75.other.other_grp), custom_call_target="tpu_custom_call" | custom-call | flops 999999995904 | tf_op jit(solution)/shard_map/acc_stage/pallas_call | solution.py:273
  65.6 0.0 collective-permute-done.4.far_b
  65.6 0.0 collective-permute-done.5.near_b
  65.6 5.8 %part_stage.2 = (f32[384,1024]{1,0:T(8,128)}, s16[400,1024]{1,0:T(8,128)(2,1)}, bf16[768,1024]{1,0:T(8,128)(2,1)}) custom-call(s32[1]{0:T(128)} %bitcast.side, bf16[4,384,384]{2,1,0:T(8,128)(2,1)} %get-tuple-element.57.picks.refs_1_, f32[1536,1]{1,0:T(8,128)} %get-tuple-element.58.w_col.refs_2_, bf16[1536,1536]{1,0:T(8,128)(2,1)} %bitcast.16, ...), custom_call_target="tpu_custom_call" | custom-call | tf_op jit(solution)/shard_map/part_stage/pallas_call | solution.py:338
  71.4 1.6 %collective-permute-start.6 = (s16[400,1024]{1,0:T(8,128)(2,1)}, s16[400,1024]{1,0:T(8,128)(2,1)}, u32[]{:S(2)}, u32[]{:S(2)}) collective-permute-start(s16[400,1024]{1,0:T(8,128)(2,1)} %get-tuple-element.96), channel_id=1, source_target_pairs={{8,16},{24,32},{40,48},{56,64},{72,80},{88,96},{104,112},{120,128}... | collective-permute-start | bytes 2457608 | tf_op jit(solution)/shard_map/ppermute | solution.py:554
  73.0 0.0 all-to-all-done.loads
  73.0 4.5 %group_stage.1 = (f32[32,512]{1,0:T(8,128)}, f32[8,40,128]{2,1,0:T(8,128)}, s32[32,128]{1,0:T(8,128)}) custom-call(bf16[32,48,128]{2,1,0:T(8,128)(2,1)} %all-to-all-done.loads, f32[512,512]{1,0:T(8,128)} %bitcast.25, f32[128,512]{1,0:T(8,128)} %get-tuple-element.83.basis, f32[1,128]{1,0:T(1,128)} %get-tuple-element.84.slots), custom_call_target="tpu_custom_call" | custom-call | tf_op jit(solution)/shard_map/group_stage/pallas_call | solution.py:448
  77.6 3.8 %part_stage.3 = (f32[384,1024]{1,0:T(8,128)}, s16[400,1024]{1,0:T(8,128)(2,1)}) custom-call(s32[1]{0:T(128)} %bitcast.side, bf16[1536,1536]{1,0:T(8,128)(2,1)} %bitcast.17, bf16[768,1024]{1,0:T(8,128)(2,1)} %get-tuple-element.89.other.other_sub, f32[768,1024]{1,0:T(8,128)} %acc_stage.1.acc), custom_call_target="tpu_custom_call" | custom-call | tf_op jit(solution)/shard_map/part_stage/pallas_call | solution.py:338
  81.4 2.9 %collective-permute-start.7 = (s16[400,1024]{1,0:T(8,128)(2,1)}, s16[400,1024]{1,0:T(8,128)(2,1)}, u32[]{:S(2)}, u32[]{:S(2)}) collective-permute-start(s16[400,1024]{1,0:T(8,128)(2,1)} %get-tuple-element.97), channel_id=1, source_target_pairs={{0,8},{8,0},{16,24},{24,16},{32,40},{40,32},{48,56},{56,48},{64,72... | collective-permute-start | bytes 2457608 | tf_op jit(solution)/shard_map/ppermute | solution.py:554
  84.3 5.3 %all-to-all-start.1 = ((f32[8,40,128]{2,1,0:T(8,128)}), f32[8,40,128]{2,1,0:T(8,128)}, u32[]{:S(2)}, u32[]{:S(2)}) async-start(f32[8,40,128]{2,1,0:T(8,128)} %get-tuple-element.85), calls=%async_computation.1 | async-start | bytes 327680 | tf_op jit(solution)/shard_map/all_to_all | solution.py:608
  89.6 8.5 %part_grp_stage.1 = (f32[384,1024]{1,0:T(8,128)}, f32[384,1024]{1,0:T(8,128)}, s16[400,1024]{1,0:T(8,128)(2,1)}, s16[400,1024]{1,0:T(8,128)(2,1)}) custom-call(s32[1]{0:T(128)} %bitcast.2.grp_side.side.refs_0_, bf16[1536,1536]{1,0:T(8,128)(2,1)} %bitcast.18, bf16[768,1024]{1,0:T(8,128)(2,1)} %get-tuple-element.89.other.other_sub, ...), custom_call_target="tpu_custom_call" | custom-call | tf_op jit(solution)/shard_map/part_grp_stage/pallas_call | solution.py:370
  98.1 3.5 %collective-permute-start.10 = (s16[400,1024]{1,0:T(8,128)(2,1)}, s16[400,1024]{1,0:T(8,128)(2,1)}, u32[]{:S(2)}, u32[]{:S(2)}) collective-permute-start(s16[400,1024]{1,0:T(8,128)(2,1)} %get-tuple-element.103), channel_id=1, source_target_pairs={{1,2},{3,4},{5,6},{2,1},{4,3},{6,5},{9,10},{11,12},{13,14},{10,9},... | collective-permute-start | bytes 2457608 | tf_op jit(solution)/shard_map/ppermute | solution.py:554
  101.7 0.1 collective-permute-start.11
  101.8 0.0 all-to-all-done.1.received
  101.8 3.6 %coarse_stage.1 = bf16[32,32,128]{2,1,0:T(8,128)(2,1)} custom-call(f32[8,40,128]{2,1,0:T(8,128)} %all-to-all-done.1.received, f32[32,512]{1,0:T(8,128)} %get-tuple-element.93.local_in, f32[256,512]{1,0:T(8,128)} %get-tuple-element.94.up, s32[32,128]{1,0:T(8,128)} %get-tuple-element.95.index), custom_call_target="tpu_custom_call" | custom-call | tf_op jit(solution)/shard_map/coarse_stage/pallas_call | solution.py:485
  105.4 24.1 %all-to-all-start.2 = ((bf16[32,32,128]{2,1,0:T(8,128)(2,1)}), bf16[32,32,128]{2,1,0:T(8,128)(2,1)}, u32[]{:S(2)}, u32[]{:S(2)}) async-start(bf16[32,32,128]{2,1,0:T(8,128)(2,1)} %coarse_stage.1), calls=%async_computation.2 | async-start | bytes 524288 | tf_op jit(solution)/shard_map/all_to_all | solution.py:617
  129.4 0.0 collective-permute-done.6.far_q
  129.5 12.0 %all-to-all-done.2 = bf16[32,32,128]{2,1,0:T(8,128)(2,1)} async-done(((bf16[32,32,128]{2,1,0:T(8,128)(2,1)}), bf16[32,32,128]{2,1,0:T(8,128)(2,1)}, u32[]{:S(2)}, u32[]{:S(2)}) %all-to-all-start.2) | async-done | bytes 262176 | tf_op jit(solution)/shard_map/all_to_all | solution.py:617
  141.4 0.0 collective-permute-done.7.near_q
  141.4 2.1 %collective-permute-start.9 = (bf16[1024,128]{1,0:T(8,128)(2,1)}, bf16[1024,128]{1,0:T(8,128)(2,1)}, u32[]{:S(2)}, u32[]{:S(2)}) collective-permute-start(bf16[1024,128]{1,0:T(8,128)(2,1)} %bitcast.9.primal.far_p.near_p.refs_6_), channel_id=1, source_target_pairs={{0,1},{1,0},{2,3},{3,2},{4,5},{5,4},{6,7},{7,6},{8,9},{9,8},{10,11... | collective-permute-start | bytes 786440 | tf_op jit(solution)/shard_map/ppermute | solution.py:554
  143.6 1.9 %collective-permute-start.8 = (bf16[1024,128]{1,0:T(8,128)(2,1)}, bf16[1024,128]{1,0:T(8,128)(2,1)}, u32[]{:S(2)}, u32[]{:S(2)}) collective-permute-start(bf16[1024,128]{1,0:T(8,128)(2,1)} %bitcast.9.primal.far_p.near_p.refs_6_), channel_id=1, source_target_pairs={{1,2},{3,4},{5,6},{2,1},{4,3},{6,5},{9,10},{11,12},{13,14},{10,9},... | collective-permute-start | bytes 786440 | tf_op jit(solution)/shard_map/ppermute | solution.py:554
  145.5 6.1 %last_stage.2._ = bf16[1536,1024]{1,0:T(8,128)(2,1)} custom-call(s32[1]{0:T(128)} %bitcast.side, bf16[4,384,384]{2,1,0:T(8,128)(2,1)} %get-tuple-element.57.picks.refs_1_, f32[1536,1]{1,0:T(8,128)} %get-tuple-element.58.w_col.refs_2_, bf16[1536,128]{1,0:T(8,128)(2,1)} %get-tuple-element.59.basis_t.refs_3_, f32[384,1024]{1,0:T(8,128)} %get-tuple-element.80.far_part, ...), custom_call_target="tpu_custom_call" | custom-call | tf_op jit(solution)/shard_map/last_stage/pallas_call | solution.py:535
  151.5 0.0 collective-permute-done.10.refs_11_
  151.5 0.0 collective-permute-done.11.refs_12_
  151.5 0.0 collective-permute-done.9.refs_10_
  151.6 0.0 collective-permute-done.8.refs_9_
  151.6 6.0 %last_stage.3 = bf16[1536,1024]{1,0:T(8,128)(2,1)} custom-call(bf16[1536,1024]{1,0:T(8,128)(2,1)} %last_stage.2._, s32[1]{0:T(128)} %bitcast.2.grp_side.side.refs_0_, bf16[4,384,384]{2,1,0:T(8,128)(2,1)} %get-tuple-element.57.picks.refs_1_, f32[1536,1]{1,0:T(8,128)} %get-tuple-element.58.w_col.refs_2_, ...), custom_call_target="tpu_custom_call", output_to_operand_aliasing={{}: (0, {})} | custom-call | tf_op jit(solution)/shard_map/last_stage/pallas_call | solution.py:535
Async XLA Ops:
  4.2 15.3 %collective-permute-start = (bf16[400,1024]{1,0:T(8,128)(2,1)}, bf16[400,1024]{1,0:T(8,128)(2,1)}, u32[]{:S(2)}, u32[]{:S(2)}) collective-permute-start(bf16[400,1024]{1,0:T(8,128)(2,1)} %get-tuple-element.55), channel_id=1, source_target_pairs={{0,1},{1,0},{2,3},{3,2},{4,5},{5,4},{6,7},{7,6},{8,9},{9,8},{10,11... | collective-permute-start | bytes 2457608 | tf_op jit(solution)/shard_map/ppermute | solution.py:554
  7.5 30.5 %collective-permute-start.1 = (bf16[400,1024]{1,0:T(8,128)(2,1)}, bf16[400,1024]{1,0:T(8,128)(2,1)}, u32[]{:S(2)}, u32[]{:S(2)}) collective-permute-start(bf16[400,1024]{1,0:T(8,128)(2,1)} %get-tuple-element.63), channel_id=1, source_target_pairs={{1,2},{3,4},{5,6},{2,1},{4,3},{6,5},{9,10},{11,12},{13,14},{10,9},... | collective-permute-start | bytes 2457608 | tf_op jit(solution)/shard_map/ppermute | solution.py:554
  9.4 32.7 %collective-permute-start.2 = (bf16[48,1024]{1,0:T(8,128)(2,1)}, bf16[48,1024]{1,0:T(8,128)(2,1)}, u32[]{:S(2)}, u32[]{:S(2)}) collective-permute-start(bf16[48,1024]{1,0:T(8,128)(2,1)} %get-tuple-element.70), channel_id=1, source_target_pairs={{8,16},{24,32},{40,48},{56,64},{72,80},{88,96},{104,112},{120,128}... | collective-permute-start | bytes 294920 | tf_op jit(solution)/shard_map/ppermute | solution.py:554
  10.7 31.4 %collective-permute-start.3 = (bf16[48,1024]{1,0:T(8,128)(2,1)}, bf16[48,1024]{1,0:T(8,128)(2,1)}, u32[]{:S(2)}, u32[]{:S(2)}) collective-permute-start(bf16[48,1024]{1,0:T(8,128)(2,1)} %get-tuple-element.71), channel_id=1, source_target_pairs={{0,8},{8,0},{16,24},{24,16},{32,40},{40,32},{48,56},{56,48},{64,72... | collective-permute-start | bytes 294920 | tf_op jit(solution)/shard_map/ppermute | solution.py:554
  13.6 52.0 %collective-permute-start.4 = (bf16[368,1024]{1,0:T(8,128)(2,1)}, bf16[368,1024]{1,0:T(8,128)(2,1)}, u32[]{:S(2)}, u32[]{:S(2)}) collective-permute-start(bf16[368,1024]{1,0:T(8,128)(2,1)} %get-tuple-element.72), channel_id=1, source_target_pairs={{8,16},{24,32},{40,48},{56,64},{72,80},{88,96},{104,112},{120,128}... | collective-permute-start | bytes 2261000 | tf_op jit(solution)/shard_map/ppermute | solution.py:554
  19.5 46.1 %collective-permute-start.5 = (bf16[368,1024]{1,0:T(8,128)(2,1)}, bf16[368,1024]{1,0:T(8,128)(2,1)}, u32[]{:S(2)}, u32[]{:S(2)}) collective-permute-start(bf16[368,1024]{1,0:T(8,128)(2,1)} %get-tuple-element.73), channel_id=1, source_target_pairs={{0,8},{8,0},{16,24},{24,16},{32,40},{40,32},{48,56},{56,48},{64,72... | collective-permute-start | bytes 2261000 | tf_op jit(solution)/shard_map/ppermute | solution.py:554
  44.7 28.3 %all-to-all-start = ((bf16[32,48,128]{2,1,0:T(8,128)(2,1)}), bf16[32,48,128]{2,1,0:T(8,128)(2,1)}, u32[]{:S(2)}, u32[]{:S(2)}) async-start(bf16[32,48,128]{2,1,0:T(8,128)(2,1)} %load_stage.1), calls=%async_computation | async-start | bytes 786432 | tf_op jit(solution)/shard_map/all_to_all | solution.py:600
  71.4 58.0 %collective-permute-start.6 = (s16[400,1024]{1,0:T(8,128)(2,1)}, s16[400,1024]{1,0:T(8,128)(2,1)}, u32[]{:S(2)}, u32[]{:S(2)}) collective-permute-start(s16[400,1024]{1,0:T(8,128)(2,1)} %get-tuple-element.96), channel_id=1, source_target_pairs={{8,16},{24,32},{40,48},{56,64},{72,80},{88,96},{104,112},{120,128}... | collective-permute-start | bytes 2457608 | tf_op jit(solution)/shard_map/ppermute | solution.py:554
  81.4 60.1 %collective-permute-start.7 = (s16[400,1024]{1,0:T(8,128)(2,1)}, s16[400,1024]{1,0:T(8,128)(2,1)}, u32[]{:S(2)}, u32[]{:S(2)}) collective-permute-start(s16[400,1024]{1,0:T(8,128)(2,1)} %get-tuple-element.97), channel_id=1, source_target_pairs={{0,8},{8,0},{16,24},{24,16},{32,40},{40,32},{48,56},{56,48},{64,72... | collective-permute-start | bytes 2457608 | tf_op jit(solution)/shard_map/ppermute | solution.py:554
  84.3 17.5 %all-to-all-start.1 = ((f32[8,40,128]{2,1,0:T(8,128)}), f32[8,40,128]{2,1,0:T(8,128)}, u32[]{:S(2)}, u32[]{:S(2)}) async-start(f32[8,40,128]{2,1,0:T(8,128)} %get-tuple-element.85), calls=%async_computation.1 | async-start | bytes 327680 | tf_op jit(solution)/shard_map/all_to_all | solution.py:608
  98.1 53.4 %collective-permute-start.10 = (s16[400,1024]{1,0:T(8,128)(2,1)}, s16[400,1024]{1,0:T(8,128)(2,1)}, u32[]{:S(2)}, u32[]{:S(2)}) collective-permute-start(s16[400,1024]{1,0:T(8,128)(2,1)} %get-tuple-element.103), channel_id=1, source_target_pairs={{1,2},{3,4},{5,6},{2,1},{4,3},{6,5},{9,10},{11,12},{13,14},{10,9},... | collective-permute-start | bytes 2457608 | tf_op jit(solution)/shard_map/ppermute | solution.py:554
  101.7 49.9 %collective-permute-start.11 = (s16[400,1024]{1,0:T(8,128)(2,1)}, s16[400,1024]{1,0:T(8,128)(2,1)}, u32[]{:S(2)}, u32[]{:S(2)}) collective-permute-start(s16[400,1024]{1,0:T(8,128)(2,1)} %get-tuple-element.104), channel_id=1, source_target_pairs={{0,1},{1,0},{2,3},{3,2},{4,5},{5,4},{6,7},{7,6},{8,9},{9,8},{10,11... | collective-permute-start | bytes 2457608 | tf_op jit(solution)/shard_map/ppermute | solution.py:554
  105.4 36.1 %all-to-all-start.2 = ((bf16[32,32,128]{2,1,0:T(8,128)(2,1)}), bf16[32,32,128]{2,1,0:T(8,128)(2,1)}, u32[]{:S(2)}, u32[]{:S(2)}) async-start(bf16[32,32,128]{2,1,0:T(8,128)(2,1)} %coarse_stage.1), calls=%async_computation.2 | async-start | bytes 524288 | tf_op jit(solution)/shard_map/all_to_all | solution.py:617
  141.4 10.1 %collective-permute-start.9 = (bf16[1024,128]{1,0:T(8,128)(2,1)}, bf16[1024,128]{1,0:T(8,128)(2,1)}, u32[]{:S(2)}, u32[]{:S(2)}) collective-permute-start(bf16[1024,128]{1,0:T(8,128)(2,1)} %bitcast.9.primal.far_p.near_p.refs_6_), channel_id=1, source_target_pairs={{0,1},{1,0},{2,3},{3,2},{4,5},{5,4},{6,7},{7,6},{8,9},{9,8},{10,11... | collective-permute-start | bytes 786440 | tf_op jit(solution)/shard_map/ppermute | solution.py:554
  143.6 8.0 %collective-permute-start.8 = (bf16[1024,128]{1,0:T(8,128)(2,1)}, bf16[1024,128]{1,0:T(8,128)(2,1)}, u32[]{:S(2)}, u32[]{:S(2)}) collective-permute-start(bf16[1024,128]{1,0:T(8,128)(2,1)} %bitcast.9.primal.far_p.near_p.refs_6_), channel_id=1, source_target_pairs={{1,2},{3,4},{5,6},{2,1},{4,3},{6,5},{9,10},{11,12},{13,14},{10,9},... | collective-permute-start | bytes 786440 | tf_op jit(solution)/shard_map/ppermute | solution.py:554
